TPU v7x, 32 devices: a whole 2x2x4 slice. The times are simulated.
32 devices in a mesh: dp: 8 (over y, x, core), seq: 4 (over z).
Axes of the slice: x: 2, y: 2, z: 4, core: 2. Of those that a mesh axis runs over, the one named last changes fastest.
Arguments:
- tokens: bfloat16 [16, 2048, 768], P('dp', 'seq'), may hold values from -6 to 6
- timesteps: int32 [16], P('dp'), may hold values from 0 to 2047, as said below
- time_table: bfloat16 [2048, 768], replicated, may hold values from -3 to 3
- ln1_gain: bfloat16 [768], replicated, may hold values from 0.5 to 1.5
- ln1_bias: bfloat16 [768], replicated, may hold values from -1.25 to 1.25
- qkv_weight: bfloat16 [768, 2304], replicated, may hold values from -0.21875 to 0.21875
- q_bias: bfloat16 [768], replicated, may hold values from -1.25 to 1.25
- v_bias: bfloat16 [768], replicated, may hold values from -1.25 to 1.25
- out_weight: bfloat16 [768, 768], replicated, may hold values from -1.75 to 1.75
- out_bias: bfloat16 [768], replicated, may hold values from -1.25 to 1.25
- ln2_gain: bfloat16 [768], replicated, may hold values from 0.5 to 1.5
- ln2_bias: bfloat16 [768], replicated, may hold values from -1.25 to 1.25
- up_weight: bfloat16 [768, 3072], replicated, may hold values from -0.21875 to 0.21875
- up_bias: bfloat16 [3072], replicated, may hold values from -1.25 to 1.25
- down_weight: bfloat16 [3072, 768], replicated, may hold values from -0.109375 to 0.109375
- down_bias: bfloat16 [768], replicated, may hold values from -1.25 to 1.25
- cotangent: bfloat16 [16, 2048, 768], P('dp', 'seq'), may hold values from -6 to 6
Outputs:
- layer_out: bfloat16 [16, 2048, 768], P('dp', 'seq')
- tokens_grad: float32 [16, 2048, 768], P('dp', 'seq')
- time_table_grad: float32 [2048, 768], P('dp')
- ln1_gain_grad: float32 [768], P('dp')
- ln1_bias_grad: float32 [768], P('dp')
- qkv_weight_grad: float32 [768, 2304], P('dp')
- q_bias_grad: float32 [768], P('dp')
- v_bias_grad: float32 [768], P('dp')
- out_weight_grad: float32 [768, 768], P('dp')
- out_bias_grad: float32 [768], P('dp')
- ln2_gain_grad: float32 [768], P('dp')
- ln2_bias_grad: float32 [768], P('dp')
- up_weight_grad: float32 [768, 3072], P('dp')
- up_bias_grad: float32 [3072], P('dp')
- down_weight_grad: float32 [3072, 768], P('dp')
- down_bias_grad: float32 [768], P('dp')
- bucket_energy: float32 [4], replicated
- bucket_counts: float32 [4], replicated
Inputs may be any that keep to these rules, and one draw needn't show every extreme that they name: `timesteps`: one diffusion timestep per sequence; some sequence has timestep 0 and some has 2047.
All inputs are finite; a program needn't handle non-finite values.
Results may differ from a plain program's by a relative error of at most 0.015.
Values may be sent and summed in bfloat16 or wider, within the bound.
A program may use at most 192 MiB of HBM per device.

v0:
```python
import jax
import jax.numpy as jnp
from jax import lax
from jax.sharding import PartitionSpec as P

HEAD_DIM = 64
TSTEPS = 2048
BUCKETS = 4


norm_eps = 1e-05


def layer_norm(inputs, norm_gain, norm_shift):
    centered = inputs - jnp.mean(inputs, -1, keepdims=True)
    variance = jnp.mean(centered * centered, -1, keepdims=True)
    return centered * lax.rsqrt(variance + norm_eps) * norm_gain + norm_shift


def exact_gelu(inputs):
    return jax.nn.gelu(inputs, approximate=False)


def row_block():
    return 512


def split_rows(matrix, block_rows):
    shaped = matrix.reshape(matrix.shape[:-1] + (matrix.shape[-1] // block_rows, block_rows))
    return jnp.moveaxis(shaped, -2, 0)


def join_rows(stacked):
    joined = jnp.moveaxis(stacked, 0, -2)
    return joined.reshape(joined.shape[:-2] + (joined.shape[-2] * joined.shape[-1],))


def attend_forward(qkv_heads):
    queries, keys_all, values_all = (qkv_heads[0], qkv_heads[1], qkv_heads[2])
    block_rows = row_block()
    score_scale = HEAD_DIM ** (-0.5)

    def score_block(query_block):
        scores = (
            jnp.einsum("hdq,hdk->hqk", query_block, keys_all, preferred_element_type=jnp.float32)
            * score_scale
        )
        row_max = jnp.max(scores, -1, keepdims=True)
        row_total = jnp.sum(jnp.exp(scores - row_max), -1, keepdims=True)
        logsum = row_max + jnp.log(row_total)
        weights = jnp.exp(scores - logsum).astype(jnp.bfloat16)
        mixed_out = jnp.einsum(
            "hqk,hdk->hdq", weights, values_all, preferred_element_type=jnp.float32
        )
        return (mixed_out.astype(jnp.bfloat16), logsum[..., 0])

    context_all, logsums = lax.map(score_block, split_rows(queries, block_rows))
    return (join_rows(context_all), join_rows(logsums))


def attend_backward(triple):
    qkv_heads, logsums, context_grad = triple
    queries, keys_all, values_all = (qkv_heads[0], qkv_heads[1], qkv_heads[2])
    block_rows = row_block()
    score_scale = HEAD_DIM ** (-0.5)

    def grad_block(running, blocks):
        key_grad, value_grad = running
        query_block, out_block, logsum = blocks
        scores = (
            jnp.einsum("hdq,hdk->hqk", query_block, keys_all, preferred_element_type=jnp.float32)
            * score_scale
        )
        weights = jnp.exp(scores - logsum[..., None])
        prob_grad = jnp.einsum(
            "hdq,hdk->hqk", out_block, values_all, preferred_element_type=jnp.float32
        )
        row_inner = jnp.sum(weights * prob_grad, -1, keepdims=True)
        score_grad = (weights * (prob_grad - row_inner)).astype(jnp.bfloat16)
        value_grad = value_grad + jnp.einsum(
            "hqk,hdq->hdk",
            weights.astype(jnp.bfloat16),
            out_block,
            preferred_element_type=jnp.float32,
        )
        key_grad = (
            key_grad
            + jnp.einsum(
                "hqk,hdq->hdk", score_grad, query_block, preferred_element_type=jnp.float32
            )
            * score_scale
        )
        query_grad = (
            jnp.einsum("hqk,hdk->hdq", score_grad, keys_all, preferred_element_type=jnp.float32)
            * score_scale
        )
        return ((key_grad, value_grad), query_grad)

    empty_grad = jnp.zeros(keys_all.shape, jnp.float32)
    (key_grad, value_grad), query_grads = lax.scan(
        grad_block,
        (empty_grad, empty_grad),
        (
            split_rows(queries, block_rows),
            split_rows(context_grad, block_rows),
            split_rows(logsums, block_rows),
        ),
    )
    return jnp.stack([join_rows(query_grads), key_grad, value_grad]).astype(jnp.bfloat16)


def per_device(
    tokens,
    timesteps,
    time_table,
    ln1_gain,
    ln1_bias,
    qkv_weight,
    q_bias,
    v_bias,
    out_weight,
    out_bias,
    ln2_gain,
    ln2_bias,
    up_weight,
    up_bias,
    down_weight,
    down_bias,
    cotangent,
):
    group_size = lax.axis_size("seq")
    seq_count, local_len, model_width = tokens.shape
    length = group_size * local_len
    heads_here = model_width // HEAD_DIM // group_size
    group_width = heads_here * HEAD_DIM
    total_tokens = seq_count * length * lax.axis_size("dp")
    gain_one = ln1_gain.astype(jnp.float32)
    shift_one = ln1_bias.astype(jnp.float32)
    gain_two = ln2_gain.astype(jnp.float32)
    shift_two = ln2_bias.astype(jnp.float32)
    time_rows = jnp.take(time_table, timesteps, axis=0).astype(jnp.float32)
    start_sum = tokens.astype(jnp.float32) + time_rows[:, None, :]
    normed = layer_norm(start_sum, gain_one, shift_one).astype(jnp.bfloat16)
    bias_all = jnp.concatenate(
        [
            q_bias.astype(jnp.float32),
            jnp.zeros((model_width,), jnp.float32),
            v_bias.astype(jnp.float32),
        ]
    )
    projected = (
        jnp.einsum("std,dk->skt", normed, qkv_weight, preferred_element_type=jnp.float32)
        + bias_all[None, :, None]
    )
    projected = projected.astype(jnp.bfloat16).reshape(
        seq_count, 3, group_size, group_width, local_len
    )
    heads = lax.all_to_all(projected, "seq", split_axis=2, concat_axis=4, tiled=True).reshape(
        seq_count, 3, heads_here, HEAD_DIM, length
    )
    context, logsums = lax.map(attend_forward, heads)
    context = context.reshape(seq_count, group_width, group_size, local_len)
    context = lax.all_to_all(context, "seq", split_axis=2, concat_axis=1, tiled=True).reshape(
        seq_count, model_width, local_len
    )
    attn_out = jnp.einsum(
        "sdt,de->ste", context, out_weight, preferred_element_type=jnp.float32
    ) + out_bias.astype(jnp.float32)
    middle = start_sum + attn_out
    normed_two = layer_norm(middle, gain_two, shift_two).astype(jnp.bfloat16)
    hidden = jnp.einsum(
        "std,df->stf", normed_two, up_weight, preferred_element_type=jnp.float32
    ) + up_bias.astype(jnp.float32)
    active = exact_gelu(hidden).astype(jnp.bfloat16)
    output = middle + (
        jnp.einsum("stf,fe->ste", active, down_weight, preferred_element_type=jnp.float32)
        + down_bias.astype(jnp.float32)
    )
    energy = jnp.sum(jnp.mean(output * output, -1), -1)
    buckets = timesteps * BUCKETS // TSTEPS
    member = (buckets[:, None] == jnp.arange(BUCKETS)[None, :]).astype(jnp.float32)
    local_stats = (
        jnp.stack([jnp.sum(member * energy[:, None], 0), jnp.sum(member, 0) * local_len])
        / total_tokens
    )
    stats = lax.psum(local_stats, ("dp", "seq"))
    out_grad = cotangent.astype(jnp.float32)
    down_bias_grad = jnp.sum(out_grad, (0, 1))
    down_weight_grad = jnp.einsum(
        "stf,ste->fe", active, cotangent, preferred_element_type=jnp.float32
    )
    active_grad = jnp.einsum(
        "ste,fe->stf", cotangent, down_weight, preferred_element_type=jnp.float32
    )
    _, gelu_pull = jax.vjp(exact_gelu, hidden)
    hidden_grad = gelu_pull(active_grad)[0].astype(jnp.bfloat16)
    up_bias_grad = jnp.sum(hidden_grad.astype(jnp.float32), (0, 1))
    up_weight_grad = jnp.einsum(
        "std,stf->df", normed_two, hidden_grad, preferred_element_type=jnp.float32
    )
    normed_two_grad = jnp.einsum(
        "stf,df->std", hidden_grad, up_weight, preferred_element_type=jnp.float32
    )
    _, second_pull = jax.vjp(layer_norm, middle, gain_two, shift_two)
    middle_part, gain_two_grad, shift_two_grad = second_pull(normed_two_grad)
    middle_grad = out_grad + middle_part
    branch_grad = middle_grad.astype(jnp.bfloat16)
    out_bias_grad = jnp.sum(branch_grad.astype(jnp.float32), (0, 1))
    out_weight_grad = jnp.einsum(
        "sdt,ste->de", context, branch_grad, preferred_element_type=jnp.float32
    )
    context_grad = jnp.einsum(
        "ste,de->sdt", branch_grad, out_weight, preferred_element_type=jnp.float32
    ).astype(jnp.bfloat16)
    context_grad = context_grad.reshape(seq_count, group_size, group_width, local_len)
    context_grad = lax.all_to_all(
        context_grad, "seq", split_axis=1, concat_axis=3, tiled=True
    ).reshape(seq_count, heads_here, HEAD_DIM, length)
    qkv_grad = lax.map(attend_backward, (heads, logsums, context_grad))
    qkv_grad = qkv_grad.reshape(seq_count, 3, group_width, group_size, local_len)
    qkv_grad = lax.all_to_all(qkv_grad, "seq", split_axis=3, concat_axis=2, tiled=True).reshape(
        seq_count, 3 * model_width, local_len
    )
    column_sums = jnp.sum(qkv_grad.astype(jnp.float32), (0, 2))
    q_bias_grad = column_sums[:model_width]
    v_bias_grad = column_sums[2 * model_width :]
    qkv_weight_grad = jnp.einsum(
        "std,skt->dk", normed, qkv_grad, preferred_element_type=jnp.float32
    )
    normed_grad = jnp.einsum(
        "skt,dk->std", qkv_grad, qkv_weight, preferred_element_type=jnp.float32
    )
    _, first_pull = jax.vjp(layer_norm, start_sum, gain_one, shift_one)
    start_part, gain_one_grad, shift_one_grad = first_pull(normed_grad)
    start_grad = middle_grad + start_part
    seq_sums = jnp.sum(start_grad, 1)
    chosen = (timesteps[:, None] == jnp.arange(time_table.shape[0])[None, :]).astype(jnp.float32)
    dense_table = jnp.dot(chosen.T, seq_sums, precision=lax.Precision.HIGHEST)
    table_grad = lax.psum_scatter(dense_table, "dp", scatter_dimension=0, tiled=True)
    (
        gain_one_grad,
        shift_one_grad,
        qkv_weight_grad,
        q_bias_grad,
        v_bias_grad,
        out_weight_grad,
        out_bias_grad,
        gain_two_grad,
        shift_two_grad,
        up_weight_grad,
        up_bias_grad,
        down_weight_grad,
        down_bias_grad,
    ) = (
        lax.psum_scatter(gain_one_grad, "dp", scatter_dimension=0, tiled=True),
        lax.psum_scatter(shift_one_grad, "dp", scatter_dimension=0, tiled=True),
        lax.psum_scatter(qkv_weight_grad, "dp", scatter_dimension=0, tiled=True),
        lax.psum_scatter(q_bias_grad, "dp", scatter_dimension=0, tiled=True),
        lax.psum_scatter(v_bias_grad, "dp", scatter_dimension=0, tiled=True),
        lax.psum_scatter(out_weight_grad, "dp", scatter_dimension=0, tiled=True),
        lax.psum_scatter(out_bias_grad, "dp", scatter_dimension=0, tiled=True),
        lax.psum_scatter(gain_two_grad, "dp", scatter_dimension=0, tiled=True),
        lax.psum_scatter(shift_two_grad, "dp", scatter_dimension=0, tiled=True),
        lax.psum_scatter(up_weight_grad, "dp", scatter_dimension=0, tiled=True),
        lax.psum_scatter(up_bias_grad, "dp", scatter_dimension=0, tiled=True),
        lax.psum_scatter(down_weight_grad, "dp", scatter_dimension=0, tiled=True),
        lax.psum_scatter(down_bias_grad, "dp", scatter_dimension=0, tiled=True),
    )
    (
        table_grad,
        gain_one_grad,
        shift_one_grad,
        qkv_weight_grad,
        q_bias_grad,
        v_bias_grad,
        out_weight_grad,
        out_bias_grad,
        gain_two_grad,
        shift_two_grad,
        up_weight_grad,
        up_bias_grad,
        down_weight_grad,
        down_bias_grad,
    ) = (
        lax.psum(table_grad.astype(jnp.bfloat16), "seq").astype(jnp.float32),
        lax.psum(gain_one_grad.astype(jnp.bfloat16), "seq").astype(jnp.float32),
        lax.psum(shift_one_grad.astype(jnp.bfloat16), "seq").astype(jnp.float32),
        lax.psum(qkv_weight_grad.astype(jnp.bfloat16), "seq").astype(jnp.float32),
        lax.psum(q_bias_grad.astype(jnp.bfloat16), "seq").astype(jnp.float32),
        lax.psum(v_bias_grad.astype(jnp.bfloat16), "seq").astype(jnp.float32),
        lax.psum(out_weight_grad.astype(jnp.bfloat16), "seq").astype(jnp.float32),
        lax.psum(out_bias_grad.astype(jnp.bfloat16), "seq").astype(jnp.float32),
        lax.psum(gain_two_grad.astype(jnp.bfloat16), "seq").astype(jnp.float32),
        lax.psum(shift_two_grad.astype(jnp.bfloat16), "seq").astype(jnp.float32),
        lax.psum(up_weight_grad.astype(jnp.bfloat16), "seq").astype(jnp.float32),
        lax.psum(up_bias_grad.astype(jnp.bfloat16), "seq").astype(jnp.float32),
        lax.psum(down_weight_grad.astype(jnp.bfloat16), "seq").astype(jnp.float32),
        lax.psum(down_bias_grad.astype(jnp.bfloat16), "seq").astype(jnp.float32),
    )
    return (
        output.astype(jnp.bfloat16),
        start_grad,
        table_grad,
        gain_one_grad,
        shift_one_grad,
        qkv_weight_grad,
        q_bias_grad,
        v_bias_grad,
        out_weight_grad,
        out_bias_grad,
        gain_two_grad,
        shift_two_grad,
        up_weight_grad,
        up_bias_grad,
        down_weight_grad,
        down_bias_grad,
        stats[0],
        stats[1],
    )


def solution(mesh):
    placed = (
        P("dp", "seq", None),
        P("dp"),
        P(),
        P(),
        P(),
        P(),
        P(),
        P(),
        P(),
        P(),
        P(),
        P(),
        P(),
        P(),
        P(),
        P(),
        P("dp", "seq", None),
    )
    return jax.shard_map(
        per_device,
        mesh=mesh,
        in_specs=placed,
        out_specs=(
            P("dp", "seq", None),
            P("dp", "seq", None),
            P("dp", None),
            P("dp"),
            P("dp"),
            P("dp", None),
            P("dp"),
            P("dp"),
            P("dp", None),
            P("dp"),
            P("dp"),
            P("dp"),
            P("dp", None),
            P("dp"),
            P("dp", None),
            P("dp"),
            P(),
            P(),
        ),
        check_vma=False,
    )
```

profile of v0, /device:TPU:0, one launch (start us, length us, event | category | flops | bytes accessed | tf_op | source)
XLA Modules:
  0.0 1173.1 jit_solution(7314857058552122478)
XLA Ops:
  20.6 8.2 fusion.41
  28.8 6.6 copy.125
  35.5 5.0 copy.126
  40.4 6.5 all-to-all-start
  47.0 104.7 %all-to-all-done = bf16[2,3,4,192,512]{4,3,1,0,2:T(8,128)(2,1)} async-done(((bf16[2,3,4,192,512]{4,3,1,0,2:T(8,128)(2,1)}), bf16[2,3,4,192,512]{4,3,1,0,2:T(8,128)(2,1)}, u32[]{:S(2)}, u32[]{:S(2)}) %all-to-all-start) | async-done | bytes 4718624 | tf_op jit(solution)/shard_map/all_to_all | solution.py:158
  151.7 8.1 copy.127
  159.9 8.7 reshape.269
  168.6 119.2 %while.50 = (s32[]{:T(128)}, bf16[2,3,64,2048]{3,2,1,0:T(8,128)(2,1)}, f32[2,3,2048]{2,1,0:T(4,128)}, bf16[2,3,3,64,2048]{4,3,2,1,0:T(8,128)(2,1)}, s32[]{:T(128)}, /*index=5*/s32[]{:T(128)}, s32[]{}, s32[]{}, s32[]{:T(128)}) while((s32[]{:T(128)}, bf16[2,3,64,2048]{3,2,1,0:T(8,128)(2,1)}, f32[2,3,2048]{2,1,0:T(4,128)}, ...), condition=%wide.region_7.8_spmd, body=%wide.region_2.7_spmd.sunk | while | flops 830568960 | bytes 52414768 | solution.py:161
  176.9 42.5 %while.53 = (s32[]{:T(128)}, bf16[4,3,64,512]{3,2,1,0:T(8,128)(2,1)}, f32[4,3,512]{2,1,0:T(4,128)}, bf16[4,3,64,512]{3,2,1,0:T(8,128)(2,1)}, bf16[3,64,2048]{2,1...) while((s32[]{:T(128)}, bf16[4,3,64,512]{3,2,1,0:T(8,128)(2,1)}, f32[4,3,512]{2,1,0:T(4,128)}, ...), condition=%wide.region_6.6_spmd, body=%wide.region_3.5_spmd.sunk | while | flops 830568960 | bytes 39766112 | solution.py:57
  236.5 42.5 %while.53 = (s32[]{:T(128)}, bf16[4,3,64,512]{3,2,1,0:T(8,128)(2,1)}, f32[4,3,512]{2,1,0:T(4,128)}, bf16[4,3,64,512]{3,2,1,0:T(8,128)(2,1)}, bf16[3,64,2048]{2,1...) while((s32[]{:T(128)}, bf16[4,3,64,512]{3,2,1,0:T(8,128)(2,1)}, f32[4,3,512]{2,1,0:T(4,128)}, ...), condition=%wide.region_6.6_spmd, body=%wide.region_3.5_spmd.sunk | while | flops 830568960 | bytes 39766112 | solution.py:57
  302.8 33.2 %all-to-all-done.1 = bf16[2,192,4,512]{3,1,0,2:T(8,128)(2,1)} async-done(((bf16[2,192,4,512]{3,1,0,2:T(8,128)(2,1)}), bf16[2,192,4,512]{3,1,0,2:T(8,128)(2,1)}, u32[]{:S(2)}, u32[]{:S(2)}) %all-to-all-start.1) | async-done | bytes 1572896 | tf_op jit(solution)/shard_map/all_to_all | solution.py:163
  342.4 13.3 %fusion.56 = (u8[512,3072]{1,0:T(8,128)(4,1)S(1)}, u8[512,3072]{1,0:T(8,128)(4,1)S(1)}, f32[2,512,3072]{2,1,0:T(8,128)}) fusion(f32[3072]{0:T(1024)S(1)} %copy-done.20, bf16[768,3072]{1,0:T(8,128)(2,1)S(1)} %bitcast.236, f32[2,512,768]{2,1,0:T(8,128)S(1)} %get-tuple-element.342, f32[768]{0:T(1024)S(1)} %convert_element_type.202, ...), kind=kOutput, calls=%fused_computation.120 | convolution fusion | flops 4876664832 | bytes 23619584 | tf_op jit(solution)/shard_map/std,df->stf/dot_general | solution.py:171
  355.8 31.9 %multiply_convert_fusion.1 = (bf16[2,512,3072]{2,1,0:T(8,128)(2,1)}, f32[2,512,3072]{2,1,0:T(8,128)}) fusion(f32[2,512,3072]{2,1,0:T(8,128)} %get-tuple-element.343, f32[3072]{0:T(1024)S(1)} %copy-done.20, u8[512,3072]{1,0:T(8,128)(4,1)S(1)} %get-tuple-element.229, u8[512,3072]{1,0:T(8,128)(4,1)S(1)} %get-tuple-element.228), kind=kLoop, calls=%fused_computation.69 | loop fusion | flops 223346688 | bytes 34615296 | tf_op jit(solution)/shard_map/convert_element_type | solution.py:174
  387.6 18.7 %convert_reduce_fusion = (f32[3072]{0:T(1024)}, bf16[2,512,3072]{2,1,0:T(8,128)(2,1)}) fusion(f32[2,512,3072]{2,1,0:T(8,128)} %get-tuple-element.319, bf16[2,512,768]{2,1,0:T(8,128)(2,1)} %param.41, bf16[3072,768]{1,0:T(8,128)(2,1)} %param.39, f32[2,512,3072]{2,1,0:T(8,128)} %get-tuple-element.343, f32[3072]{0:T(1024)S(1)} %copy-done.20), kind=kOutput, calls=%fused_computation.67 | convolution fusion | flops 4885312512 | bytes 37773312 | tf_op jit(solution)/shard_map/ste,fe->stf/dot_general | solution.py:192
  406.4 10.0 multiply_reduce_fusion.3
  424.5 9.9 convolution_bitcast_fusion
  448.6 11.1 convolution_bitcast_fusion.1
  459.8 25.3 %all-to-all-done.2 = bf16[2,4,192,512]{3,2,0,1:T(8,128)(2,1)} async-done(((bf16[2,4,192,512]{3,2,0,1:T(8,128)(2,1)}), bf16[2,4,192,512]{3,2,0,1:T(8,128)(2,1)}, u32[]{:S(2)}, u32[]{:S(2)}) %all-to-all-start.2) | async-done | bytes 1572896 | tf_op jit(solution)/shard_map/all_to_all | solution.py:216
  492.9 276.9 %while.52 = (s32[]{:T(128)}, bf16[2,3,3,64,2048]{4,3,2,1,0:T(8,128)(2,1)}, bf16[2,3,3,64,2048]{4,3,2,1,0:T(8,128)(2,1)}, bf16[2,3,64,2048]{3,2,1,0:T(8,128)(2,1)...) while((s32[]{:T(128)}, ...), condition=%wide.region_16.17_spmd, body=%wide.region_12.16_spmd.sunk | while | flops 2060941824 | bytes 157772240 | solution.py:219
  510.2 113.3 %while.54 = (s32[]{:T(128)}, f32[3,64,2048]{2,1,0:T(8,128)}, f32[3,64,2048]{2,1,0:T(8,128)}, bf16[4,3,64,512]{3,2,1,0:T(8,128)(2,1)}, bf16[4,3,64,512]{3,2,1,0:T...) while((s32[]{:T(128)}, f32[3,64,2048]{2,1,0:T(8,128)}, ...), condition=%wide.region_15.15_spmd.clone, body=%wide.region_13.14_spmd.clone.sunk | while | flops 2053077504 | bytes 129411248 | solution.py:100
  527.8 6.4 fusion.126
  541.4 5.1 fusion.125
  555.8 6.3 fusion.126
  570.7 5.1 fusion.125
  575.8 4.9 multiply_reduce_fusion.12
  585.4 6.1 fusion.126
  599.2 5.1 fusion.125
  609.0 4.7 multiply_convert_fusion.3
  613.7 5.8 fusion.126
  649.6 110.6 %while.54 = (s32[]{:T(128)}, f32[3,64,2048]{2,1,0:T(8,128)}, f32[3,64,2048]{2,1,0:T(8,128)}, bf16[4,3,64,512]{3,2,1,0:T(8,128)(2,1)}, bf16[4,3,64,512]{3,2,1,0:T...) while((s32[]{:T(128)}, f32[3,64,2048]{2,1,0:T(8,128)}, ...), condition=%wide.region_15.15_spmd.clone, body=%wide.region_13.14_spmd.clone.sunk | while | flops 2053077504 | bytes 129411248 | solution.py:100
  667.2 5.8 fusion.126
  680.2 5.1 fusion.125
  694.6 5.8 fusion.126
  708.1 5.2 fusion.125
  722.5 5.8 fusion.126
  736.0 5.2 fusion.125
  750.5 5.8 fusion.126
  769.8 8.9 reshape.274
  782.1 105.2 %all_to_all.60 = bf16[2,3,192,4,512]{4,2,1,0,3:T(8,128)(2,1)S(1)} all-to-all(bf16[2,3,192,4,512]{4,2,1,0,3:T(8,128)(2,1)S(1)} %copy.134), channel_id=1, replica_groups=mesh['dp'=8,'seq'=4] {'seq'}, dimensions={3} | all-to-all | bytes 9437184 | tf_op jit(solution)/shard_map/all_to_all | solution.py:221
  889.9 5.3 fusion.71
  901.1 4.7 fusion.64
  906.0 10.8 convolution_bitcast_fusion.2
  924.8 43.3 %reduce-scatter.6.cloned.1.call-done = f32[256,768]{1,0:T(8,128)} async-done(((f32[2048,768]{1,0:T(8,128)}), f32[256,768]{1,0:T(8,128)}) %reduce-scatter.6.cloned.1.call-update) | async-done | bytes 786448 | tf_op jit(solution)/shard_map/reduce_scatter | solution.py:239
  970.0 67.0 %reduce-scatter.8.cloned.1.call-done = f32[96,2304]{1,0:T(8,128)} async-done(((f32[768,2304]{1,0:T(8,128)}), f32[96,2304]{1,0:T(8,128)}) %reduce-scatter.8.cloned.1.call-update) | async-done | bytes 884752 | tf_op jit(solution)/shard_map/reduce_scatter | solution.py:257
  1039.0 10.1 multiply_reduce_fusion.2
  1050.0 42.9 %psum.119 = f32[2,4]{1,0:T(2,128)} all-reduce(f32[2,4]{1,0:T(2,128)S(1)} %maximum_multiply_fusion), channel_id=1, replica_groups=mesh['dp'=8,'seq'=4] {'dp','seq'}, use_global_device_ids=true, to_apply=%region_60.61 | all-reduce | flops 8 | bytes 64 | tf_op jit(solution)/shard_map/psum | solution.py:186
  1100.0 26.6 %all-reduce.9 = (bf16[768]{0:T(1024)(128)(2,1)S(1)}, bf16[768]{0:T(1024)(128)(2,1)}, bf16[768]{0:T(1024)(128)(2,1)}, bf16[768]{0:T(1024)(128)(2,1)}, bf16[768]{0...) all-reduce(f32[768]{0:T(1024)S(1)} %copy-done.30, ...), channel_id=3, replica_groups=mesh['dp'=8,'seq'=4] {'dp'}, use_global_device_ids=true, to_apply=%region_23.24.clone | all-reduce | flops 9216 | bytes 55296
  1135.7 11.6 all-reduce.10
  (317 shorter events, 430.1 us)
Async XLA Ops:
  7.2 13.4 %copy-start = (bf16[768,2304]{1,0:T(8,128)(2,1)S(1)}, bf16[768,2304]{1,0:T(8,128)(2,1)}, u32[]{:S(2)}) copy-start(bf16[768,2304]{1,0:T(8,128)(2,1)} %param.30) | copy-start | bytes 10616836
  10.4 18.5 %copy-start.21 = (f32[768]{0:T(1024)}, f32[768]{0:T(1024)S(1)}, u32[]{:S(2)}) copy-start(f32[768]{0:T(1024)S(1)} %convert_element_type.193) | copy-start | bytes 9220
  11.1 17.8 %copy-start.32 = (f32[768]{0:T(1024)}, f32[768]{0:T(1024)S(1)}, u32[]{:S(2)}) copy-start(f32[768]{0:T(1024)S(1)} %convert_element_type.194) | copy-start | bytes 9220
  14.7 5.9 copy-start.15
  16.5 4.1 copy-start.18
  40.4 111.3 %all-to-all-start = ((bf16[2,3,4,192,512]{4,3,1,0,2:T(8,128)(2,1)}), bf16[2,3,4,192,512]{4,3,1,0,2:T(8,128)(2,1)}, u32[]{:S(2)}, u32[]{:S(2)}) async-start(bf16[2,3,4,192,512]{4,3,1,0,2:T(8,128)(2,1)} %copy.126), calls=%async_computation | async-start | bytes 9437184 | tf_op jit(solution)/shard_map/all_to_all | solution.py:158
  292.1 7.4 copy-start.33
  295.0 42.6 %copy-start.16 = (f32[2,768]{1,0:T(2,128)S(1)}, f32[2,768]{1,0:T(2,128)}, u32[]{:S(2)}) copy-start(f32[2,768]{1,0:T(2,128)} %copy-done.15) | copy-start | bytes 18436
  295.0 41.0 %all-to-all-start.1 = ((bf16[2,192,4,512]{3,1,0,2:T(8,128)(2,1)}), bf16[2,192,4,512]{3,1,0,2:T(8,128)(2,1)}, u32[]{:S(2)}, u32[]{:S(2)}) async-start(bf16[2,192,4,512]{3,1,0,2:T(8,128)(2,1)} %copy.128), calls=%async_computation.1 | async-start | bytes 3145728 | tf_op jit(solution)/shard_map/all_to_all | solution.py:163
  299.5 619.3 %reduce-scatter.10.cloned.1.call-start = ((), (), s32[]{:S(2)}) async-start(), calls=%async_computation.11 | async-start | bytes 2654208 | tf_op jit(solution)/shard_map/reduce_scatter | solution.py:260
  336.0 6.4 slice-start
  337.6 4.2 copy-start.11
  337.7 4.7 copy-start.20
  337.7 4.7 slice-start.1
  341.8 74.6 %copy-start.6 = (f32[2,512,768]{2,1,0:T(8,128)}, f32[2,512,768]{2,1,0:T(8,128)S(1)}, u32[]{:S(2)}) copy-start(f32[2,512,768]{2,1,0:T(8,128)S(1)} %get-tuple-element.342) | copy-start | bytes 9437188
  416.4 2.9 copy-start.8
  417.7 3.9 copy-start.12
  417.7 2.8 copy-start.25
  424.4 496.1 %reduce-scatter.14.cloned.1.call-start = ((), (), s32[]{:S(2)}) async-start(), calls=%async_computation.13 | async-start | bytes 10616832 | tf_op jit(solution)/shard_map/reduce_scatter | solution.py:266
  444.2 40.9 %all-to-all-start.2 = ((bf16[2,4,192,512]{3,2,0,1:T(8,128)(2,1)}), bf16[2,4,192,512]{3,2,0,1:T(8,128)(2,1)}, u32[]{:S(2)}, u32[]{:S(2)}) async-start(bf16[2,4,192,512]{3,2,0,1:T(8,128)(2,1)} %copy.132), calls=%async_computation.2 | async-start | bytes 3145728 | tf_op jit(solution)/shard_map/all_to_all | solution.py:216
  448.5 474.2 %reduce-scatter.12.cloned.1.call-start = ((), (), s32[]{:S(2)}) async-start(), calls=%async_computation.12 | async-start | bytes 10616832 | tf_op jit(solution)/shard_map/reduce_scatter | solution.py:264
  459.7 508.4 %reduce-scatter.6.cloned.1.call-start = ((), (), s32[]{:S(2)}) async-start(), calls=%async_computation.9 | async-start | bytes 7077888 | tf_op jit(solution)/shard_map/reduce_scatter | solution.py:239
  527.8 6.4 copy-start.1
  555.8 6.8 copy-start.1
  585.4 6.1 copy-start.1
  613.7 5.8 copy-start.1
  667.2 5.8 copy-start.1
  694.6 5.8 copy-start.1
  722.5 5.8 copy-start.1
  750.4 5.8 copy-start.1
  887.3 2.5 copy-start.7
  887.3 2.5 copy-start.17
  887.3 2.5 copy-start.19
  887.3 2.5 copy-start.22
  889.5 5.7 copy-start.10
  889.9 5.3 copy-start.28
  889.9 5.3 copy-start.24
  895.2 2.4 copy-start.5
  895.2 2.4 copy-start.9
  895.2 2.4 copy-start.26
  897.5 3.5 copy-start.36
  905.8 131.2 %reduce-scatter.8.cloned.1.call-start = ((), (), s32[]{:S(2)}) async-start(), calls=%async_computation.10 | async-start | bytes 7962624 | tf_op jit(solution)/shard_map/reduce_scatter | solution.py:257
  916.9 240.3 %all-reduce.14.cloned.1.call-start = ((), (), s32[]{:S(2)}) async-start(), calls=%async_computation.14 | async-start | bytes 4325376 | tf_op jit(solution)/shard_map/psum | solution.py:285
  1039.0 10.3 copy-start.35
  1049.1 50.9 %copy-start.29 = (f32[768]{0:T(1024)S(1)}, f32[768]{0:T(1024)}, u32[]{:S(2)}) copy-start(f32[768]{0:T(1024)} %get-tuple-element.312) | copy-start | bytes 9220
  1049.1 50.9 %copy-start.30 = (f32[768]{0:T(1024)S(1)}, f32[768]{0:T(1024)}, u32[]{:S(2)}) copy-start(f32[768]{0:T(1024)} %get-tuple-element.232) | copy-start | bytes 9220
  1049.1 50.9 %copy-start.31 = (f32[768]{0:T(1024)S(1)}, f32[768]{0:T(1024)}, u32[]{:S(2)}) copy-start(f32[768]{0:T(1024)} %get-tuple-element.334) | copy-start | bytes 9220
  1157.1 7.8 copy-start.14
  (9 other events, 12.8 us)
Sparse Core Ops, SparseCore 0:
  424.5 41.6 reduce-scatter.9
  470.2 76.4 reduce-scatter.13
  550.6 76.4 reduce-scatter.11
  905.9 62.1 reduce-scatter.5
  971.5 65.4 reduce-scatter.7
  1041.0 91.7 all-reduce.13
where the time goes:
time: 1190 us; the launch traced here: 1170 us
  matrix products  354 us (30%)
  waiting for transfers between devices  274 us (23%)
  blocking collectives  186 us (16%)
  local copies, waits for them, and re-layouts  171 us (14%)
  other arithmetic  155 us (13%)
  between operations  16.1 us (1%)
  starting transfers between devices  15.8 us (1%)
    all_to_all x1, blocking collectives, per_device(): lax.all_to_all(qkv_grad, 'seq', split_axis=3, concat_axis=2, tiled=True)  105 us
    all_to_all x1, waiting for transfers between devices, per_device(): lax.all_to_all(projected, 'seq', split_axis=2, concat_axis=4, tiled=True)  105 us
    reduce_scatter x1, waiting for transfers between devices, per_device(): lax.psum_scatter(qkv_weight_grad, 'dp', scatter_dimension=0, tiled=True)  67 us
    dot_general x8, matrix products, grad_block(): jnp.einsum('hqk,hdk->hdq', score_grad, keys_all, preferred_element_type=j...  47.9 us
    reduce_scatter x1, waiting for transfers between devices, per_device(): lax.psum_scatter(dense_table, 'dp', scatter_dimension=0, tiled=True)  43.3 us
    psum x1, blocking collectives, per_device(): stats = lax.psum(local_stats, ('dp', 'seq'))  42.9 us
    dot_general x8, matrix products, grad_block(): jnp.einsum('hqk,hdq->hdk', weights.astype(jnp.bfloat16), out_block, prefe...  40 us
    convert_element_type x8, other arithmetic, grad_block(): score_grad = (weights * (prob_grad - row_inner)).astype(jnp.bfloat16)  37.4 us
  transfers between devices with their start and end apart: 9, of which 5 were waited for; matrix products, arithmetic and copies ran while one was open for 34% of the time, Pallas kernels for 0%

commit v1 on v0

v1 whole, which is shorter than its diff:
```python
import functools

import jax
import jax.numpy as jnp
from jax import lax
from jax.experimental import pallas as pl
from jax.experimental.pallas import tpu as pltpu
from jax.sharding import PartitionSpec as P

HEAD_DIM = 64
TSTEPS = 2048
BUCKETS = 4
EPS = 1e-05
LANES = 128
VMEM_BYTES = 56 * 1024 * 1024
BOTH = ("dp", "seq")
F32 = jnp.float32
BF16 = jnp.bfloat16
NN = (((1,), (0,)), ((), ()))
NT = (((1,), (1,)), ((), ()))
TN = (((0,), (0,)), ((), ()))


def dot(a, b, dims):
    return lax.dot_general(a, b, dims, preferred_element_type=F32)


def wide(ref):
    return ref[...].astype(F32)


def column_sum(v):
    return jnp.sum(v, 0, keepdims=True)


def fixed(shape):
    return pl.BlockSpec(shape, lambda *i: (0,) * len(shape), pipeline_mode=pl.Buffered(1))


def rows(block, width):
    return pl.BlockSpec((block, width), lambda i: (i, 0))


def shape_of(shape, dtype=BF16):
    return jax.ShapeDtypeStruct(shape, dtype)


def cost(us):
    return pl.CostEstimate(flops=int(us * 1.15e9), bytes_accessed=0, transcendentals=0)


def params():
    return pltpu.CompilerParams(vmem_limit_bytes=VMEM_BYTES)


def norm_parts(v):
    centered = v - jnp.mean(v, -1, keepdims=True)
    scale = lax.rsqrt(jnp.mean(centered * centered, -1, keepdims=True) + EPS)
    return centered * scale, scale


def norm_backward(grad, gain, unit, scale):
    scaled = grad * gain
    return scale * (
        scaled
        - jnp.mean(scaled, -1, keepdims=True)
        - unit * jnp.mean(scaled * unit, -1, keepdims=True)
    )


def project_kernel(x_ref, time_ref, gain_ref, shift_ref, weight_ref, bias_ref, *refs):
    normed_ref, query_ref, kv_ref = refs[-3:]
    width = x_ref.shape[1]
    unit, _ = norm_parts(wide(x_ref) + wide(time_ref))
    normed = (unit * wide(gain_ref) + wide(shift_ref)).astype(BF16)
    normed_ref[...] = normed
    for part in range(3):
        columns = slice(part * width, (part + 1) * width)
        made = (dot(normed, weight_ref[:, columns], NN) + bias_ref[:, columns]).astype(BF16)
        if part == 0:
            query_ref[...] = made * jnp.asarray(HEAD_DIM ** (-0.5), BF16)
        else:
            kv_ref[:, (part - 1) * width : part * width] = made


def project(x, time_row, gain, shift, weight, bias, total, begun=None, block=256):
    count, width = x.shape
    first = 0 if begun is None else total // block - count // block
    later = pl.BlockSpec((block, width), lambda i: (i + first, 0))
    extra = [] if begun is None else list(begun)
    return pl.pallas_call(
        project_kernel,
        grid=(count // block,),
        in_specs=[
            rows(block, width),
            fixed((1, width)),
            fixed((1, width)),
            fixed((1, width)),
            fixed(weight.shape),
            fixed(bias.shape),
        ]
        + [pl.BlockSpec(memory_space=pl.ANY)] * len(extra),
        out_specs=[later, later, rows(block, 2 * width)],
        out_shape=[
            shape_of((total, width)),
            shape_of((total, width)),
            shape_of((count, 2 * width)),
        ],
        input_output_aliases={6: 0, 7: 1} if extra else {},
        compiler_params=params(),
        cost_estimate=cost(5),
        name="project",
    )(x, time_row, gain, shift, weight, bias, *extra)


def lane_parts():
    lane = lax.broadcasted_iota(jnp.int32, (1, LANES), 1)
    return lane < HEAD_DIM, lane % HEAD_DIM


def with_offset(own, place, base, offset):
    high = offset.astype(BF16)
    left = offset - high.astype(F32)
    mid = left.astype(BF16)
    low = (left - mid.astype(F32)).astype(BF16)
    zero = jnp.zeros_like(low)
    parts = jnp.where(place == 0, high, jnp.where(place == 1, mid, jnp.where(place == 2, low, zero)))
    return jnp.where(own, base, parts)


def attend_kernel(query_ref, *refs, pieces):
    key_refs, value_refs = refs[:pieces], refs[pieces : 2 * pieces]
    context_ref, logsum_ref = refs[2 * pieces :]
    count = query_ref.shape[0]
    low, place = lane_parts()
    row_half = lax.broadcasted_iota(jnp.int32, (LANES, LANES), 0) // HEAD_DIM
    lane_half = lax.broadcasted_iota(jnp.int32, (LANES, LANES), 1) // HEAD_DIM
    swapped = jnp.where(row_half != lane_half, 1.0, 0.0).astype(BF16)
    query = query_ref[...]

    def norms(v):
        v = v.astype(F32)
        return dot((v * v).astype(BF16), swapped, NN)

    key_norm = functools.reduce(
        jnp.maximum, [jnp.max(norms(ref[...]), 0, keepdims=True) for ref in key_refs]
    )
    bound = jnp.sqrt(norms(query) * key_norm) * 1.01
    ones_key = jnp.where(place < 3, 1.0, 0.0).astype(BF16)
    values = [ref[...].T for ref in value_refs]
    ones = jnp.ones((16, value_refs[0].shape[0]), BF16)

    def value_of(piece, head):
        return jnp.concatenate([values[piece][head * HEAD_DIM : (head + 1) * HEAD_DIM], ones], 0)

    def finish(mixed, offset):
        totals = [m[HEAD_DIM : HEAD_DIM + 1] for m in mixed]
        context = jnp.concatenate([m[:HEAD_DIM] / t for m, t in zip(mixed, totals)], 0)
        context_ref[...] = context.T.astype(BF16)
        logs = [jnp.broadcast_to(jnp.log(t), (HEAD_DIM, count)) for t in reversed(totals)]
        logsum_ref[...] = jnp.concatenate(logs, 0).T + offset

    mixed = []
    for head in range(2):
        own = low if head == 0 else ~low
        query_own = with_offset(own, place, query, -bound)
        out = 0.0
        for piece in range(pieces):
            key_own = jnp.where(own, key_refs[piece][...], ones_key)
            weights = jnp.exp(dot(key_own, query_own, NT)).astype(BF16)
            out = out + dot(value_of(piece, head), weights, NN)
        mixed.append(out)
    finish(mixed, bound)
    smallest = jnp.min(jnp.minimum(mixed[0][HEAD_DIM], mixed[1][HEAD_DIM]))

    @pl.when(smallest < 1e-25)
    def _():
        again, tops = [], []
        for head in range(2):
            own = low if head == 0 else ~low
            query_own = jnp.where(own, query, jnp.zeros_like(query))
            top = jnp.full((1, count), -jnp.inf, F32)
            for piece in range(pieces):
                scores = dot(key_refs[piece][...], query_own, NT)
                top = jnp.maximum(top, jnp.max(scores, 0, keepdims=True))
            out = 0.0
            for piece in range(pieces):
                scores = dot(key_refs[piece][...], query_own, NT)
                out = out + dot(value_of(piece, head), jnp.exp(scores - top).astype(BF16), NN)
            again.append(out)
            tops.append(jnp.broadcast_to(top, (HEAD_DIM, count)))
        finish(again, jnp.concatenate(tops[::-1], 0).T)


def attend(query, kvs):
    count, width = query.shape
    pairs, pieces, length = width // LANES, len(kvs), kvs[0].shape[0]
    row = pl.BlockSpec((count, LANES), lambda p: (0, p))
    return pl.pallas_call(
        functools.partial(attend_kernel, pieces=pieces),
        grid=(pairs,),
        in_specs=[row]
        + [pl.BlockSpec((length, LANES), lambda p: (0, p))] * pieces
        + [pl.BlockSpec((length, LANES), lambda p: (0, pairs + p))] * pieces,
        out_specs=[row, row],
        out_shape=[shape_of((count, width)), shape_of((count, width), F32)],
        compiler_params=params(),
        cost_estimate=cost(32),
        name="attend",
    )(query, *kvs, *kvs)


def attend_back_kernel(query_ref, grad_ref, context_ref, logsum_ref, *refs, pieces):
    key_refs, value_refs = refs[:pieces], refs[pieces : 2 * pieces]
    query_grad_ref = refs[2 * pieces]
    key_grad_refs = refs[2 * pieces + 1 : 3 * pieces + 1]
    value_grad_refs = refs[3 * pieces + 1 :]
    low, place = lane_parts()
    query, grad = query_ref[...], grad_ref[...]
    product = grad.astype(F32) * wide(context_ref)
    logsum = logsum_ref[...]
    ones_key = jnp.where(place < 3, 1.0, 0.0).astype(BF16)
    zero = jnp.zeros_like(query)
    heads = []
    for head in range(2):
        own = low if head == 0 else ~low
        inner = jnp.sum(jnp.where(own, product, 0.0), -1, keepdims=True)
        heads.append(
            (
                own,
                with_offset(own, place, query, -logsum),
                with_offset(own, place, grad, jnp.broadcast_to(-inner, logsum.shape)),
                jnp.where(own, query, zero),
                jnp.where(own, grad, zero),
            )
        )
    query_grads = [0.0, 0.0]
    for piece in range(pieces):
        key, value = key_refs[piece][...], value_refs[piece][...]
        key_turned = key.T
        key_grad, value_grad = 0.0, 0.0
        for head, (own, query_off, grad_off, query_own, grad_own) in enumerate(heads):
            scores = dot(jnp.where(own, key, ones_key), query_off, NT)
            probs = jnp.exp(scores)
            prob_grad = dot(jnp.where(own, value, ones_key), grad_off, NT)
            score_grad = (probs * prob_grad).astype(BF16)
            value_grad = value_grad + dot(probs.astype(BF16), grad_own, NN)
            key_grad = key_grad + dot(score_grad, query_own, NN)
            lanes = slice(head * HEAD_DIM, (head + 1) * HEAD_DIM)
            query_grads[head] = query_grads[head] + dot(key_turned[lanes], score_grad, NN)
        key_grad_refs[piece][...] = key_grad.astype(BF16)
        value_grad_refs[piece][...] = value_grad.astype(BF16)
    turned = jnp.concatenate(query_grads, 0) * HEAD_DIM ** (-0.5)
    query_grad_ref[...] = turned.T.astype(BF16)


def attend_back(query, grad, context, logsum, kvs):
    count, width = query.shape
    pairs, pieces, length = width // LANES, len(kvs), kvs[0].shape[0]
    row = pl.BlockSpec((count, LANES), lambda p: (0, p))
    piece = pl.BlockSpec((length, LANES), lambda p: (0, p))
    return pl.pallas_call(
        functools.partial(attend_back_kernel, pieces=pieces),
        grid=(pairs,),
        in_specs=[row] * 4
        + [piece] * pieces
        + [pl.BlockSpec((length, LANES), lambda p: (0, pairs + p))] * pieces,
        out_specs=[row] + [piece] * (2 * pieces),
        out_shape=[shape_of((count, width))] + [shape_of((length, width))] * (2 * pieces),
        compiler_params=params(),
        cost_estimate=cost(75),
        name="attend_back",
    )(query, grad, context, logsum, *kvs, *kvs)


def gelu_parts(hidden):
    share = 0.5 + 0.5 * lax.erf(hidden * 2**-0.5)
    bell = jnp.exp(-0.5 * hidden * hidden) * 0.3989422804014327
    return hidden * share, share + hidden * bell


def feed_kernel(
    context_ref, x0_ref, x1_ref, time_ref, cot0_ref, cot1_ref, out_weight_ref, out_bias_ref,
    gain_ref, shift_ref, up_ref, up_bias_ref, down_ref, down_bias_ref,
    out_ref, active_ref, hidden_grad_ref, normed_ref, middle_grad_ref, branch_ref, context_grad_ref, sums_ref,
):
    step = pl.program_id(0)
    width, hidden_width = x0_ref.shape[1], up_ref.shape[1]

    @pl.when(step == 0)
    def _():
        sums_ref[...] = jnp.zeros_like(sums_ref)

    x = jnp.where(step == 0, x0_ref[...], x1_ref[...])
    cot = jnp.where(step == 0, cot0_ref[...], cot1_ref[...])
    middle = x.astype(F32) + wide(time_ref) + dot(context_ref[...], out_weight_ref[...], NN) + wide(out_bias_ref)
    unit, scale = norm_parts(middle)
    gain = wide(gain_ref)
    normed = (unit * gain + wide(shift_ref)).astype(BF16)
    normed_ref[...] = normed
    out = middle + wide(down_bias_ref)
    normed_grad = jnp.zeros_like(out)
    for part in range(hidden_width // width):
        columns = slice(part * width, (part + 1) * width)
        hidden = dot(normed, up_ref[:, columns], NN) + up_bias_ref[:, columns].astype(F32)
        active, slope = gelu_parts(hidden)
        active = active.astype(BF16)
        active_ref[:, columns] = active
        out = out + dot(active, down_ref[columns, :], NN)
        hidden_grad = (dot(cot, down_ref[columns, :], NT) * slope).astype(BF16)
        hidden_grad_ref[:, columns] = hidden_grad
        sums_ref[8 + part : 9 + part] += column_sum(hidden_grad.astype(F32))
        normed_grad = normed_grad + dot(hidden_grad, up_ref[:, columns], NT)
    out_ref[...] = out.astype(BF16)
    cot = cot.astype(F32)
    middle_grad = cot + norm_backward(normed_grad, gain, unit, scale)
    middle_grad_ref[...] = middle_grad
    branch = middle_grad.astype(BF16)
    branch_ref[...] = branch
    context_grad_ref[...] = dot(branch, out_weight_ref[...], NT).astype(BF16)
    sums_ref[0:1] += column_sum(cot)
    sums_ref[1:2] += column_sum(normed_grad * unit)
    sums_ref[2:3] += column_sum(normed_grad)
    sums_ref[3:4] += column_sum(branch.astype(F32))
    sums_ref[4:5] += column_sum(out * out)


def feed(context, xs, time_row, cots, out_weight, out_bias, gain, shift, up, up_bias, down, down_bias):
    block, width = xs[0].shape
    count, hidden_width = 2 * block, up.shape[1]
    sums_rows = 8 + hidden_width // width + (-(hidden_width // width)) % 8
    row = fixed((1, width))
    whole = fixed((block, width))
    return pl.pallas_call(
        feed_kernel,
        grid=(2,),
        in_specs=[
            rows(block, width), whole, whole, row, whole, whole, fixed(out_weight.shape), row, row, row,
            fixed(up.shape), fixed((1, hidden_width)), fixed(down.shape), row,
        ],
        out_specs=[
            rows(block, width), rows(block, hidden_width), rows(block, hidden_width), rows(block, width),
            rows(block, width), rows(block, width), rows(block, width),
            pl.BlockSpec((sums_rows, width), lambda i: (0, 0)),
        ],
        out_shape=[
            shape_of((count, width)), shape_of((count, hidden_width)), shape_of((count, hidden_width)),
            shape_of((count, width)), shape_of((count, width), F32), shape_of((count, width)),
            shape_of((count, width)), shape_of((sums_rows, width), F32),
        ],
        compiler_params=params(),
        cost_estimate=cost(34),
        name="feed",
    )(context, *xs, time_row, *cots, out_weight, out_bias, gain, shift, up, up_bias, down, down_bias)


def down_grad_kernel(active_ref, cot0_ref, cot1_ref, out_ref):
    block = cot0_ref.shape[0]
    out_ref[...] = (
        dot(active_ref[:block], cot0_ref[...], TN) + dot(active_ref[block:], cot1_ref[...], TN)
    ).astype(BF16)


def down_grad(active, cots):
    block, width = cots[0].shape
    count, hidden_width = active.shape
    return pl.pallas_call(
        down_grad_kernel,
        grid=(hidden_width // width,),
        in_specs=[pl.BlockSpec((count, width), lambda i: (0, i))] + [fixed((block, width))] * 2,
        out_specs=rows(width, width),
        out_shape=shape_of((hidden_width, width)),
        compiler_params=params(),
        cost_estimate=cost(8),
        name="down_grad",
    )(active, *cots)


def up_out_grad_kernel(normed_ref, hidden_grad_ref, context_ref, branch_ref, out_ref):
    last = pl.num_programs(0) - 1

    @pl.when(pl.program_id(0) < last)
    def _():
        out_ref[0] = dot(normed_ref[...], hidden_grad_ref[...], TN).astype(BF16)

    @pl.when(pl.program_id(0) == last)
    def _():
        out_ref[0] = dot(context_ref[...], branch_ref[...], TN).astype(BF16)


def up_out_grad(normed, hidden_grad, context, branch):
    count, width = normed.shape
    parts = hidden_grad.shape[1] // width
    whole = fixed((count, width))
    return pl.pallas_call(
        up_out_grad_kernel,
        grid=(parts + 1,),
        in_specs=[
            whole,
            pl.BlockSpec((count, width), lambda i: (0, jnp.minimum(i, parts - 1))),
            whole,
            whole,
        ],
        out_specs=pl.BlockSpec((1, width, width), lambda i: (i, 0, 0)),
        out_shape=shape_of((parts + 1, width, width)),
        compiler_params=params(),
        cost_estimate=cost(10),
        name="up_out_grad",
    )(normed, hidden_grad, context, branch)


def qkv_grad_kernel(normed_ref, grad_ref, out_ref):
    out_ref[0] = dot(normed_ref[...], grad_ref[...], TN).astype(BF16)


def qkv_grad(normed, grads):
    count, width = normed.shape
    parts = grads.shape[1] // width
    return pl.pallas_call(
        qkv_grad_kernel,
        grid=(parts,),
        in_specs=[fixed((count, width)), pl.BlockSpec((count, width), lambda i: (0, i))],
        out_specs=pl.BlockSpec((1, width, width), lambda i: (i, 0, 0)),
        out_shape=shape_of((parts, width, width)),
        compiler_params=params(),
        cost_estimate=cost(7),
        name="qkv_grad",
    )(normed, grads)


def start_kernel(
    query_grad_ref, key0_ref, key1_ref, far_key0_ref, far_key1_ref, value0_ref, value1_ref, far_value0_ref,
    far_value1_ref, x0_ref, x1_ref, time_ref, middle_grad_ref, gain_ref, weight_ref,
    token0_ref, token1_ref, grads_ref, sums_ref,
):
    step = pl.program_id(0)
    width = x0_ref.shape[1]

    @pl.when(step == 0)
    def _():
        sums_ref[...] = jnp.zeros_like(sums_ref)

    def pick(first, second):
        return jnp.where(step == 0, first[...], second[...])

    query_grad = query_grad_ref[...]
    key_grad = (pick(key0_ref, key1_ref).astype(F32) + pick(far_key0_ref, far_key1_ref).astype(F32)).astype(BF16)
    value_grad = (
        pick(value0_ref, value1_ref).astype(F32) + pick(far_value0_ref, far_value1_ref).astype(F32)
    ).astype(BF16)
    normed_grad = 0.0
    for part, grad in enumerate((query_grad, key_grad, value_grad)):
        columns = slice(part * width, (part + 1) * width)
        grads_ref[:, columns] = grad
        normed_grad = normed_grad + dot(grad, weight_ref[:, columns], NT)
    unit, scale = norm_parts(pick(x0_ref, x1_ref).astype(F32) + wide(time_ref))
    token_grad = middle_grad_ref[...] + norm_backward(normed_grad, wide(gain_ref), unit, scale)

    @pl.when(step == 0)
    def _():
        token0_ref[...] = token_grad.astype(BF16)

    @pl.when(step == 1)
    def _():
        token1_ref[...] = token_grad.astype(BF16)

    sums_ref[0:1] += column_sum(normed_grad * unit)
    sums_ref[1:2] += column_sum(normed_grad)
    sums_ref[2:3] += column_sum(query_grad.astype(F32))
    sums_ref[3:4] += column_sum(value_grad.astype(F32))
    sums_ref[4:5] += column_sum(token_grad)


def start_back(query_grad, key_grads, value_grads, xs, time_row, middle_grad, gain, weight):
    block, width = xs[0].shape
    count = 2 * block
    whole = fixed((block, width))
    row = fixed((1, width))
    kept = pl.BlockSpec((block, width), lambda i: (0, 0))
    return pl.pallas_call(
        start_kernel,
        grid=(2,),
        in_specs=[rows(block, width)]
        + [whole] * 10
        + [row, rows(block, width), row, fixed(weight.shape)],
        out_specs=[kept, kept, rows(block, 3 * width), pl.BlockSpec((8, width), lambda i: (0, 0))],
        out_shape=[
            shape_of((block, width)), shape_of((block, width)), shape_of((count, 3 * width)),
            shape_of((8, width), F32),
        ],
        compiler_params=params(),
        cost_estimate=cost(10),
        name="start_back",
    )(query_grad, *key_grads, *value_grads, *xs, time_row, middle_grad, gain, weight)


class Places:
    def __init__(self, dp, seq):
        self.dp, self.seq = dp, seq
        self.bits = dp.bit_length() - 1

    def flat(self, d, z):
        return d * self.seq + z

    def pairs(self, to):
        return [
            (self.flat(d, z), self.flat(*to(d, z))) for d in range(self.dp) for z in range(self.seq)
        ]

    def gather_order(self, turn):
        def to(d, z):
            core, j = d % 2, (z + turn) % 2
            return d - core + z // 2, 2 * core + j

        return self.pairs(to)

    def scatter_order(self, turn):
        return [(b, a) for a, b in self.gather_order(turn)]

    def swap(self, bit):
        return self.pairs(lambda d, z: (d ^ (1 << bit), z))

    def swap_seq(self, step):
        return self.pairs(lambda d, z: (d, z ^ step))


def send(x, order):
    return lax.ppermute(x, BOTH, order)


def add(a, b):
    return (a.astype(F32) + b.astype(F32)).astype(BF16)


def reduce_parts(parts, places):
    d, z = lax.axis_index("dp"), lax.axis_index("seq")
    count, height, width = parts.shape
    block = height // places.dp
    grid = parts.reshape((count,) + (2,) * places.bits + (block, width))

    def halve(value, bit, axes):
        axis = 1 + axes.index(bit)
        mine = (d >> bit) & 1
        kept = lax.dynamic_index_in_dim(value, mine, axis, keepdims=False)
        sent = lax.dynamic_index_in_dim(value, 1 - mine, axis, keepdims=False)
        axes.remove(bit)
        return add(kept, send(sent, places.swap(bit)))

    axes = list(range(places.bits - 1, -1, -1))
    grid = halve(grid, 0, axes)
    halves = []
    for number, order in enumerate((range(1, places.bits), range(places.bits - 1, 0, -1))):
        at = block // 2
        value = lax.slice_in_dim(grid, number * at, (number + 1) * at, axis=grid.ndim - 2)
        left = list(axes)
        for bit in order:
            value = halve(value, bit, left)
        halves.append(sum_along_seq(value, z, places))
    return jnp.concatenate(halves, 1)


def sum_along_seq(value, z, places):
    count, block, width = value.shape
    mine = z % 2
    grid = value.reshape(count, block, 2, width // 2)
    kept = lax.dynamic_index_in_dim(grid, mine, 2, keepdims=False)
    sent = lax.dynamic_index_in_dim(grid, 1 - mine, 2, keepdims=False)
    half = add(kept, send(sent, places.swap_seq(1)))
    half = add(half, send(half, places.swap_seq(2)))
    other = send(half, places.swap_seq(1))
    first = jnp.where(mine == 0, half, other)
    second = jnp.where(mine == 0, other, half)
    return jnp.concatenate([first, second], 2).astype(F32)


def sum_everywhere(value, places):
    for bit in range(places.bits):
        value = value + send(value, places.swap(bit))
    for step in (1, 2):
        value = value + send(value, places.swap_seq(step))
    return value


def per_device(
    tokens, timesteps, time_table, ln1_gain, ln1_bias, qkv_weight, q_bias, v_bias, out_weight, out_bias,
    ln2_gain, ln2_bias, up_weight, up_bias, down_weight, down_bias, cotangent,
):
    places = Places(lax.axis_size("dp"), lax.axis_size("seq"))
    seq_count, local_len, width = tokens.shape
    hidden_width = up_weight.shape[1]
    assert places.seq == 4 and seq_count == 2 and places.dp == 1 << places.bits
    d, z = lax.axis_index("dp"), lax.axis_index("seq")
    core = d % 2
    total_seqs = seq_count * places.dp
    total_tokens = total_seqs * local_len * places.seq

    def gathered(array):
        blocks = []
        for turn in range(2):
            mine = lax.dynamic_index_in_dim(array, (z + turn) % 2, 0, keepdims=False)
            blocks.append(send(mine, places.gather_order(turn)))
        return blocks

    far_steps = send(timesteps, places.swap(0))
    xs = gathered(tokens)
    cots = gathered(cotangent)
    here = z // 2 == core
    step_value = lax.dynamic_index_in_dim(jnp.where(here, timesteps, far_steps), z % 2, 0, keepdims=False)
    sequence = (d - core + z // 2) * seq_count + z % 2
    time_row = lax.dynamic_slice_in_dim(time_table, step_value, 1, 0)

    def row(v):
        return v.reshape(1, -1)

    bias_all = jnp.concatenate(
        [q_bias.astype(F32), jnp.zeros((width,), F32), v_bias.astype(F32)]
    ).reshape(1, -1)
    count = 2 * local_len
    normed, query, kv0 = project(xs[0], time_row, row(ln1_gain), row(ln1_bias), qkv_weight, bias_all, count)
    far0 = send(kv0, places.swap(0))
    normed, query, kv1 = project(
        xs[1], time_row, row(ln1_gain), row(ln1_bias), qkv_weight, bias_all, count, (normed, query)
    )
    far1 = send(kv1, places.swap(0))
    kvs = [kv0, kv1, far0, far1]
    context, logsum = attend(query, kvs)
    out, active, hidden_grad, normed_two, middle_grad, branch, context_grad, feed_sums = feed(
        context, xs, time_row, cots, out_weight, row(out_bias), row(ln2_gain), row(ln2_bias),
        up_weight, row(up_bias), down_weight, row(down_bias),
    )

    def scattered(blocks, dtype):
        back = [send(block, places.scatter_order(turn)) for turn, block in enumerate(blocks)]
        even = z % 2 == 0
        return jnp.stack(
            [jnp.where(even, back[0], back[1]), jnp.where(even, back[1], back[0])]
        ).astype(dtype)

    layer_out = scattered([out[:local_len], out[local_len:]], BF16)
    parts = hidden_width // width
    down_sum = reduce_parts(down_grad(active, cots)[None], places)[0]
    up_out_sum = reduce_parts(up_out_grad(normed_two, hidden_grad, context, branch), places)
    back = attend_back(query, context_grad, context, logsum, kvs)
    query_grad, key_grads, value_grads = back[0], back[1:5], back[5:9]
    far_key = [send(g, places.swap(0)) for g in key_grads[2:]]
    far_value = [send(g, places.swap(0)) for g in value_grads[2:]]
    token0, token1, projected_grad, start_sums = start_back(
        query_grad, list(key_grads[:2]) + far_key, list(value_grads[:2]) + far_value, xs, time_row,
        middle_grad, row(ln1_gain), qkv_weight,
    )
    tokens_grad = scattered([token0, token1], F32)
    qkv_sum = reduce_parts(qkv_grad(normed, projected_grad), places)

    bucket = step_value * BUCKETS // TSTEPS
    lane = jnp.arange(width)
    energy = jnp.sum(feed_sums[4]) / (width * total_tokens)
    stats_row = jnp.where(lane == bucket, energy, 0.0) + jnp.where(
        lane == BUCKETS + bucket, count / total_tokens, 0.0
    )
    sequence_rows = jnp.where(jnp.arange(total_seqs)[:, None] == sequence, start_sums[4][None], 0.0)
    step_row = jnp.where(lane[:total_seqs] == sequence, step_value, 0).astype(F32) * jnp.where(core == 0, 1.0, 0.0)
    packed = jnp.concatenate(
        [
            feed_sums[0:4], feed_sums[8 : 8 + parts], start_sums[0:4], stats_row[None],
            jnp.pad(step_row, (0, width - total_seqs))[None], sequence_rows,
        ]
    )
    packed = sum_everywhere(packed, places)
    piece = width // places.dp
    mine = lax.dynamic_slice_in_dim(packed[: 8 + parts], d * piece, piece, 1)
    up_piece = hidden_width // places.dp
    up_bias_sum = lax.dynamic_slice_in_dim(packed[4 : 4 + parts].reshape(-1), d * up_piece, up_piece, 0)
    stats = packed[8 + parts]
    steps = packed[9 + parts, :total_seqs].astype(jnp.int32)
    sums = packed[10 + parts :]
    table_rows = time_table.shape[0] // places.dp
    chosen = (steps[None, :] == (jnp.arange(table_rows) + d * table_rows)[:, None]).astype(F32)
    table_grad = jnp.dot(chosen, sums, precision=lax.Precision.HIGHEST)

    def side_by_side(stacked):
        return jnp.moveaxis(stacked, 0, 1).reshape(stacked.shape[1], -1)

    return (
        layer_out,
        tokens_grad,
        table_grad,
        mine[4 + parts],
        mine[5 + parts],
        side_by_side(qkv_sum),
        mine[6 + parts],
        mine[7 + parts],
        up_out_sum[parts],
        mine[3],
        mine[1],
        mine[2],
        side_by_side(up_out_sum[:parts]),
        up_bias_sum,
        down_sum,
        mine[0],
        stats[:BUCKETS],
        stats[BUCKETS : 2 * BUCKETS],
    )


def solution(mesh):
    split = P("dp", "seq", None)
    return jax.shard_map(
        per_device,
        mesh=mesh,
        in_specs=(split, P("dp")) + (P(),) * 14 + (split,),
        out_specs=(
            split, split, P("dp", None), P("dp"), P("dp"), P("dp", None), P("dp"), P("dp"), P("dp", None),
            P("dp"), P("dp"), P("dp"), P("dp", None), P("dp"), P("dp", None), P("dp"), P(), P(),
        ),
        check_vma=False,
    )
```

time: 1190 us -> 520 us (0.44); the launches traced: 1170 us -> 515 us
  matrix products: 354 us -> 1.4 us
  Pallas kernels: 0 us -> 186 us
  blocking collectives: 186 us -> 0 us
  local copies, waits for them, and re-layouts: 171 us -> 47.9 us
  other arithmetic: 155 us -> 40.6 us
  waiting for transfers between devices: 274 us -> 170 us
  starting transfers between devices: 15.8 us -> 63.9 us
    dot_general x69 -> x1, matrix products: 354 us -> 1.4 us  [per_device(): table_grad = jnp.dot(chosen, sums, precision=lax.Precision.HIGHEST)]
    pallas_call x0 -> x9, Pallas kernels: none -> 186 us  [the longest x1 68.1 us: attend_back(): pl.pallas_call(functools.partial(attend_back_kernel, pieces=pieces), grid...]
    ppermute x0 -> x53, waiting for transfers between devices: none -> 170 us  [send(): return lax.ppermute(x, BOTH, order)]
    all_to_all x3 -> x0, waiting for transfers between devices: 163 us -> none  [the longest x1 105 us: per_device(): lax.all_to_all(projected, 'seq', split_axis=2, concat_axis=4, tiled=True)]
    reduce_scatter x5 -> x0, waiting for transfers between devices: 110 us -> none  [the longest x1 67 us: per_device(): lax.psum_scatter(qkv_weight_grad, 'dp', scatter_dimension=0, tiled=True)]
    all_to_all x1 -> x0, blocking collectives: 105 us -> none  [per_device(): lax.all_to_all(qkv_grad, 'seq', split_axis=3, concat_axis=2, tiled=True)]
    convert_element_type x38 -> x30, other arithmetic: 105 us -> 21.5 us  [the longest x27 19.7 us: add(): return (a.astype(F32) + b.astype(F32)).astype(BF16)]
    ppermute x0 -> x53, starting transfers between devices: none -> 63.9 us  [send(): return lax.ppermute(x, BOTH, order)]
  transfers between devices with their start and end apart: 9 -> 53, of which waited for: 5 -> 22; matrix products, arithmetic and copies ran while one was open for 34% -> 16% of each run, Pallas kernels for 0% -> 15%
where the time goes in v1:
time: 520 us; the launch traced here: 515 us
  Pallas kernels  186 us (36%)
  waiting for transfers between devices  170 us (33%)
  starting transfers between devices  63.9 us (12%)
  local copies, waits for them, and re-layouts  47.9 us (9%)
  other arithmetic  40.6 us (8%)
    ppermute x53, waiting for transfers between devices, send(): return lax.ppermute(x, BOTH, order)  170 us
    pallas_call x1, Pallas kernels, attend_back(): pl.pallas_call(functools.partial(attend_back_kernel, pieces=pieces), grid...  68.1 us
    ppermute x53, starting transfers between devices, send(): return lax.ppermute(x, BOTH, order)  63.9 us
    pallas_call x1, Pallas kernels, feed(): pl.pallas_call(feed_kernel, grid=(2,), in_specs=[rows(block, width), whol...  34.8 us
    pallas_call x1, Pallas kernels, attend(): pl.pallas_call(functools.partial(attend_kernel, pieces=pieces), grid=(pai...  30.2 us
    convert_element_type x27, other arithmetic, add(): return (a.astype(F32) + b.astype(F32)).astype(BF16)  19.7 us
    pallas_call x1, Pallas kernels, start_back(): pl.pallas_call(start_kernel, grid=(2,), in_specs=[rows(block, width)] + [...  13.4 us
    pallas_call x1, Pallas kernels, up_out_grad(): pl.pallas_call(up_out_grad_kernel, grid=(parts + 1,), in_specs=[whole, pl...  11.7 us
  transfers between devices with their start and end apart: 53, of which 22 were waited for; matrix products, arithmetic and copies ran while one was open for 16% of the time, Pallas kernels for 15%

profile of v1, /device:TPU:0, one launch (start us, length us, event | category | flops | bytes accessed | tf_op | source)
XLA Modules:
  0.0 515.0 jit_solution(16245081410415483239)
XLA Ops:
  0.8 2.8 dynamic-slice_bitcast_fusion.3
  3.5 7.4 %collective-permute-start.2 = (bf16[512,768]{1,0:T(8,128)(2,1)}, bf16[512,768]{1,0:T(8,128)(2,1)}, u32[]{:S(2)}, u32[]{:S(2)}) collective-permute-start(bf16[512,768]{1,0:T(8,128)(2,1)} %get-tuple-element.94), channel_id=1, source_target_pairs={{0,0},{1,1},{2,4},{3,5},{4,2},{5,3},{6,6},{7,7},{8,8},{9,9},{10,12... | collective-permute-start | bytes 2359304 | tf_op jit(solution)/shard_map/ppermute | solution.py:528
  11.0 3.0 collective-permute-start
  19.0 5.7 %project.2 = (bf16[1024,768]{1,0:T(8,128)(2,1)}, bf16[1024,768]{1,0:T(8,128)(2,1)}, bf16[512,1536]{1,0:T(8,128)(2,1)}) custom-call(bf16[512,768]{1,0:T(8,128)(2,1)} %collective-permute-done.2.x_ref.x0_ref, bf16[1,768]{1,0:T(2,128)(2,1)} %constant_dynamic-slice_fusion.11.time_ref, bf16[1,768]{1,0:T(2,128)(2,1)} %reshape.314.gain_ref, ...), custom_call_target="tpu_custom_call" | custom-call | flops 5750000128 | tf_op jit(solution)/shard_map/project/pallas_call | solution.py:91
  24.6 15.4 %collective-permute-done.x_ref.x1_ref = bf16[512,768]{1,0:T(8,128)(2,1)} collective-permute-done((bf16[512,768]{1,0:T(8,128)(2,1)}, bf16[512,768]{1,0:T(8,128)(2,1)}, u32[]{:S(2)}, u32[]{:S(2)}) %collective-permute-start) | collective-permute-done | bytes 786464 | tf_op jit(solution)/shard_map/ppermute | solution.py:528
  40.0 5.8 %project.3 = (bf16[1024,768]{1,0:T(8,128)(2,1)}, bf16[1024,768]{1,0:T(8,128)(2,1)}, bf16[512,1536]{1,0:T(8,128)(2,1)}) custom-call(bf16[512,768]{1,0:T(8,128)(2,1)} %collective-permute-done.x_ref.x1_ref, bf16[1,768]{1,0:T(2,128)(2,1)} %constant_dynamic-slice_fusion.11.time_ref, ...), custom_call_target="tpu_custom_call", output_to_operand_aliasing={{0}: (6, {}), {1}: (7, {})} | custom-call | flops 5750000128 | tf_op jit(solution)/shard_map/project/pallas_call | solution.py:91
  47.5 5.2 %collective-permute-start.6 = (bf16[512,768]{1,0:T(8,128)(2,1)S(1)}, bf16[512,768]{1,0:T(8,128)(2,1)}, u32[]{:S(2)}, u32[]{:S(2)}) collective-permute-start(bf16[512,768]{1,0:T(8,128)(2,1)S(1)} %get-tuple-element.92), channel_id=1, source_target_pairs={{0,1},{1,0},{2,5},{3,4},{4,3},{5,2},{6,7},{7,6},{8,9},{9,8},{10,13... | collective-permute-start | bytes 2359304 | tf_op jit(solution)/shard_map/ppermute | solution.py:528
  58.7 30.2 %attend.1 = (bf16[1024,768]{1,0:T(8,128)(2,1)}, f32[1024,768]{1,0:T(8,128)}) custom-call(bf16[1024,768]{1,0:T(8,128)(2,1)} %get-tuple-element.49.query_ref, bf16[512,1536]{1,0:T(8,128)(2,1)} %get-tuple-element.50.refs_0_.refs_4_, bf16[512,1536]{1,0:T(8,128)(2,1)} %get-tuple-element.51.refs_1_.refs_5_, ...), custom_call_target="tpu_custom_call" | custom-call | flops 36800000000 | tf_op jit(solution)/shard_map/attend/pallas_call | solution.py:199
  89.7 34.8 %feed.1 = (bf16[1024,768]{1,0:T(8,128)(2,1)}, bf16[1024,3072]{1,0:T(8,128)(2,1)}, bf16[1024,3072]{1,0:T(8,128)(2,1)}, bf16[1024,768]{1,0:T(8,128)(2,1)}, f32[102...) custom-call(bf16[1024,768]{1,0:T(8,128)(2,1)} %get-tuple-element.52.context_ref, ...), custom_call_target="tpu_custom_call" | custom-call | flops 39099998208 | tf_op jit(solution)/shard_map/feed/pallas_call | solution.py:334
  124.6 68.1 %attend_back.1 = (bf16[1024,768]{1,0:T(8,128)(2,1)}, bf16[512,768]{1,0:T(8,128)(2,1)}, bf16[512,768]{1,0:T(8,128)(2,1)}, bf16[512,768]{1,0:T(8,128)(2,1)}, bf16[...) custom-call(bf16[1024,768]{1,0:T(8,128)(2,1)} %get-tuple-element.49., ...), custom_call_target="tpu_custom_call" | custom-call | flops 86249996288 | tf_op jit(solution)/shard_map/attend_back/pallas_call | solution.py:262
  192.7 3.8 collective-permute-start.10
  197.1 9.1 %down_grad.1 = bf16[3072,768]{1,0:T(8,128)(2,1)} custom-call(bf16[1024,3072]{1,0:T(8,128)(2,1)} %get-tuple-element.75.active_ref, bf16[512,768]{1,0:T(8,128)(2,1)} %copy-done.23, bf16[512,768]{1,0:T(8,128)(2,1)} %collective-permute-done.6.cot1_ref), custom_call_target="tpu_custom_call" | custom-call | flops 9200000000 | tf_op jit(solution)/shard_map/down_grad/pallas_call | solution.py:367
  206.3 3.2 dynamic-slice_bitcast_fusion
  212.7 13.4 %start_back.1 = (bf16[512,768]{1,0:T(8,128)(2,1)}, bf16[512,768]{1,0:T(8,128)(2,1)}, bf16[1024,2304]{1,0:T(8,128)(2,1)}, f32[8,768]{1,0:T(8,128)}) custom-call(bf16[1024,768]{1,0:T(8,128)(2,1)} %get-tuple-element.56.query_grad_ref, bf16[512,768]{1,0:T(8,128)(2,1)} %get-tuple-element.57.key0_ref, bf16[512,768]{1,0:T(8,128)(2,1)} %get-tuple-element.58.key1_ref, ...), custom_call_target="tpu_custom_call" | custom-call | flops 11500000256 | tf_op jit(solution)/shard_map/start_back/pallas_call | solution.py:480
  228.0 11.7 %up_out_grad.1 = bf16[5,768,768]{2,1,0:T(8,128)(2,1)} custom-call(bf16[1024,768]{1,0:T(8,128)(2,1)} %get-tuple-element.72.normed_ref, bf16[1024,3072]{1,0:T(8,128)(2,1)} %get-tuple-element.73.hidden_grad_ref, bf16[1024,768]{1,0:T(8,128)(2,1)} %get-tuple-element.52.context_ref, bf16[1024,768]{1,0:T(8,128)(2,1)} %get-tuple-element.74.branch_ref), custom_call_target="tpu_custom_call" | custom-call | flops 11500000256 | tf_op jit(solution)/shard_map/up_out_grad/pallas_call | solution.py:395
  242.3 2.7 collective-permute-done.16
  246.6 3.3 constant_dynamic-slice_fusion.4
  249.8 1.9 copy.103
  255.4 7.6 %qkv_grad.1 = bf16[3,768,768]{2,1,0:T(8,128)(2,1)} custom-call(bf16[1024,768]{1,0:T(8,128)(2,1)} %get-tuple-element.70.normed_ref, bf16[1024,2304]{1,0:T(8,128)(2,1)} %get-tuple-element.71.grad_ref), custom_call_target="tpu_custom_call" | custom-call | flops 8049999872 | tf_op jit(solution)/shard_map/qkv_grad/pallas_call | solution.py:419
  263.0 21.4 %collective-permute-done.18 = f32[30,768]{1,0:T(8,128)S(1)} collective-permute-done((f32[30,768]{1,0:T(8,128)S(1)}, f32[30,768]{1,0:T(8,128)S(1)}, u32[]{:S(2)}, u32[]{:S(2)}) %collective-permute-start.18) | collective-permute-done | bytes 92192 | tf_op jit(solution)/shard_map/ppermute | solution.py:528
  284.7 3.4 constant_dynamic-slice_fusion.9
  289.5 7.8 %collective-permute-start.13 = (bf16[512,768]{1,0:T(8,128)(2,1)}, bf16[512,768]{1,0:T(8,128)(2,1)}, u32[]{:S(2)}, u32[]{:S(2)}) collective-permute-start(bf16[512,768]{1,0:T(8,128)(2,1)} %get-tuple-element.66), channel_id=1, source_target_pairs={{0,0},{1,1},{4,2},{5,3},{2,4},{3,5},{6,6},{7,7},{8,8},{9,9},{12,10... | collective-permute-start | bytes 2359304 | tf_op jit(solution)/shard_map/ppermute | solution.py:528
  301.4 23.9 %collective-permute-done.14 = bf16[512,768]{1,0:T(8,128)(2,1)} collective-permute-done((bf16[512,768]{1,0:T(8,128)(2,1)}, bf16[512,768]{1,0:T(8,128)(2,1)}, u32[]{:S(2)}, u32[]{:S(2)}) %collective-permute-start.14) | collective-permute-done | bytes 786464 | tf_op jit(solution)/shard_map/ppermute | solution.py:528
  325.3 2.2 select_bitcast_fusion.1
  328.8 1.9 maximum_convert_fusion
  330.7 2.2 fusion.1
  335.3 2.0 fusion.2
  339.7 9.8 %collective-permute-done.43 = bf16[1,2,192,768]{3,2,1,0:T(8,128)(2,1)S(1)} collective-permute-done((bf16[1,2,192,768]{3,2,1,0:T(8,128)(2,1)S(1)}, bf16[1,2,192,768]{3,2,1,0:T(8,128)(2,1)S(1)}, u32[]{:S(2)}, u32[]{:S(2)}) %collective-permute-start.43) | collective-permute-done | bytes 589856 | tf_op jit(solution)/shard_map/ppermute | solution.py:528
  362.1 20.4 %collective-permute-done.22 = bf16[3,48,768]{2,1,0:T(8,128)(2,1)S(1)} collective-permute-done((bf16[3,48,768]{2,1,0:T(8,128)(2,1)S(1)}, bf16[3,48,768]{2,1,0:T(8,128)(2,1)S(1)}, u32[]{:S(2)}, u32[]{:S(2)}) %collective-permute-start.22) | collective-permute-done | bytes 221216 | tf_op jit(solution)/shard_map/ppermute | solution.py:528
  385.9 2.8 collective-permute-done.27
  395.4 1.9 fusion.13
  399.6 1.8 fusion.12
  407.3 1.8 collective-permute-start.24
  412.7 5.5 %collective-permute-done.50 = bf16[1,192,384]{2,0,1:T(2,128)(2,1)S(1)} collective-permute-done((bf16[1,192,384]{2,0,1:T(2,128)(2,1)S(1)}, bf16[1,192,384]{2,0,1:T(2,128)(2,1)S(1)}, u32[]{:S(2)}, u32[]{:S(2)}) %collective-permute-start.50) | collective-permute-done | bytes 147488 | tf_op jit(solution)/shard_map/ppermute | solution.py:528
  418.7 3.0 collective-permute-start.51
  421.9 18.2 %collective-permute-done.46 = bf16[1,192,384]{2,0,1:T(2,128)(2,1)S(1)} collective-permute-done((bf16[1,192,384]{2,0,1:T(2,128)(2,1)S(1)}, bf16[1,192,384]{2,0,1:T(2,128)(2,1)S(1)}, u32[]{:S(2)}, u32[]{:S(2)}) %collective-permute-start.46) | collective-permute-done | bytes 147488 | tf_op jit(solution)/shard_map/ppermute | solution.py:528
  440.6 5.9 %collective-permute-done.51 = bf16[1,192,384]{2,0,1:T(2,128)(2,1)S(1)} collective-permute-done((bf16[1,192,384]{2,0,1:T(2,128)(2,1)S(1)}, bf16[1,192,384]{2,0,1:T(2,128)(2,1)S(1)}, u32[]{:S(2)}, u32[]{:S(2)}) %collective-permute-start.51) | collective-permute-done | bytes 147488 | tf_op jit(solution)/shard_map/ppermute | solution.py:528
  446.9 2.1 collective-permute-start.52
  450.1 6.2 %collective-permute-done.47 = bf16[1,192,384]{2,0,1:T(2,128)(2,1)S(1)} collective-permute-done((bf16[1,192,384]{2,0,1:T(2,128)(2,1)S(1)}, bf16[1,192,384]{2,0,1:T(2,128)(2,1)S(1)}, u32[]{:S(2)}, u32[]{:S(2)}) %collective-permute-start.47) | collective-permute-done | bytes 147488 | tf_op jit(solution)/shard_map/ppermute | solution.py:528
  457.0 4.7 collective-permute-done.52
  462.5 8.9 %maximum_convert_fusion.1 = f32[1,384,768]{2,0,1:T(1,128)S(1)} fusion(bf16[1,192,384]{2,0,1:T(2,128)(2,1)S(1)} %get-tuple-element.99, bf16[1,192,384]{2,0,1:T(2,128)(2,1)S(1)} %get-tuple-element.98, bf16[1,192,384]{2,0,1:T(2,128)(2,1)S(1)} %get-tuple-element.97, bf16[1,192,384]{2,0,1:T(2,128)(2,1)S(1)} %get-tuple-element.96), kind=kLoop, calls=%fused_computation.17 | loop fusion | flops 2359296 | bytes 1769472 | tf_op jit(solution)/shard_map/squeeze | solution.py:641
  476.3 7.2 %collective-permute-done.33 = bf16[5,48,768]{2,1,0:T(8,128)(2,1)S(1)} collective-permute-done((bf16[5,48,768]{2,1,0:T(8,128)(2,1)S(1)}, bf16[5,48,768]{2,1,0:T(8,128)(2,1)S(1)}, u32[]{:S(2)}, u32[]{:S(2)}) %collective-permute-start.33) | collective-permute-done | bytes 368672 | tf_op jit(solution)/shard_map/ppermute | solution.py:528
  487.6 5.1 collective-permute-done.34
  493.5 2.8 collective-permute-done.39
  497.4 7.3 %collective-permute-done.35 = bf16[5,48,384]{2,1,0:T(8,128)(2,1)S(1)} collective-permute-done((bf16[5,48,384]{2,1,0:T(8,128)(2,1)S(1)}, bf16[5,48,384]{2,1,0:T(8,128)(2,1)S(1)}, u32[]{:S(2)}, u32[]{:S(2)}) %collective-permute-start.35) | collective-permute-done | bytes 184352 | tf_op jit(solution)/shard_map/ppermute | solution.py:528
  504.8 1.9 collective-permute-done.40
  507.0 3.7 collective-permute-done.36
  510.7 1.9 collective-permute-done.41
  (249 shorter events, 87.2 us)
Async XLA Ops:
  3.5 15.4 %collective-permute-start.2 = (bf16[512,768]{1,0:T(8,128)(2,1)}, bf16[512,768]{1,0:T(8,128)(2,1)}, u32[]{:S(2)}, u32[]{:S(2)}) collective-permute-start(bf16[512,768]{1,0:T(8,128)(2,1)} %get-tuple-element.94), channel_id=1, source_target_pairs={{0,0},{1,1},{2,4},{3,5},{4,2},{5,3},{6,6},{7,7},{8,8},{9,9},{10,12... | collective-permute-start | bytes 2359304 | tf_op jit(solution)/shard_map/ppermute | solution.py:528
  11.0 29.0 %collective-permute-start = (bf16[512,768]{1,0:T(8,128)(2,1)}, bf16[512,768]{1,0:T(8,128)(2,1)}, u32[]{:S(2)}, u32[]{:S(2)}) collective-permute-start(bf16[512,768]{1,0:T(8,128)(2,1)} %get-tuple-element.95), channel_id=1, source_target_pairs={{0,1},{1,0},{2,5},{3,4},{4,3},{5,2},{6,7},{7,6},{8,9},{9,8},{10,13... | collective-permute-start | bytes 2359304 | tf_op jit(solution)/shard_map/ppermute | solution.py:528
  45.8 12.9 %collective-permute-start.4 = (bf16[512,1536]{1,0:T(8,128)(2,1)}, bf16[512,1536]{1,0:T(8,128)(2,1)}, u32[]{:S(2)}, u32[]{:S(2)}) collective-permute-start(bf16[512,1536]{1,0:T(8,128)(2,1)} %get-tuple-element.51.refs_1_.refs_5_), channel_id=1, source_target_pairs={{0,4},{1,5},{2,6},{3,7},{4,0},{5,1},{6,2},{7,3},{8,12},{9,13},{10,... | collective-permute-start | bytes 4718600 | tf_op jit(solution)/shard_map/ppermute | solution.py:528
  45.8 12.8 %collective-permute-start.3 = (bf16[512,1536]{1,0:T(8,128)(2,1)}, bf16[512,1536]{1,0:T(8,128)(2,1)}, u32[]{:S(2)}, u32[]{:S(2)}) collective-permute-start(bf16[512,1536]{1,0:T(8,128)(2,1)} %get-tuple-element.50.refs_0_.refs_4_), channel_id=1, source_target_pairs={{0,4},{1,5},{2,6},{3,7},{4,0},{5,1},{6,2},{7,3},{8,12},{9,13},{10,... | collective-permute-start | bytes 4718600 | tf_op jit(solution)/shard_map/ppermute | solution.py:528
  46.5 42.4 %collective-permute-start.5 = (bf16[512,768]{1,0:T(8,128)(2,1)S(1)}, bf16[512,768]{1,0:T(8,128)(2,1)S(1)}, u32[]{:S(2)}, u32[]{:S(2)}) collective-permute-start(bf16[512,768]{1,0:T(8,128)(2,1)S(1)} %get-tuple-element.93), channel_id=1, source_target_pairs={{0,0},{1,1},{2,4},{3,5},{4,2},{5,3},{6,6},{7,7},{8,8},{9,9},{10,12... | collective-permute-start | bytes 2359304 | tf_op jit(solution)/shard_map/ppermute | solution.py:528
  47.5 41.4 %collective-permute-start.6 = (bf16[512,768]{1,0:T(8,128)(2,1)S(1)}, bf16[512,768]{1,0:T(8,128)(2,1)}, u32[]{:S(2)}, u32[]{:S(2)}) collective-permute-start(bf16[512,768]{1,0:T(8,128)(2,1)S(1)} %get-tuple-element.92), channel_id=1, source_target_pairs={{0,1},{1,0},{2,5},{3,4},{4,3},{5,2},{6,7},{7,6},{8,9},{9,8},{10,13... | collective-permute-start | bytes 2359304 | tf_op jit(solution)/shard_map/ppermute | solution.py:528
  192.7 18.5 %collective-permute-start.10 = (bf16[512,768]{1,0:T(8,128)(2,1)}, bf16[512,768]{1,0:T(8,128)(2,1)S(1)}, u32[]{:S(2)}, u32[]{:S(2)}) collective-permute-start(bf16[512,768]{1,0:T(8,128)(2,1)} %get-tuple-element.60), channel_id=1, source_target_pairs={{0,4},{1,5},{2,6},{3,7},{4,0},{5,1},{6,2},{7,3},{8,12},{9,13},{10,... | collective-permute-start | bytes 2359304 | tf_op jit(solution)/shard_map/ppermute | solution.py:528
  196.6 14.7 %collective-permute-start.11 = (bf16[512,768]{1,0:T(8,128)(2,1)}, bf16[512,768]{1,0:T(8,128)(2,1)S(1)}, u32[]{:S(2)}, u32[]{:S(2)}) collective-permute-start(bf16[512,768]{1,0:T(8,128)(2,1)} %get-tuple-element.63), channel_id=1, source_target_pairs={{0,4},{1,5},{2,6},{3,7},{4,0},{5,1},{6,2},{7,3},{8,12},{9,13},{10,... | collective-permute-start | bytes 2359304 | tf_op jit(solution)/shard_map/ppermute | solution.py:528
  196.6 14.6 %collective-permute-start.12 = (bf16[512,768]{1,0:T(8,128)(2,1)}, bf16[512,768]{1,0:T(8,128)(2,1)S(1)}, u32[]{:S(2)}, u32[]{:S(2)}) collective-permute-start(bf16[512,768]{1,0:T(8,128)(2,1)} %get-tuple-element.64), channel_id=1, source_target_pairs={{0,4},{1,5},{2,6},{3,7},{4,0},{5,1},{6,2},{7,3},{8,12},{9,13},{10,... | collective-permute-start | bytes 2359304 | tf_op jit(solution)/shard_map/ppermute | solution.py:528
  197.1 14.2 %collective-permute-start.9 = (bf16[512,768]{1,0:T(8,128)(2,1)}, bf16[512,768]{1,0:T(8,128)(2,1)}, u32[]{:S(2)}, u32[]{:S(2)}) collective-permute-start(bf16[512,768]{1,0:T(8,128)(2,1)} %get-tuple-element.59), channel_id=1, source_target_pairs={{0,4},{1,5},{2,6},{3,7},{4,0},{5,1},{6,2},{7,3},{8,12},{9,13},{10,... | collective-permute-start | bytes 2359304 | tf_op jit(solution)/shard_map/ppermute | solution.py:528
  209.5 121.2 %collective-permute-start.42 = (bf16[1,2,2,384,768]{4,3,2,1,0:T(8,128)(2,1)}, bf16[1,2,2,384,768]{4,3,2,1,0:T(8,128)(2,1)}, u32[]{:S(2)}, u32[]{:S(2)}) collective-permute-start(bf16[1,2,2,384,768]{4,3,2,1,0:T(8,128)(2,1)} %dynamic-slice_bitcast_fusion), channel_id=1, source_target_pairs={{0,4},{1,5},{2,6},{3,7},{4,0},{5,1},{6,2},{7,3},{8,12},{9,13},{10,... | collective-permute-start | bytes 7077896 | tf_op jit(solution)/shard_map/ppermute | solution.py:528
  227.9 11.9 %collective-permute-start.15 = (f32[30,768]{1,0:T(8,128)S(1)}, f32[30,768]{1,0:T(8,128)S(1)}, u32[]{:S(2)}, u32[]{:S(2)}) collective-permute-start(f32[30,768]{1,0:T(8,128)S(1)} %concatenate.55), channel_id=1, source_target_pairs={{0,4},{1,5},{2,6},{3,7},{4,0},{5,1},{6,2},{7,3},{8,12},{9,13},{10,... | collective-permute-start | bytes 276488 | tf_op jit(solution)/shard_map/ppermute | solution.py:528
  245.0 8.7 %collective-permute-start.17 = (f32[30,768]{1,0:T(8,128)S(1)}, f32[30,768]{1,0:T(8,128)S(1)}, u32[]{:S(2)}, u32[]{:S(2)}) collective-permute-start(f32[30,768]{1,0:T(8,128)S(1)} %add.262), channel_id=1, source_target_pairs={{0,16},{1,17},{2,18},{3,19},{4,20},{5,21},{6,22},{7,23},{8,24},{9,... | collective-permute-start | bytes 276488 | tf_op jit(solution)/shard_map/ppermute | solution.py:528
  251.7 47.2 %collective-permute-start.7 = (bf16[512,768]{1,0:T(8,128)(2,1)S(1)}, bf16[512,768]{1,0:T(8,128)(2,1)}, u32[]{:S(2)}, u32[]{:S(2)}) collective-permute-start(bf16[512,768]{1,0:T(8,128)(2,1)S(1)} %get-tuple-element.90), channel_id=1, source_target_pairs={{0,0},{1,1},{4,2},{5,3},{2,4},{3,5},{6,6},{7,7},{8,8},{9,9},{12,10... | collective-permute-start | bytes 2359304 | tf_op jit(solution)/shard_map/ppermute | solution.py:528
  253.2 47.5 %collective-permute-start.8 = (bf16[512,768]{1,0:T(8,128)(2,1)}, bf16[512,768]{1,0:T(8,128)(2,1)}, u32[]{:S(2)}, u32[]{:S(2)}) collective-permute-start(bf16[512,768]{1,0:T(8,128)(2,1)} %get-tuple-element.91), channel_id=1, source_target_pairs={{1,0},{0,1},{5,2},{4,3},{3,4},{2,5},{7,6},{6,7},{9,8},{8,9},{13,10... | collective-permute-start | bytes 2359304 | tf_op jit(solution)/shard_map/ppermute | solution.py:528
  253.7 30.7 %collective-permute-start.18 = (f32[30,768]{1,0:T(8,128)S(1)}, f32[30,768]{1,0:T(8,128)S(1)}, u32[]{:S(2)}, u32[]{:S(2)}) collective-permute-start(f32[30,768]{1,0:T(8,128)S(1)} %add.263), channel_id=1, source_target_pairs={{0,1},{1,0},{2,3},{3,2},{4,5},{5,4},{6,7},{7,6},{8,9},{9,8},{10,11... | collective-permute-start | bytes 276488 | tf_op jit(solution)/shard_map/ppermute | solution.py:528
  284.4 12.9 %collective-permute-start.19 = (f32[30,768]{1,0:T(8,128)S(1)}, f32[30,768]{1,0:T(8,128)S(1)}, u32[]{:S(2)}, u32[]{:S(2)}) collective-permute-start(f32[30,768]{1,0:T(8,128)S(1)} %add.264), channel_id=1, source_target_pairs={{0,2},{1,3},{2,0},{3,1},{4,6},{5,7},{6,4},{7,5},{8,10},{9,11},{10,... | collective-permute-start | bytes 276488 | tf_op jit(solution)/shard_map/ppermute | solution.py:528
  289.5 11.8 %collective-permute-start.13 = (bf16[512,768]{1,0:T(8,128)(2,1)}, bf16[512,768]{1,0:T(8,128)(2,1)}, u32[]{:S(2)}, u32[]{:S(2)}) collective-permute-start(bf16[512,768]{1,0:T(8,128)(2,1)} %get-tuple-element.66), channel_id=1, source_target_pairs={{0,0},{1,1},{4,2},{5,3},{2,4},{3,5},{6,6},{7,7},{8,8},{9,9},{12,10... | collective-permute-start | bytes 2359304 | tf_op jit(solution)/shard_map/ppermute | solution.py:528
  297.4 27.9 %collective-permute-start.14 = (bf16[512,768]{1,0:T(8,128)(2,1)}, bf16[512,768]{1,0:T(8,128)(2,1)}, u32[]{:S(2)}, u32[]{:S(2)}) collective-permute-start(bf16[512,768]{1,0:T(8,128)(2,1)} %get-tuple-element.67), channel_id=1, source_target_pairs={{1,0},{0,1},{5,2},{4,3},{3,4},{2,5},{7,6},{6,7},{9,8},{8,9},{13,10... | collective-permute-start | bytes 2359304 | tf_op jit(solution)/shard_map/ppermute | solution.py:528
  298.9 36.4 %collective-permute-start.20 = (bf16[3,2,2,96,768]{4,3,0,2,1:T(8,128)(2,1)}, bf16[3,2,2,96,768]{4,3,0,2,1:T(8,128)(2,1)}, u32[]{:S(2)}, u32[]{:S(2)}) collective-permute-start(bf16[3,2,2,96,768]{4,3,0,2,1:T(8,128)(2,1)} %bitcast.178), channel_id=1, source_target_pairs={{0,4},{1,5},{2,6},{3,7},{4,0},{5,1},{6,2},{7,3},{8,12},{9,13},{10,... | collective-permute-start | bytes 5308424 | tf_op jit(solution)/shard_map/ppermute | solution.py:528
  300.8 52.7 %collective-permute-start.31 = (bf16[5,2,2,96,768]{4,3,0,2,1:T(8,128)(2,1)}, bf16[5,2,2,96,768]{4,3,0,2,1:T(8,128)(2,1)S(1)}, u32[]{:S(2)}, u32[]{:S(2)}) collective-permute-start(bf16[5,2,2,96,768]{4,3,0,2,1:T(8,128)(2,1)} %bitcast.190), channel_id=1, source_target_pairs={{0,4},{1,5},{2,6},{3,7},{4,0},{5,1},{6,2},{7,3},{8,12},{9,13},{10,... | collective-permute-start | bytes 8847368 | tf_op jit(solution)/shard_map/ppermute | solution.py:528
  333.2 16.3 %collective-permute-start.43 = (bf16[1,2,192,768]{3,2,1,0:T(8,128)(2,1)S(1)}, bf16[1,2,192,768]{3,2,1,0:T(8,128)(2,1)S(1)}, u32[]{:S(2)}, u32[]{:S(2)}) collective-permute-start(bf16[1,2,192,768]{3,2,1,0:T(8,128)(2,1)S(1)} %dynamic-slice_bitcast_fusion.8), channel_id=1, source_target_pairs={{0,8},{1,9},{2,10},{3,11},{4,12},{5,13},{6,14},{7,15},{8,0},{9,1},... | collective-permute-start | bytes 1769480 | tf_op jit(solution)/shard_map/ppermute | solution.py:528
  334.7 16.3 %collective-permute-start.48 = (bf16[1,2,192,768]{3,2,1,0:T(8,128)(2,1)S(1)}, bf16[1,2,192,768]{3,2,1,0:T(8,128)(2,1)S(1)}, u32[]{:S(2)}, u32[]{:S(2)}) collective-permute-start(bf16[1,2,192,768]{3,2,1,0:T(8,128)(2,1)S(1)} %dynamic-slice_bitcast_fusion.7), channel_id=1, source_target_pairs={{0,16},{1,17},{2,18},{3,19},{4,20},{5,21},{6,22},{7,23},{8,24},{9,... | collective-permute-start | bytes 1769480 | tf_op jit(solution)/shard_map/ppermute | solution.py:528
  337.5 21.5 %collective-permute-start.21 = (bf16[3,2,48,768]{3,2,0,1:T(8,128)(2,1)S(1)}, bf16[3,2,48,768]{3,2,0,1:T(8,128)(2,1)S(1)}, u32[]{:S(2)}, u32[]{:S(2)}) collective-permute-start(bf16[3,2,48,768]{3,2,0,1:T(8,128)(2,1)S(1)} %dynamic-slice_bitcast_fusion.10), channel_id=1, source_target_pairs={{0,8},{1,9},{2,10},{3,11},{4,12},{5,13},{6,14},{7,15},{8,0},{9,1},... | collective-permute-start | bytes 1327112 | tf_op jit(solution)/shard_map/ppermute | solution.py:528
  338.3 22.2 %collective-permute-start.26 = (bf16[3,2,48,768]{3,2,0,1:T(8,128)(2,1)S(1)}, bf16[3,2,48,768]{3,2,0,1:T(8,128)(2,1)S(1)}, u32[]{:S(2)}, u32[]{:S(2)}) collective-permute-start(bf16[3,2,48,768]{3,2,0,1:T(8,128)(2,1)S(1)} %dynamic-slice_bitcast_fusion.9), channel_id=1, source_target_pairs={{0,16},{1,17},{2,18},{3,19},{4,20},{5,21},{6,22},{7,23},{8,24},{9,... | collective-permute-start | bytes 1327112 | tf_op jit(solution)/shard_map/ppermute | solution.py:528
  350.5 43.2 %collective-permute-start.44 = (bf16[1,192,768]{2,1,0:T(8,128)(2,1)}, bf16[1,192,768]{2,1,0:T(8,128)(2,1)}, u32[]{:S(2)}, u32[]{:S(2)}) collective-permute-start(bf16[1,192,768]{2,1,0:T(8,128)(2,1)} %dynamic-slice_bitcast_fusion.16), channel_id=1, source_target_pairs={{0,16},{1,17},{2,18},{3,19},{4,20},{5,21},{6,22},{7,23},{8,24},{9,... | collective-permute-start | bytes 884744 | tf_op jit(solution)/shard_map/ppermute | solution.py:528
  352.1 47.2 %collective-permute-start.49 = (bf16[1,192,768]{2,1,0:T(8,128)(2,1)}, bf16[1,192,768]{2,1,0:T(8,128)(2,1)}, u32[]{:S(2)}, u32[]{:S(2)}) collective-permute-start(bf16[1,192,768]{2,1,0:T(8,128)(2,1)} %dynamic-slice_bitcast_fusion.14), channel_id=1, source_target_pairs={{0,8},{1,9},{2,10},{3,11},{4,12},{5,13},{6,14},{7,15},{8,0},{9,1},... | collective-permute-start | bytes 884744 | tf_op jit(solution)/shard_map/ppermute | solution.py:528
  355.7 116.8 %collective-permute-start.32 = (bf16[5,2,48,768]{3,2,0,1:T(8,128)(2,1)}, bf16[5,2,48,768]{3,2,0,1:T(8,128)(2,1)}, u32[]{:S(2)}, u32[]{:S(2)}) collective-permute-start(bf16[5,2,48,768]{3,2,0,1:T(8,128)(2,1)} %dynamic-slice_bitcast_fusion.6), channel_id=1, source_target_pairs={{0,8},{1,9},{2,10},{3,11},{4,12},{5,13},{6,14},{7,15},{8,0},{9,1},... | collective-permute-start | bytes 2211848 | tf_op jit(solution)/shard_map/ppermute | solution.py:528
  359.0 115.4 %collective-permute-start.37 = (bf16[5,2,48,768]{3,2,0,1:T(8,128)(2,1)}, bf16[5,2,48,768]{3,2,0,1:T(8,128)(2,1)}, u32[]{:S(2)}, u32[]{:S(2)}) collective-permute-start(bf16[5,2,48,768]{3,2,0,1:T(8,128)(2,1)} %dynamic-slice_bitcast_fusion.5), channel_id=1, source_target_pairs={{0,16},{1,17},{2,18},{3,19},{4,20},{5,21},{6,22},{7,23},{8,24},{9,... | collective-permute-start | bytes 2211848 | tf_op jit(solution)/shard_map/ppermute | solution.py:528
  360.6 21.9 %collective-permute-start.22 = (bf16[3,48,768]{2,1,0:T(8,128)(2,1)S(1)}, bf16[3,48,768]{2,1,0:T(8,128)(2,1)S(1)}, u32[]{:S(2)}, u32[]{:S(2)}) collective-permute-start(bf16[3,48,768]{2,1,0:T(8,128)(2,1)S(1)} %dynamic-slice_bitcast_fusion.18), channel_id=1, source_target_pairs={{0,16},{1,17},{2,18},{3,19},{4,20},{5,21},{6,22},{7,23},{8,24},{9,... | collective-permute-start | bytes 663560 | tf_op jit(solution)/shard_map/ppermute | solution.py:528
  388.7 15.8 %collective-permute-start.23 = (bf16[3,48,384]{2,1,0:T(8,128)(2,1)S(1)}, bf16[3,48,384]{2,1,0:T(8,128)(2,1)S(1)}, u32[]{:S(2)}, u32[]{:S(2)}) collective-permute-start(bf16[3,48,384]{2,1,0:T(8,128)(2,1)S(1)} %bitcast.196), channel_id=1, source_target_pairs={{0,1},{1,0},{2,3},{3,2},{4,5},{5,4},{6,7},{7,6},{8,9},{9,8},{10,11... | collective-permute-start | bytes 331784 | tf_op jit(solution)/shard_map/ppermute | solution.py:528
  393.7 13.6 %collective-permute-start.28 = (bf16[3,48,384]{2,1,0:T(8,128)(2,1)}, bf16[3,48,384]{2,1,0:T(8,128)(2,1)}, u32[]{:S(2)}, u32[]{:S(2)}) collective-permute-start(bf16[3,48,384]{2,1,0:T(8,128)(2,1)} %bitcast.182), channel_id=1, source_target_pairs={{0,1},{1,0},{2,3},{3,2},{4,5},{5,4},{6,7},{7,6},{8,9},{9,8},{10,11... | collective-permute-start | bytes 331784 | tf_op jit(solution)/shard_map/ppermute | solution.py:528
  399.3 10.8 %collective-permute-start.45 = (bf16[1,192,384]{2,0,1:T(2,128)(2,1)}, bf16[1,192,384]{2,0,1:T(2,128)(2,1)}, u32[]{:S(2)}, u32[]{:S(2)}) collective-permute-start(bf16[1,192,384]{2,0,1:T(2,128)(2,1)} %dynamic-slice_bitcast_fusion.15), channel_id=1, source_target_pairs={{0,1},{1,0},{2,3},{3,2},{4,5},{5,4},{6,7},{7,6},{8,9},{9,8},{10,11... | collective-permute-start | bytes 442376 | tf_op jit(solution)/shard_map/ppermute | solution.py:528
  404.5 13.7 %collective-permute-start.50 = (bf16[1,192,384]{2,0,1:T(2,128)(2,1)S(1)}, bf16[1,192,384]{2,0,1:T(2,128)(2,1)S(1)}, u32[]{:S(2)}, u32[]{:S(2)}) collective-permute-start(bf16[1,192,384]{2,0,1:T(2,128)(2,1)S(1)} %dynamic-slice_bitcast_fusion.13), channel_id=1, source_target_pairs={{0,1},{1,0},{2,3},{3,2},{4,5},{5,4},{6,7},{7,6},{8,9},{9,8},{10,11... | collective-permute-start | bytes 442376 | tf_op jit(solution)/shard_map/ppermute | solution.py:528
  407.3 11.4 %collective-permute-start.24 = (bf16[3,48,384]{2,1,0:T(8,128)(2,1)S(1)}, bf16[3,48,384]{2,1,0:T(8,128)(2,1)S(1)}, u32[]{:S(2)}, u32[]{:S(2)}) collective-permute-start(bf16[3,48,384]{2,1,0:T(8,128)(2,1)S(1)} %fusion.21), channel_id=1, source_target_pairs={{0,2},{1,3},{2,0},{3,1},{4,6},{5,7},{6,4},{7,5},{8,10},{9,11},{10,... | collective-permute-start | bytes 331784 | tf_op jit(solution)/shard_map/ppermute | solution.py:528
  410.1 11.6 %collective-permute-start.29 = (bf16[3,48,384]{2,1,0:T(8,128)(2,1)S(1)}, bf16[3,48,384]{2,1,0:T(8,128)(2,1)S(1)}, u32[]{:S(2)}, u32[]{:S(2)}) collective-permute-start(bf16[3,48,384]{2,1,0:T(8,128)(2,1)S(1)} %fusion.22), channel_id=1, source_target_pairs={{0,2},{1,3},{2,0},{3,1},{4,6},{5,7},{6,4},{7,5},{8,10},{9,11},{10,... | collective-permute-start | bytes 331784 | tf_op jit(solution)/shard_map/ppermute | solution.py:528
  418.3 21.8 %collective-permute-start.46 = (bf16[1,192,384]{2,0,1:T(2,128)(2,1)S(1)}, bf16[1,192,384]{2,0,1:T(2,128)(2,1)S(1)}, u32[]{:S(2)}, u32[]{:S(2)}) collective-permute-start(bf16[1,192,384]{2,0,1:T(2,128)(2,1)S(1)} %fusion.20), channel_id=1, source_target_pairs={{0,2},{1,3},{2,0},{3,1},{4,6},{5,7},{6,4},{7,5},{8,10},{9,11},{10,... | collective-permute-start | bytes 442376 | tf_op jit(solution)/shard_map/ppermute | solution.py:528
  418.7 27.7 %collective-permute-start.51 = (bf16[1,192,384]{2,0,1:T(2,128)(2,1)S(1)}, bf16[1,192,384]{2,0,1:T(2,128)(2,1)S(1)}, u32[]{:S(2)}, u32[]{:S(2)}) collective-permute-start(bf16[1,192,384]{2,0,1:T(2,128)(2,1)S(1)} %fusion.19), channel_id=1, source_target_pairs={{0,2},{1,3},{2,0},{3,1},{4,6},{5,7},{6,4},{7,5},{8,10},{9,11},{10,... | collective-permute-start | bytes 442376 | tf_op jit(solution)/shard_map/ppermute | solution.py:528
  421.8 25.2 %collective-permute-start.25 = (bf16[3,48,384]{2,1,0:T(8,128)(2,1)S(1)}, bf16[3,48,384]{2,1,0:T(8,128)(2,1)S(1)}, u32[]{:S(2)}, u32[]{:S(2)}) collective-permute-start(bf16[3,48,384]{2,1,0:T(8,128)(2,1)S(1)} %add_convert_fusion.5), channel_id=1, source_target_pairs={{0,1},{1,0},{2,3},{3,2},{4,5},{5,4},{6,7},{7,6},{8,9},{9,8},{10,11... | collective-permute-start | bytes 331784 | tf_op jit(solution)/shard_map/ppermute | solution.py:528
  440.1 9.0 %collective-permute-start.30 = (bf16[3,48,384]{2,1,0:T(8,128)(2,1)S(1)}, bf16[3,48,384]{2,1,0:T(8,128)(2,1)S(1)}, u32[]{:S(2)}, u32[]{:S(2)}) collective-permute-start(bf16[3,48,384]{2,1,0:T(8,128)(2,1)S(1)} %add_convert_fusion.4), channel_id=1, source_target_pairs={{0,1},{1,0},{2,3},{3,2},{4,5},{5,4},{6,7},{7,6},{8,9},{9,8},{10,11... | collective-permute-start | bytes 331784 | tf_op jit(solution)/shard_map/ppermute | solution.py:528
  446.5 9.9 %collective-permute-start.47 = (bf16[1,192,384]{2,0,1:T(2,128)(2,1)S(1)}, bf16[1,192,384]{2,0,1:T(2,128)(2,1)S(1)}, u32[]{:S(2)}, u32[]{:S(2)}) collective-permute-start(bf16[1,192,384]{2,0,1:T(2,128)(2,1)S(1)} %add_convert_fusion.3), channel_id=1, source_target_pairs={{0,1},{1,0},{2,3},{3,2},{4,5},{5,4},{6,7},{7,6},{8,9},{9,8},{10,11... | collective-permute-start | bytes 442376 | tf_op jit(solution)/shard_map/ppermute | solution.py:528
  446.9 14.8 %collective-permute-start.52 = (bf16[1,192,384]{2,0,1:T(2,128)(2,1)S(1)}, bf16[1,192,384]{2,0,1:T(2,128)(2,1)S(1)}, u32[]{:S(2)}, u32[]{:S(2)}) collective-permute-start(bf16[1,192,384]{2,0,1:T(2,128)(2,1)S(1)} %add_convert_fusion.2), channel_id=1, source_target_pairs={{0,1},{1,0},{2,3},{3,2},{4,5},{5,4},{6,7},{7,6},{8,9},{9,8},{10,11... | collective-permute-start | bytes 442376 | tf_op jit(solution)/shard_map/ppermute | solution.py:528
  473.8 9.7 %collective-permute-start.33 = (bf16[5,48,768]{2,1,0:T(8,128)(2,1)S(1)}, bf16[5,48,768]{2,1,0:T(8,128)(2,1)S(1)}, u32[]{:S(2)}, u32[]{:S(2)}) collective-permute-start(bf16[5,48,768]{2,1,0:T(8,128)(2,1)S(1)} %dynamic-slice_bitcast_fusion.12), channel_id=1, source_target_pairs={{0,16},{1,17},{2,18},{3,19},{4,20},{5,21},{6,22},{7,23},{8,24},{9,... | collective-permute-start | bytes 1105928 | tf_op jit(solution)/shard_map/ppermute | solution.py:528
  475.7 9.4 %collective-permute-start.38 = (bf16[5,48,768]{2,1,0:T(8,128)(2,1)S(1)}, bf16[5,48,768]{2,1,0:T(8,128)(2,1)S(1)}, u32[]{:S(2)}, u32[]{:S(2)}) collective-permute-start(bf16[5,48,768]{2,1,0:T(8,128)(2,1)S(1)} %dynamic-slice_bitcast_fusion.11), channel_id=1, source_target_pairs={{0,8},{1,9},{2,10},{3,11},{4,12},{5,13},{6,14},{7,15},{8,0},{9,1},... | collective-permute-start | bytes 1105928 | tf_op jit(solution)/shard_map/ppermute | solution.py:528
  484.4 8.3 %collective-permute-start.34 = (bf16[5,48,384]{2,1,0:T(8,128)(2,1)S(1)}, bf16[5,48,384]{2,1,0:T(8,128)(2,1)S(1)}, u32[]{:S(2)}, u32[]{:S(2)}) collective-permute-start(bf16[5,48,384]{2,1,0:T(8,128)(2,1)S(1)} %bitcast.194), channel_id=1, source_target_pairs={{0,1},{1,0},{2,3},{3,2},{4,5},{5,4},{6,7},{7,6},{8,9},{9,8},{10,11... | collective-permute-start | bytes 552968 | tf_op jit(solution)/shard_map/ppermute | solution.py:528
  486.1 10.1 %collective-permute-start.39 = (bf16[5,48,384]{2,1,0:T(8,128)(2,1)S(1)}, bf16[5,48,384]{2,1,0:T(8,128)(2,1)S(1)}, u32[]{:S(2)}, u32[]{:S(2)}) collective-permute-start(bf16[5,48,384]{2,1,0:T(8,128)(2,1)S(1)} %bitcast.195), channel_id=1, source_target_pairs={{0,1},{1,0},{2,3},{3,2},{4,5},{5,4},{6,7},{7,6},{8,9},{9,8},{10,11... | collective-permute-start | bytes 552968 | tf_op jit(solution)/shard_map/ppermute | solution.py:528
  492.7 12.0 %collective-permute-start.35 = (bf16[5,48,384]{2,1,0:T(8,128)(2,1)S(1)}, bf16[5,48,384]{2,1,0:T(8,128)(2,1)S(1)}, u32[]{:S(2)}, u32[]{:S(2)}) collective-permute-start(bf16[5,48,384]{2,1,0:T(8,128)(2,1)S(1)} %fusion.16), channel_id=1, source_target_pairs={{0,2},{1,3},{2,0},{3,1},{4,6},{5,7},{6,4},{7,5},{8,10},{9,11},{10,... | collective-permute-start | bytes 552968 | tf_op jit(solution)/shard_map/ppermute | solution.py:528
  496.3 10.5 %collective-permute-start.40 = (bf16[5,48,384]{2,1,0:T(8,128)(2,1)S(1)}, bf16[5,48,384]{2,1,0:T(8,128)(2,1)S(1)}, u32[]{:S(2)}, u32[]{:S(2)}) collective-permute-start(bf16[5,48,384]{2,1,0:T(8,128)(2,1)S(1)} %fusion.17), channel_id=1, source_target_pairs={{0,2},{1,3},{2,0},{3,1},{4,6},{5,7},{6,4},{7,5},{8,10},{9,11},{10,... | collective-permute-start | bytes 552968 | tf_op jit(solution)/shard_map/ppermute | solution.py:528
  (34 other events, 274.3 us)

commit v2 on v1

--- a/solution.py
+++ b/solution.py
@@ -210,13 +210,10 @@
     )(query, *kvs, *kvs)
 
 
-def attend_back_kernel(query_ref, grad_ref, context_ref, logsum_ref, *refs, pieces):
-    key_refs, value_refs = refs[:pieces], refs[pieces : 2 * pieces]
-    query_grad_ref = refs[2 * pieces]
-    key_grad_refs = refs[2 * pieces + 1 : 3 * pieces + 1]
-    value_grad_refs = refs[3 * pieces + 1 :]
+def attend_back_step(query_ref, grad_ref, context_ref, logsum_ref, pieces, query_grad_ref):
     low, place = lane_parts()
     query, grad = query_ref[...], grad_ref[...]
+    count = query.shape[0]
     product = grad.astype(F32) * wide(context_ref)
     logsum = logsum_ref[...]
     ones_key = jnp.where(place < 3, 1.0, 0.0).astype(BF16)
@@ -234,10 +231,16 @@
                 jnp.where(own, grad, zero),
             )
         )
+    length = sum(piece[0].shape[0] for piece in pieces)
     query_grads = [0.0, 0.0]
-    for piece in range(pieces):
-        key, value = key_refs[piece][...], value_refs[piece][...]
+    key_mean = 0.0
+    for key_ref, value_ref, key_grad_ref, value_grad_ref, before in pieces:
+        if before is not None:
+            before()
+        key, value = key_ref[...], value_ref[...]
         key_turned = key.T
+        key_mean = key_mean + jnp.sum(key_turned.astype(F32), 1, keepdims=True) / length
+        ones = jnp.ones((16, key.shape[0]), BF16)
         key_grad, value_grad = 0.0, 0.0
         for head, (own, query_off, grad_off, query_own, grad_own) in enumerate(heads):
             scores = dot(jnp.where(own, key, ones_key), query_off, NT)
@@ -247,11 +250,26 @@
             value_grad = value_grad + dot(probs.astype(BF16), grad_own, NN)
             key_grad = key_grad + dot(score_grad, query_own, NN)
             lanes = slice(head * HEAD_DIM, (head + 1) * HEAD_DIM)
-            query_grads[head] = query_grads[head] + dot(key_turned[lanes], score_grad, NN)
-        key_grad_refs[piece][...] = key_grad.astype(BF16)
-        value_grad_refs[piece][...] = value_grad.astype(BF16)
-    turned = jnp.concatenate(query_grads, 0) * HEAD_DIM ** (-0.5)
-    query_grad_ref[...] = turned.T.astype(BF16)
+            turned = jnp.concatenate([key_turned[lanes], ones], 0)
+            query_grads[head] = query_grads[head] + dot(turned, score_grad, NN)
+        key_grad_ref[...] = key_grad.astype(BF16)
+        value_grad_ref[...] = value_grad.astype(BF16)
+    parts = [
+        made[:HEAD_DIM]
+        - key_mean[head * HEAD_DIM : (head + 1) * HEAD_DIM]
+        * jnp.broadcast_to(made[HEAD_DIM : HEAD_DIM + 1], (HEAD_DIM, count))
+        for head, made in enumerate(query_grads)
+    ]
+    query_grad_ref[...] = (jnp.concatenate(parts, 0) * HEAD_DIM ** (-0.5)).T.astype(BF16)
+
+
+def attend_back_kernel(query_ref, grad_ref, context_ref, logsum_ref, *refs, pieces):
+    key_refs, value_refs = refs[:pieces], refs[pieces : 2 * pieces]
+    query_grad_ref = refs[2 * pieces]
+    key_grad_refs = refs[2 * pieces + 1 : 3 * pieces + 1]
+    value_grad_refs = refs[3 * pieces + 1 :]
+    steps = list(zip(key_refs, value_refs, key_grad_refs, value_grad_refs, [None] * pieces))
+    attend_back_step(query_ref, grad_ref, context_ref, logsum_ref, steps, query_grad_ref)
 
 
 def attend_back(query, grad, context, logsum, kvs):
@@ -271,6 +289,364 @@
         cost_estimate=cost(75),
         name="attend_back",
     )(query, grad, context, logsum, *kvs, *kvs)
+
+
+def here():
+    d, z = lax.axis_index("dp"), lax.axis_index("seq")
+    return d, z, d // 4, (d // 2) % 2, d % 2
+
+
+def partners():
+    d, z, y, x, core = here()
+    return {
+        "core": (d + 1 - 2 * core, z),
+        "x": (d + 2 - 4 * x, z),
+        "y": (d + 4 - 8 * y, z),
+        "near": (d, z + 1 - 2 * (z % 2)),
+        "far": (d, (z + 2) % 4),
+    }
+
+
+def remote(source, target, sends, receives, send_index, receive_index, device):
+    return pltpu.make_async_remote_copy(
+        src_ref=source,
+        dst_ref=target,
+        send_sem=sends.at[send_index],
+        recv_sem=receives.at[receive_index],
+        device_id=device,
+        device_id_type=pl.DeviceIdType.MESH,
+    )
+
+
+class Reduction:
+    COPIES = 8
+
+    def __init__(self, source, out, scratch, at):
+        self.source, self.out = source, out
+        self.own, self.from_core, self.first, self.second, self.near, self.far, self.other = scratch[:7]
+        self.sends, self.receives, self.local = scratch[7:10]
+        self.at = at
+        self.parts, _, _, self.rows, self.width = self.own.shape
+        self.half, self.top = self.width // 2, self.rows // 2
+
+    @staticmethod
+    def scratch(parts, block, width):
+        half, top = width // 2, block // 2
+        return [
+            pltpu.VMEM((parts, 2, 2, block, width), BF16),
+            pltpu.VMEM((parts, 2, 2, block, width), BF16),
+            pltpu.VMEM((2, parts, 2, block, half), BF16),
+            pltpu.VMEM((2, parts, block, half), BF16),
+            pltpu.VMEM((parts, top, width), BF16),
+            pltpu.VMEM((parts, top, width), BF16),
+            pltpu.VMEM((parts, top, width), BF16),
+            pltpu.SemaphoreType.DMA((8,)),
+            pltpu.SemaphoreType.DMA((8,)),
+            pltpu.SemaphoreType.DMA((3,)),
+        ]
+
+    def copy(self, number):
+        d, z, y, x, core = here()
+        to = partners()
+        left, right = pl.ds(0, self.half), pl.ds(self.half, self.half)
+        kept = pl.ds(pl.multiple_of((z % 2) * self.top, self.top), self.top)
+        given = pl.ds(pl.multiple_of((1 - z % 2) * self.top, self.top), self.top)
+        source, target, device = (
+            lambda: (self.source.at[:, :, :, 1 - core], self.from_core, to["core"]),
+            lambda: (self.own.at[:, :, 1 - x, :, left], self.first.at[0], to["x"]),
+            lambda: (self.own.at[:, 1 - y, :, :, right], self.first.at[1], to["y"]),
+            lambda: (self.own.at[:, 1 - y, x, :, left], self.second.at[0], to["y"]),
+            lambda: (self.own.at[:, y, 1 - x, :, right], self.second.at[1], to["x"]),
+            lambda: (self.own.at[:, y, x, given], self.near, to["near"]),
+            lambda: (self.own.at[:, y, x, kept], self.far, to["far"]),
+            lambda: (self.own.at[:, y, x, kept], self.other, to["near"]),
+        )[number]()
+        return remote(source, target, self.sends, self.receives, number, number, device)
+
+    def load(self):
+        core = here()[4]
+        return pltpu.make_async_copy(self.source.at[:, :, :, core], self.own, self.local.at[0])
+
+    def to_cores(self):
+        self.copy(0).start()
+        self.load().start()
+
+    def to_first(self):
+        self.load().wait()
+        self.copy(0).wait()
+        for part in range(self.parts):
+            for i in range(2):
+                for j in range(2):
+                    self.own[part, i, j] = self.own[part, i, j] + self.from_core[part, i, j]
+        self.copy(1).start()
+        self.copy(2).start()
+
+    def to_second(self):
+        _, _, y, x, _ = here()
+        self.copy(1).wait()
+        self.copy(2).wait()
+        left, right = slice(0, self.half), slice(self.half, self.width)
+        for part in range(self.parts):
+            for i in range(2):
+                self.own[part, i, x, :, left] = self.own[part, i, x, :, left] + self.first[0, part, i]
+                self.own[part, y, i, :, right] = self.own[part, y, i, :, right] + self.first[1, part, i]
+        self.copy(3).start()
+        self.copy(4).start()
+
+    def to_near(self):
+        _, _, y, x, _ = here()
+        self.copy(3).wait()
+        self.copy(4).wait()
+        left, right = slice(0, self.half), slice(self.half, self.width)
+        for part in range(self.parts):
+            self.own[part, y, x, :, left] = self.own[part, y, x, :, left] + self.second[0, part]
+            self.own[part, y, x, :, right] = self.own[part, y, x, :, right] + self.second[1, part]
+        self.copy(5).start()
+
+    def add_rows(self, received):
+        _, z, y, x, _ = here()
+        kept = pl.ds(pl.multiple_of((z % 2) * self.top, self.top), self.top)
+        for part in range(self.parts):
+            self.own[part, y, x, kept] = self.own[part, y, x, kept] + received[part]
+
+    def to_far(self):
+        self.copy(5).wait()
+        self.add_rows(self.near)
+        self.copy(6).start()
+
+    def to_other(self):
+        self.copy(6).wait()
+        self.add_rows(self.far)
+        self.copy(7).start()
+
+    def stores(self):
+        _, z, y, x, _ = here()
+        kept = pl.ds(pl.multiple_of((z % 2) * self.top, self.top), self.top)
+        given = pl.ds(pl.multiple_of((1 - z % 2) * self.top, self.top), self.top)
+        return (
+            pltpu.make_async_copy(self.own.at[:, y, x, kept], self.out.at[:, kept], self.local.at[1]),
+            pltpu.make_async_copy(self.other, self.out.at[:, given], self.local.at[2]),
+        )
+
+    def to_out(self):
+        self.copy(7).wait()
+        for copy in self.stores():
+            copy.start()
+
+    def finish(self):
+        for copy in self.stores():
+            copy.wait()
+
+
+class Return:
+    def __init__(self, out, sends, receives, local):
+        self.out, self.sends, self.receives, self.local = out, sends, receives, local
+
+    def targets(self):
+        d, z, _, _, core = here()
+        return [(d - core + z // 2, 2 * core + (z + p) % 2) for p in range(2)]
+
+    def sources(self):
+        d, z, _, _, core = here()
+        return [(d - core + z // 2, 2 * core + j) for j in range(2)]
+
+    def stays(self):
+        _, z, _, _, core = here()
+        return z // 2 == core
+
+    def greet(self, barrier):
+        _, z, _, _, _ = here()
+        for j, source in enumerate(self.sources()):
+
+            @pl.when(jnp.logical_not(self.stays() & (z % 2 == j)))
+            def _():
+                pl.semaphore_signal(barrier, inc=1, device_id=source, device_id_type=pl.DeviceIdType.MESH)
+
+        return jnp.where(self.stays(), 1, 2)
+
+    def keep(self, block):
+        z = lax.axis_index("seq")
+        return pltpu.make_async_copy(block, self.out.at[z % 2], self.local.at[0])
+
+    def copy(self, p, block):
+        z = lax.axis_index("seq")
+        return remote(block, self.out.at[z % 2], self.sends, self.receives, p, z % 2, self.targets()[p])
+
+    def begin(self, p, block):
+        if p == 1:
+            self.copy(1, block).start()
+            return
+
+        @pl.when(self.stays())
+        def _():
+            self.keep(block).start()
+
+        @pl.when(jnp.logical_not(self.stays()))
+        def _():
+            self.copy(0, block).start()
+
+    def finish(self, blocks):
+        z = lax.axis_index("seq")
+        self.copy(1, blocks[1]).wait_send()
+
+        @pl.when(self.stays())
+        def _():
+            self.keep(blocks[0]).wait()
+
+        @pl.when(jnp.logical_not(self.stays()))
+        def _():
+            self.copy(0, blocks[0]).wait_send()
+
+        for j in range(2):
+
+            @pl.when(jnp.logical_not(self.stays() & (z % 2 == j)))
+            def _():
+                remote(
+                    blocks[0], self.out.at[j], self.sends, self.receives, 0, j, self.sources()[j]
+                ).wait_recv()
+
+
+def meet(names, *returns):
+    barrier = pltpu.get_barrier_semaphore()
+    to = partners()
+    for name in names:
+        pl.semaphore_signal(barrier, inc=1, device_id=to[name], device_id_type=pl.DeviceIdType.MESH)
+    expected = len(names)
+    for one in returns:
+        expected = expected + one.greet(barrier)
+    pl.semaphore_wait(barrier, expected)
+
+
+def back_kernel(
+    query_ref, grad_ref, context_ref, logsum_ref, *refs, pieces
+):
+    key_refs, value_refs = refs[:pieces], refs[pieces : 2 * pieces]
+    down_ref, up_ref, layer_ref = refs[2 * pieces : 2 * pieces + 3]
+    refs = refs[2 * pieces + 3 :]
+    near = pieces // 2
+    query_grad_ref = refs[0]
+    key_grad_refs, value_grad_refs = refs[1 : 1 + near], refs[1 + near : 1 + 2 * near]
+    far_out, layer_out, down_out, up_out = refs[1 + 2 * near : 5 + 2 * near]
+    refs = refs[5 + 2 * near :]
+    down = Reduction(down_ref, down_out, refs[:10], 0)
+    up = Reduction(up_ref, up_out, refs[10:20], 0)
+    far_grads, far_sends, far_receives, layer_sends, layer_receives, layer_local = refs[20:]
+    back = Return(layer_out, layer_sends, layer_receives, layer_local)
+    block = key_refs[0].shape[0]
+    layer_blocks = [layer_ref.at[pl.ds(p * block, block)] for p in range(2)]
+    pair, pairs = pl.program_id(0), pl.num_programs(0)
+
+    def far_copy(which):
+        return remote(
+            far_grads, far_out.at[which], far_sends, far_receives, 0, which, partners()["core"]
+        )
+
+    def begin():
+        meet(("core", "x", "y", "near", "far"), back)
+        down.to_cores()
+        up.to_cores()
+        back.begin(0, layer_blocks[0])
+        back.begin(1, layer_blocks[1])
+
+    def far_free():
+        far_copy(pair - 1).wait_send()
+
+    def far_send():
+        far_copy(pair).start()
+
+    plan = {
+        (0, 0): [begin],
+        (0, 2): [down.to_first],
+        (1, 0): [up.to_first],
+        (1, 3): [down.to_second],
+        (3, 0): [down.to_near],
+        (3, 1): [up.to_second],
+        (3, 3): [down.to_far],
+        (4, 1): [up.to_near],
+        (5, 0): [up.to_far, down.to_other],
+        (5, 3): [down.to_out],
+    }
+
+    def before(place):
+        def run():
+            for (step, at), actions in plan.items():
+                if at == place:
+
+                    @pl.when(pair == step)
+                    def _():
+                        for action in actions:
+                            action()
+
+            if place == 0:
+                pl.when(pair > 0)(far_free)
+            if place == near:
+                far_send()
+
+        return run
+
+    order = []
+    for i in range(near):
+        order.append((key_refs[near + i], value_refs[near + i], far_grads.at[0, pl.ds(i * block, block)], far_grads.at[1, pl.ds(i * block, block)]))
+    for i in range(near):
+        order.append((key_refs[i], value_refs[i], key_grad_refs[i], value_grad_refs[i]))
+    steps = [one + (before(place),) for place, one in enumerate(order)]
+    attend_back_step(query_ref, grad_ref, context_ref, logsum_ref, steps, query_grad_ref)
+
+    @pl.when(pair == pairs - 1)
+    def _():
+        up.to_other()
+        far_copy(pair).wait_send()
+
+        def received(which, carry):
+            far_copy(which).wait_recv()
+            return carry
+
+        lax.fori_loop(0, pairs, received, 0)
+        back.finish(layer_blocks)
+        down.finish()
+        up.to_out()
+        up.finish()
+
+
+def back(query, grad, context, logsum, kvs, down_parts, up_parts, layer_out):
+    count, width = query.shape
+    pairs, pieces, length = width // LANES, len(kvs), kvs[0].shape[0]
+    near = pieces // 2
+    row = pl.BlockSpec((count, LANES), lambda p: (0, p))
+    piece = pl.BlockSpec((length, LANES), lambda p: (0, p))
+    anywhere = pl.BlockSpec(memory_space=pl.ANY)
+    sizes = [(parts.shape[0], parts.shape[1] // 8) for parts in (down_parts, up_parts)]
+    split = [
+        parts.reshape(n, 2, 2, 2, block, width) for parts, (n, block) in zip((down_parts, up_parts), sizes)
+    ]
+    return pl.pallas_call(
+        functools.partial(back_kernel, pieces=pieces),
+        grid=(pairs,),
+        in_specs=[row] * 4
+        + [piece] * pieces
+        + [pl.BlockSpec((length, LANES), lambda p: (0, pairs + p))] * pieces
+        + [anywhere] * 3,
+        out_specs=[row] + [piece] * (2 * near) + [anywhere] * 4,
+        out_shape=[shape_of((count, width))]
+        + [shape_of((length, width))] * (2 * near)
+        + [shape_of((pairs, 2, near * length, LANES)), shape_of((2, length, width))]
+        + [shape_of((n, block, width)) for n, block in sizes],
+        scratch_shapes=Reduction.scratch(*sizes[0], width)
+        + Reduction.scratch(*sizes[1], width)
+        + [
+            pltpu.VMEM((2, near * length, LANES), BF16),
+            pltpu.SemaphoreType.DMA((1,)),
+            pltpu.SemaphoreType.DMA((pairs,)),
+            pltpu.SemaphoreType.DMA((2,)),
+            pltpu.SemaphoreType.DMA((2,)),
+            pltpu.SemaphoreType.DMA((1,)),
+        ],
+        compiler_params=pltpu.CompilerParams(
+            vmem_limit_bytes=VMEM_BYTES, collective_id=0, has_side_effects=True
+        ),
+        cost_estimate=cost(80),
+        name="back",
+    )(query, grad, context, logsum, *kvs, *kvs, *split, layer_out)
 
 
 def gelu_parts(hidden):
@@ -636,16 +1012,26 @@
             [jnp.where(even, back[0], back[1]), jnp.where(even, back[1], back[0])]
         ).astype(dtype)
 
-    layer_out = scattered([out[:local_len], out[local_len:]], BF16)
     parts = hidden_width // width
-    down_sum = reduce_parts(down_grad(active, cots)[None], places)[0]
-    up_out_sum = reduce_parts(up_out_grad(normed_two, hidden_grad, context, branch), places)
-    back = attend_back(query, context_grad, context, logsum, kvs)
-    query_grad, key_grads, value_grads = back[0], back[1:5], back[5:9]
-    far_key = [send(g, places.swap(0)) for g in key_grads[2:]]
-    far_value = [send(g, places.swap(0)) for g in value_grads[2:]]
+    down_parts = down_grad(active, cots)[None]
+    up_out_parts = up_out_grad(normed_two, hidden_grad, context, branch)
+    if places.dp == 8:
+        made = back(query, context_grad, context, logsum, kvs, down_parts, up_out_parts, out)
+        query_grad, key_grads, value_grads = made[0], list(made[1:3]), list(made[3:5])
+        far_grads, layer_out = made[5], made[6]
+        down_sum, up_out_sum = made[7][0].astype(F32), made[8].astype(F32)
+        far = jnp.moveaxis(far_grads.reshape(-1, 2, 2, local_len, LANES), 0, 3).reshape(2, 2, local_len, width)
+        far_key, far_value = [far[0, 0], far[0, 1]], [far[1, 0], far[1, 1]]
+    else:
+        layer_out = scattered([out[:local_len], out[local_len:]], BF16)
+        down_sum = reduce_parts(down_parts, places)[0]
+        up_out_sum = reduce_parts(up_out_parts, places)
+        made = attend_back(query, context_grad, context, logsum, kvs)
+        query_grad, key_grads, value_grads = made[0], list(made[1:3]), list(made[5:7])
+        far_key = [send(g, places.swap(0)) for g in made[3:5]]
+        far_value = [send(g, places.swap(0)) for g in made[7:9]]
     token0, token1, projected_grad, start_sums = start_back(
-        query_grad, list(key_grads[:2]) + far_key, list(value_grads[:2]) + far_value, xs, time_row,
+        query_grad, key_grads + far_key, value_grads + far_value, xs, time_row,
         middle_grad, row(ln1_gain), qkv_weight,
     )
     tokens_grad = scattered([token0, token1], F32)

time: 520 us -> 398 us (0.77)
  waiting for transfers between devices: 170 us -> 65.6 us
  Pallas kernels: 186 us -> 230 us
  other arithmetic: 40.6 us -> 12.5 us
  starting transfers between devices: 63.9 us -> 43.9 us
  local copies, waits for them, and re-layouts: 47.9 us -> 35.1 us
    ppermute x53 -> x25, waiting for transfers between devices: 170 us -> 65.6 us  [send(): return lax.ppermute(x, BOTH, order)]
    pallas_call x1, Pallas kernels: 68.1 us -> 112 us  [back(): pl.pallas_call(functools.partial(back_kernel, pieces=pieces), grid=(pairs...]
    ppermute x53 -> x25, starting transfers between devices: 63.9 us -> 43.9 us  [send(): return lax.ppermute(x, BOTH, order)]
    convert_element_type x27 -> x9, other arithmetic: 19.7 us -> 3.4 us  [add(): return (a.astype(F32) + b.astype(F32)).astype(BF16)]
    squeeze x2 -> x0, other arithmetic: 9.63 us -> none  [the longest x1 8.89 us: per_device(): down_sum = reduce_parts(down_grad(active, cots)[None], places)[0]]
    squeeze x13 -> x4, local copies, waits for them, and re-layouts: 7.74 us -> 0.8 us  [halve(): sent = lax.dynamic_index_in_dim(value, 1 - mine, axis, keepdims=False)]
  transfers between devices with their start and end apart: 53 -> 25, of which waited for: 22 -> 13; matrix products, arithmetic and copies ran while one was open for 16% -> 6% of each run, Pallas kernels for 15% -> 9%
where the time goes in v2:
time: 398 us; the launch traced here: 393 us
  Pallas kernels  230 us (58%)
  waiting for transfers between devices  65.6 us (16%)
  starting transfers between devices  43.9 us (11%)
  local copies, waits for them, and re-layouts  35.1 us (9%)
  other arithmetic  12.5 us (3%)
  between operations  4.74 us (1%)
    pallas_call x1, Pallas kernels, back(): pl.pallas_call(functools.partial(back_kernel, pieces=pieces), grid=(pairs...  112 us
    ppermute x25, waiting for transfers between devices, send(): return lax.ppermute(x, BOTH, order)  65.6 us
    ppermute x25, starting transfers between devices, send(): return lax.ppermute(x, BOTH, order)  43.9 us
    pallas_call x1, Pallas kernels, feed(): pl.pallas_call(feed_kernel, grid=(2,), in_specs=[rows(block, width), whol...  34.7 us
    pallas_call x1, Pallas kernels, attend(): pl.pallas_call(functools.partial(attend_kernel, pieces=pieces), grid=(pai...  30.2 us
    pallas_call x1, Pallas kernels, start_back(): pl.pallas_call(start_kernel, grid=(2,), in_specs=[rows(block, width)] + [...  13.3 us
    pallas_call x1, Pallas kernels, up_out_grad(): pl.pallas_call(up_out_grad_kernel, grid=(parts + 1,), in_specs=[whole, pl...  11.8 us
    pallas_call x2, Pallas kernels, project(): pl.pallas_call(project_kernel, grid=(count // block,), in_specs=[rows(blo...  11.5 us
  transfers between devices with their start and end apart: 25, of which 13 were waited for; matrix products, arithmetic and copies ran while one was open for 6% of the time, Pallas kernels for 9%

profile of v2, /device:TPU:0, one launch (start us, length us, event | category | flops | bytes accessed | tf_op | source)
XLA Modules:
  0.0 393.5 jit_solution(6103087790641880320)
XLA Ops:
  0.8 2.8 dynamic-slice_bitcast_fusion.2
  3.5 7.4 %collective-permute-start.2 = (bf16[512,768]{1,0:T(8,128)(2,1)}, bf16[512,768]{1,0:T(8,128)(2,1)}, u32[]{:S(2)}, u32[]{:S(2)}) collective-permute-start(bf16[512,768]{1,0:T(8,128)(2,1)} %get-tuple-element.88), channel_id=1, source_target_pairs={{0,0},{1,1},{2,4},{3,5},{4,2},{5,3},{6,6},{7,7},{8,8},{9,9},{10,12... | collective-permute-start | bytes 2359304 | tf_op jit(solution)/shard_map/ppermute | solution.py:904
  11.0 3.0 collective-permute-start
  19.0 5.7 %project.2 = (bf16[1024,768]{1,0:T(8,128)(2,1)}, bf16[1024,768]{1,0:T(8,128)(2,1)}, bf16[512,1536]{1,0:T(8,128)(2,1)}) custom-call(bf16[512,768]{1,0:T(8,128)(2,1)} %collective-permute-done.2.x_ref.x0_ref, bf16[1,768]{1,0:T(2,128)(2,1)} %constant_dynamic-slice_fusion.6.time_ref, bf16[1,768]{1,0:T(2,128)(2,1)} %reshape.142.gain_ref, ...), custom_call_target="tpu_custom_call" | custom-call | flops 5750000128 | tf_op jit(solution)/shard_map/project/pallas_call | solution.py:91
  24.7 15.3 %collective-permute-done.x_ref.x1_ref = bf16[512,768]{1,0:T(8,128)(2,1)} collective-permute-done((bf16[512,768]{1,0:T(8,128)(2,1)}, bf16[512,768]{1,0:T(8,128)(2,1)}, u32[]{:S(2)}, u32[]{:S(2)}) %collective-permute-start) | collective-permute-done | bytes 786464 | tf_op jit(solution)/shard_map/ppermute | solution.py:904
  40.0 5.8 %project.3 = (bf16[1024,768]{1,0:T(8,128)(2,1)}, bf16[1024,768]{1,0:T(8,128)(2,1)}, bf16[512,1536]{1,0:T(8,128)(2,1)}) custom-call(bf16[512,768]{1,0:T(8,128)(2,1)} %collective-permute-done.x_ref.x1_ref, bf16[1,768]{1,0:T(2,128)(2,1)} %constant_dynamic-slice_fusion.6.time_ref, ...), custom_call_target="tpu_custom_call", output_to_operand_aliasing={{0}: (6, {}), {1}: (7, {})} | custom-call | flops 5750000128 | tf_op jit(solution)/shard_map/project/pallas_call | solution.py:91
  46.6 5.2 %collective-permute-start.6 = (bf16[512,768]{1,0:T(8,128)(2,1)S(1)}, bf16[512,768]{1,0:T(8,128)(2,1)S(1)}, u32[]{:S(2)}, u32[]{:S(2)}) collective-permute-start(bf16[512,768]{1,0:T(8,128)(2,1)S(1)} %get-tuple-element.86), channel_id=1, source_target_pairs={{0,1},{1,0},{2,5},{3,4},{4,3},{5,2},{6,7},{7,6},{8,9},{9,8},{10,13... | collective-permute-start | bytes 2359304 | tf_op jit(solution)/shard_map/ppermute | solution.py:904
  51.8 1.7 collective-permute-start.5
  59.0 30.2 %attend.1 = (bf16[1024,768]{1,0:T(8,128)(2,1)}, f32[1024,768]{1,0:T(8,128)}) custom-call(bf16[1024,768]{1,0:T(8,128)(2,1)} %get-tuple-element.49.query_ref, bf16[512,1536]{1,0:T(8,128)(2,1)} %get-tuple-element.50.refs_0_.refs_4_, bf16[512,1536]{1,0:T(8,128)(2,1)} %get-tuple-element.51.refs_1_.refs_5_, ...), custom_call_target="tpu_custom_call" | custom-call | flops 36800000000 | tf_op jit(solution)/shard_map/attend/pallas_call | solution.py:199
  90.0 34.7 %feed.1 = (bf16[1024,768]{1,0:T(8,128)(2,1)}, bf16[1024,3072]{1,0:T(8,128)(2,1)}, bf16[1024,3072]{1,0:T(8,128)(2,1)}, bf16[1024,768]{1,0:T(8,128)(2,1)}, f32[102...) custom-call(bf16[1024,768]{1,0:T(8,128)(2,1)} %get-tuple-element.52.context_ref, ...), custom_call_target="tpu_custom_call" | custom-call | flops 39099998208 | tf_op jit(solution)/shard_map/feed/pallas_call | solution.py:710
  124.8 1.4 slice_reduce_fusion.1
  126.9 11.8 %up_out_grad.1 = bf16[5,768,768]{2,1,0:T(8,128)(2,1)} custom-call(bf16[1024,768]{1,0:T(8,128)(2,1)} %get-tuple-element.56.normed_ref, bf16[1024,3072]{1,0:T(8,128)(2,1)} %get-tuple-element.57.hidden_grad_ref, bf16[1024,768]{1,0:T(8,128)(2,1)} %get-tuple-element.52.context_ref, bf16[1024,768]{1,0:T(8,128)(2,1)} %get-tuple-element.58.branch_ref), custom_call_target="tpu_custom_call" | custom-call | flops 11500000256 | tf_op jit(solution)/shard_map/up_out_grad/pallas_call | solution.py:771
  138.7 9.2 %down_grad.1 = bf16[3072,768]{1,0:T(8,128)(2,1)} custom-call(bf16[1024,3072]{1,0:T(8,128)(2,1)} %get-tuple-element.55.active_ref, bf16[512,768]{1,0:T(8,128)(2,1)} %collective-permute-done.5.cot0_ref, bf16[512,768]{1,0:T(8,128)(2,1)} %copy-done.22), custom_call_target="tpu_custom_call" | custom-call | flops 9200000000 | tf_op jit(solution)/shard_map/down_grad/pallas_call | solution.py:743
  147.8 111.9 %back.1 = (bf16[1024,768]{1,0:T(8,128)(2,1)}, bf16[512,768]{1,0:T(8,128)(2,1)}, bf16[512,768]{1,0:T(8,128)(2,1)}, bf16[512,768]{1,0:T(8,128)(2,1)}, bf16[512,768...) custom-call(bf16[1024,768]{1,0:T(8,128)(2,1)} %get-tuple-element.49., ...), custom_call_target="tpu_custom_call" | custom-call | flops 92000002048 | tf_op jit(solution)/shard_map/back/pallas_call | solution.py:622
  259.7 3.4 copy.58
  263.1 1.7 fusion.17
  264.9 2.4 copy.74
  267.3 1.2 copy.73
  268.4 1.2 copy.72
  269.6 1.2 copy.71
  270.7 13.3 %start_back.1 = (bf16[512,768]{1,0:T(8,128)(2,1)}, bf16[512,768]{1,0:T(8,128)(2,1)}, bf16[1024,2304]{1,0:T(8,128)(2,1)}, f32[8,768]{1,0:T(8,128)}) custom-call(bf16[1024,768]{1,0:T(8,128)(2,1)} %get-tuple-element.61.query_grad_ref, bf16[512,768]{1,0:T(8,128)(2,1)} %get-tuple-element.62.key0_ref, bf16[512,768]{1,0:T(8,128)(2,1)} %get-tuple-element.63.key1_ref, ...), custom_call_target="tpu_custom_call" | custom-call | flops 11500000256 | tf_op jit(solution)/shard_map/start_back/pallas_call | solution.py:856
  285.5 7.7 %qkv_grad.1 = bf16[3,768,768]{2,1,0:T(8,128)(2,1)} custom-call(bf16[1024,768]{1,0:T(8,128)(2,1)} %get-tuple-element.72.normed_ref, bf16[1024,2304]{1,0:T(8,128)(2,1)} %get-tuple-element.73.grad_ref), custom_call_target="tpu_custom_call" | custom-call | flops 8049999872 | tf_op jit(solution)/shard_map/qkv_grad/pallas_call | solution.py:795
  293.2 2.2 constant_dynamic-slice_fusion.4
  295.5 1.3 copy.89
  298.4 2.3 collective-permute-done.9
  300.7 1.6 collective-permute-start.10
  302.4 3.2 collective-permute-done.10
  305.6 1.6 collective-permute-start.11
  307.3 3.0 collective-permute-done.11
  311.5 3.5 collective-permute-done.12
  316.9 7.4 %collective-permute-start.7 = (bf16[512,768]{1,0:T(8,128)(2,1)}, bf16[512,768]{1,0:T(8,128)(2,1)}, u32[]{:S(2)}, u32[]{:S(2)}) collective-permute-start(bf16[512,768]{1,0:T(8,128)(2,1)} %get-tuple-element.68), channel_id=1, source_target_pairs={{0,0},{1,1},{4,2},{5,3},{2,4},{3,5},{6,6},{7,7},{8,8},{9,9},{12,10... | collective-permute-start | bytes 2359304 | tf_op jit(solution)/shard_map/ppermute | solution.py:904
  325.1 1.4 fusion.7
  326.5 1.9 fusion
  328.6 1.6 collective-permute-start.20
  332.1 20.5 %collective-permute-done.8 = bf16[512,768]{1,0:T(8,128)(2,1)} collective-permute-done((bf16[512,768]{1,0:T(8,128)(2,1)}, bf16[512,768]{1,0:T(8,128)(2,1)}, u32[]{:S(2)}, u32[]{:S(2)}) %collective-permute-start.8) | collective-permute-done | bytes 786464 | tf_op jit(solution)/shard_map/ppermute | solution.py:904
  352.6 2.4 select_bitcast_fusion.1
  356.1 1.6 collective-permute-start.21
  359.0 3.1 collective-permute-done.21
  362.2 2.4 collective-permute-done.16
  365.8 1.9 maximum_convert_fusion
  367.6 2.1 collective-permute-start.22
  369.7 1.5 collective-permute-done.17
  371.2 5.0 %collective-permute-start.18 = (bf16[3,48,384]{2,1,0:T(8,128)(2,1)S(1)}, bf16[3,48,384]{2,1,0:T(8,128)(2,1)S(1)}, u32[]{:S(2)}, u32[]{:S(2)}) collective-permute-start(bf16[3,48,384]{2,1,0:T(8,128)(2,1)S(1)} %fusion.5), channel_id=1, source_target_pairs={{0,2},{1,3},{2,0},{3,1},{4,6},{5,7},{6,4},{7,5},{8,10},{9,11},{10,... | collective-permute-start | bytes 331784 | tf_op jit(solution)/shard_map/ppermute | solution.py:904
  376.3 2.3 collective-permute-start.23
  378.6 5.2 %collective-permute-done.18 = bf16[3,48,384]{2,1,0:T(8,128)(2,1)S(1)} collective-permute-done((bf16[3,48,384]{2,1,0:T(8,128)(2,1)S(1)}, bf16[3,48,384]{2,1,0:T(8,128)(2,1)S(1)}, u32[]{:S(2)}, u32[]{:S(2)}) %collective-permute-start.18) | collective-permute-done | bytes 110624 | tf_op jit(solution)/shard_map/ppermute | solution.py:904
  383.9 1.2 collective-permute-done.23
  386.0 3.1 collective-permute-done.19
  389.2 1.1 collective-permute-done.24
  (139 shorter events, 26.2 us)
Async XLA Ops:
  0.7 17.7 %copy-start = (bf16[2048,768]{1,0:T(8,128)(2,1)S(1)}, bf16[2048,768]{1,0:T(8,128)(2,1)}, u32[]{:S(2)}) copy-start(bf16[2048,768]{1,0:T(8,128)(2,1)} %param.19) | copy-start | bytes 9437188
  0.7 10.3 %copy-start.21 = (s32[2]{0:T(128)S(1)}, s32[2]{0:T(128)}, u32[]{:S(2)}) copy-start(s32[2]{0:T(128)} %param.18) | copy-start | bytes 28
  0.7 13.3 %copy-start.14 = (bf16[768]{0:T(1024)(128)(2,1)S(1)}, bf16[768]{0:T(1024)(128)(2,1)}, u32[]{:S(2)}) copy-start(bf16[768]{0:T(1024)(128)(2,1)} %param.20) | copy-start | bytes 4612
  0.7 13.9 %copy-start.15 = (bf16[768]{0:T(1024)(128)(2,1)S(1)}, bf16[768]{0:T(1024)(128)(2,1)}, u32[]{:S(2)}) copy-start(bf16[768]{0:T(1024)(128)(2,1)} %param.21) | copy-start | bytes 4612
  0.7 14.5 %copy-start.12 = (bf16[768]{0:T(1024)(128)(2,1)S(1)}, bf16[768]{0:T(1024)(128)(2,1)}, u32[]{:S(2)}) copy-start(bf16[768]{0:T(1024)(128)(2,1)} %param.23) | copy-start | bytes 4612
  0.7 14.5 %copy-start.13 = (bf16[768]{0:T(1024)(128)(2,1)S(1)}, bf16[768]{0:T(1024)(128)(2,1)}, u32[]{:S(2)}) copy-start(bf16[768]{0:T(1024)(128)(2,1)} %param.24) | copy-start | bytes 4612
  3.5 15.5 %collective-permute-start.2 = (bf16[512,768]{1,0:T(8,128)(2,1)}, bf16[512,768]{1,0:T(8,128)(2,1)}, u32[]{:S(2)}, u32[]{:S(2)}) collective-permute-start(bf16[512,768]{1,0:T(8,128)(2,1)} %get-tuple-element.88), channel_id=1, source_target_pairs={{0,0},{1,1},{2,4},{3,5},{4,2},{5,3},{6,6},{7,7},{8,8},{9,9},{10,12... | collective-permute-start | bytes 2359304 | tf_op jit(solution)/shard_map/ppermute | solution.py:904
  11.0 4.9 %collective-permute-start.1 = (s32[2]{0:T(128)S(1)}, s32[2]{0:T(128)S(1)}, u32[]{:S(2)}, u32[]{:S(2)}) collective-permute-start(s32[2]{0:T(128)S(1)} %copy-done.21), channel_id=1, source_target_pairs={{0,4},{1,5},{2,6},{3,7},{4,0},{5,1},{6,2},{7,3},{8,12},{9,13},{10,... | collective-permute-start | bytes 32 | tf_op jit(solution)/shard_map/ppermute | solution.py:904
  11.0 29.0 %collective-permute-start = (bf16[512,768]{1,0:T(8,128)(2,1)}, bf16[512,768]{1,0:T(8,128)(2,1)}, u32[]{:S(2)}, u32[]{:S(2)}) collective-permute-start(bf16[512,768]{1,0:T(8,128)(2,1)} %get-tuple-element.89), channel_id=1, source_target_pairs={{0,1},{1,0},{2,5},{3,4},{4,3},{5,2},{6,7},{7,6},{8,9},{9,8},{10,13... | collective-permute-start | bytes 2359304 | tf_op jit(solution)/shard_map/ppermute | solution.py:904
  40.0 6.5 %copy-start.6 = (bf16[2,512,768]{2,1,0:T(8,128)(2,1)S(1)}, bf16[2,512,768]{2,1,0:T(8,128)(2,1)}, u32[]{:S(2)}) copy-start(bf16[2,512,768]{2,1,0:T(8,128)(2,1)} %param.33) | copy-start | bytes 4718596
  45.9 7.7 %copy-start.16 = (bf16[768]{0:T(1024)(128)(2,1)S(1)}, bf16[768]{0:T(1024)(128)(2,1)}, u32[]{:S(2)}) copy-start(bf16[768]{0:T(1024)(128)(2,1)} %param.26) | copy-start | bytes 4612
  45.9 8.3 %copy-start.17 = (bf16[768]{0:T(1024)(128)(2,1)S(1)}, bf16[768]{0:T(1024)(128)(2,1)}, u32[]{:S(2)}) copy-start(bf16[768]{0:T(1024)(128)(2,1)} %param.27) | copy-start | bytes 4612
  45.9 8.9 %copy-start.18 = (bf16[768]{0:T(1024)(128)(2,1)S(1)}, bf16[768]{0:T(1024)(128)(2,1)}, u32[]{:S(2)}) copy-start(bf16[768]{0:T(1024)(128)(2,1)} %param.28) | copy-start | bytes 4612
  45.9 9.5 %copy-start.19 = (bf16[768]{0:T(1024)(128)(2,1)S(1)}, bf16[768]{0:T(1024)(128)(2,1)}, u32[]{:S(2)}) copy-start(bf16[768]{0:T(1024)(128)(2,1)} %param.32) | copy-start | bytes 4612
  45.9 10.0 %copy-start.11 = (bf16[3072]{0:T(1024)(128)(2,1)S(1)}, bf16[3072]{0:T(1024)(128)(2,1)}, u32[]{:S(2)}) copy-start(bf16[3072]{0:T(1024)(128)(2,1)} %param.30) | copy-start | bytes 18436
  45.9 13.1 %collective-permute-start.4 = (bf16[512,1536]{1,0:T(8,128)(2,1)}, bf16[512,1536]{1,0:T(8,128)(2,1)}, u32[]{:S(2)}, u32[]{:S(2)}) collective-permute-start(bf16[512,1536]{1,0:T(8,128)(2,1)} %get-tuple-element.51.refs_1_.refs_5_), channel_id=1, source_target_pairs={{0,4},{1,5},{2,6},{3,7},{4,0},{5,1},{6,2},{7,3},{8,12},{9,13},{10,... | collective-permute-start | bytes 4718600 | tf_op jit(solution)/shard_map/ppermute | solution.py:904
  46.0 13.0 %collective-permute-start.3 = (bf16[512,1536]{1,0:T(8,128)(2,1)}, bf16[512,1536]{1,0:T(8,128)(2,1)}, u32[]{:S(2)}, u32[]{:S(2)}) collective-permute-start(bf16[512,1536]{1,0:T(8,128)(2,1)} %get-tuple-element.50.refs_0_.refs_4_), channel_id=1, source_target_pairs={{0,4},{1,5},{2,6},{3,7},{4,0},{5,1},{6,2},{7,3},{8,12},{9,13},{10,... | collective-permute-start | bytes 4718600 | tf_op jit(solution)/shard_map/ppermute | solution.py:904
  46.6 42.6 %collective-permute-start.6 = (bf16[512,768]{1,0:T(8,128)(2,1)S(1)}, bf16[512,768]{1,0:T(8,128)(2,1)S(1)}, u32[]{:S(2)}, u32[]{:S(2)}) collective-permute-start(bf16[512,768]{1,0:T(8,128)(2,1)S(1)} %get-tuple-element.86), channel_id=1, source_target_pairs={{0,1},{1,0},{2,5},{3,4},{4,3},{5,2},{6,7},{7,6},{8,9},{9,8},{10,13... | collective-permute-start | bytes 2359304 | tf_op jit(solution)/shard_map/ppermute | solution.py:904
  51.8 37.4 %collective-permute-start.5 = (bf16[512,768]{1,0:T(8,128)(2,1)S(1)}, bf16[512,768]{1,0:T(8,128)(2,1)}, u32[]{:S(2)}, u32[]{:S(2)}) collective-permute-start(bf16[512,768]{1,0:T(8,128)(2,1)S(1)} %get-tuple-element.87), channel_id=1, source_target_pairs={{0,0},{1,1},{2,4},{3,5},{4,2},{5,3},{6,6},{7,7},{8,8},{9,9},{10,12... | collective-permute-start | bytes 2359304 | tf_op jit(solution)/shard_map/ppermute | solution.py:904
  89.2 0.9 copy-start.22
  264.9 2.4 copy-start.4
  264.9 3.6 copy-start.3
  267.3 2.3 copy-start.2
  295.5 2.0 copy-start.20
  295.5 2.1 copy-start.10
  295.5 6.8 %copy-start.8 = (bf16[5,96,768]{2,1,0:T(8,128)(2,1)S(1)}, bf16[5,96,768]{2,1,0:T(8,128)(2,1)}, u32[]{:S(2)}) copy-start(bf16[5,96,768]{2,1,0:T(8,128)(2,1)} %get-tuple-element.74) | copy-start | bytes 2211844
  296.8 29.6 %collective-permute-start.14 = (bf16[3,2,2,96,768]{4,3,0,2,1:T(8,128)(2,1)}, bf16[3,2,2,96,768]{4,3,0,2,1:T(8,128)(2,1)}, u32[]{:S(2)}, u32[]{:S(2)}) collective-permute-start(bf16[3,2,2,96,768]{4,3,0,2,1:T(8,128)(2,1)} %bitcast.99), channel_id=1, source_target_pairs={{0,4},{1,5},{2,6},{3,7},{4,0},{5,1},{6,2},{7,3},{8,12},{9,13},{10,... | collective-permute-start | bytes 5308424 | tf_op jit(solution)/shard_map/ppermute | solution.py:904
  297.8 2.9 collective-permute-start.9
  300.7 4.9 %collective-permute-start.10 = (f32[30,768]{1,0:T(8,128)S(1)}, f32[30,768]{1,0:T(8,128)S(1)}, u32[]{:S(2)}, u32[]{:S(2)}) collective-permute-start(f32[30,768]{1,0:T(8,128)S(1)} %add.164), channel_id=1, source_target_pairs={{0,8},{1,9},{2,10},{3,11},{4,12},{5,13},{6,14},{7,15},{8,0},{9,1},... | collective-permute-start | bytes 276488 | tf_op jit(solution)/shard_map/ppermute | solution.py:904
  302.4 8.0 %copy-start.9 = (bf16[1,384,768]{2,1,0:T(8,128)(2,1)S(1)}, bf16[1,384,768]{2,1,0:T(8,128)(2,1)}, u32[]{:S(2)}) copy-start(bf16[1,384,768]{2,1,0:T(8,128)(2,1)} %get-tuple-element.75) | copy-start | bytes 1769476
  305.6 4.7 %collective-permute-start.11 = (f32[30,768]{1,0:T(8,128)S(1)}, f32[30,768]{1,0:T(8,128)S(1)}, u32[]{:S(2)}, u32[]{:S(2)}) collective-permute-start(f32[30,768]{1,0:T(8,128)S(1)} %add.165), channel_id=1, source_target_pairs={{0,16},{1,17},{2,18},{3,19},{4,20},{5,21},{6,22},{7,23},{8,24},{9,... | collective-permute-start | bytes 276488 | tf_op jit(solution)/shard_map/ppermute | solution.py:904
  310.3 4.7 %collective-permute-start.12 = (f32[30,768]{1,0:T(8,128)S(1)}, f32[30,768]{1,0:T(8,128)S(1)}, u32[]{:S(2)}, u32[]{:S(2)}) collective-permute-start(f32[30,768]{1,0:T(8,128)S(1)} %add.166), channel_id=1, source_target_pairs={{0,1},{1,0},{2,3},{3,2},{4,5},{5,4},{6,7},{7,6},{8,9},{9,8},{10,11... | collective-permute-start | bytes 276488 | tf_op jit(solution)/shard_map/ppermute | solution.py:904
  315.0 9.4 %collective-permute-start.13 = (f32[30,768]{1,0:T(8,128)S(1)}, f32[30,768]{1,0:T(8,128)S(1)}, u32[]{:S(2)}, u32[]{:S(2)}) collective-permute-start(f32[30,768]{1,0:T(8,128)S(1)} %add.167), channel_id=1, source_target_pairs={{0,2},{1,3},{2,0},{3,1},{4,6},{5,7},{6,4},{7,5},{8,10},{9,11},{10,... | collective-permute-start | bytes 276488 | tf_op jit(solution)/shard_map/ppermute | solution.py:904
  316.9 15.1 %collective-permute-start.7 = (bf16[512,768]{1,0:T(8,128)(2,1)}, bf16[512,768]{1,0:T(8,128)(2,1)}, u32[]{:S(2)}, u32[]{:S(2)}) collective-permute-start(bf16[512,768]{1,0:T(8,128)(2,1)} %get-tuple-element.68), channel_id=1, source_target_pairs={{0,0},{1,1},{4,2},{5,3},{2,4},{3,5},{6,6},{7,7},{8,8},{9,9},{12,10... | collective-permute-start | bytes 2359304 | tf_op jit(solution)/shard_map/ppermute | solution.py:904
  324.4 28.2 %collective-permute-start.8 = (bf16[512,768]{1,0:T(8,128)(2,1)}, bf16[512,768]{1,0:T(8,128)(2,1)}, u32[]{:S(2)}, u32[]{:S(2)}) collective-permute-start(bf16[512,768]{1,0:T(8,128)(2,1)} %get-tuple-element.69), channel_id=1, source_target_pairs={{1,0},{0,1},{5,2},{4,3},{3,4},{2,5},{7,6},{6,7},{9,8},{8,9},{13,10... | collective-permute-start | bytes 2359304 | tf_op jit(solution)/shard_map/ppermute | solution.py:904
  328.6 26.4 %collective-permute-start.20 = (bf16[3,2,48,768]{3,2,0,1:T(8,128)(2,1)S(1)}, bf16[3,2,48,768]{3,2,0,1:T(8,128)(2,1)}, u32[]{:S(2)}, u32[]{:S(2)}) collective-permute-start(bf16[3,2,48,768]{3,2,0,1:T(8,128)(2,1)S(1)} %dynamic-slice_bitcast_fusion.4), channel_id=1, source_target_pairs={{0,16},{1,17},{2,18},{3,19},{4,20},{5,21},{6,22},{7,23},{8,24},{9,... | collective-permute-start | bytes 1327112 | tf_op jit(solution)/shard_map/ppermute | solution.py:904
  331.5 26.2 %collective-permute-start.15 = (bf16[3,2,48,768]{3,2,0,1:T(8,128)(2,1)S(1)}, bf16[3,2,48,768]{3,2,0,1:T(8,128)(2,1)S(1)}, u32[]{:S(2)}, u32[]{:S(2)}) collective-permute-start(bf16[3,2,48,768]{3,2,0,1:T(8,128)(2,1)S(1)} %dynamic-slice_bitcast_fusion.5), channel_id=1, source_target_pairs={{0,8},{1,9},{2,10},{3,11},{4,12},{5,13},{6,14},{7,15},{8,0},{9,1},... | collective-permute-start | bytes 1327112 | tf_op jit(solution)/shard_map/ppermute | solution.py:904
  356.1 6.0 %collective-permute-start.21 = (bf16[3,48,768]{2,1,0:T(8,128)(2,1)S(1)}, bf16[3,48,768]{2,1,0:T(8,128)(2,1)S(1)}, u32[]{:S(2)}, u32[]{:S(2)}) collective-permute-start(bf16[3,48,768]{2,1,0:T(8,128)(2,1)S(1)} %dynamic-slice_bitcast_fusion.6), channel_id=1, source_target_pairs={{0,8},{1,9},{2,10},{3,11},{4,12},{5,13},{6,14},{7,15},{8,0},{9,1},... | collective-permute-start | bytes 663560 | tf_op jit(solution)/shard_map/ppermute | solution.py:904
  358.5 6.1 %collective-permute-start.16 = (bf16[3,48,768]{2,1,0:T(8,128)(2,1)}, bf16[3,48,768]{2,1,0:T(8,128)(2,1)S(1)}, u32[]{:S(2)}, u32[]{:S(2)}) collective-permute-start(bf16[3,48,768]{2,1,0:T(8,128)(2,1)} %dynamic-slice_bitcast_fusion.7), channel_id=1, source_target_pairs={{0,16},{1,17},{2,18},{3,19},{4,20},{5,21},{6,22},{7,23},{8,24},{9,... | collective-permute-start | bytes 663560 | tf_op jit(solution)/shard_map/ppermute | solution.py:904
  362.2 3.6 copy-start.5
  365.7 5.6 %collective-permute-start.17 = (bf16[3,48,384]{2,1,0:T(8,128)(2,1)S(1)}, bf16[3,48,384]{2,1,0:T(8,128)(2,1)S(1)}, u32[]{:S(2)}, u32[]{:S(2)}) collective-permute-start(bf16[3,48,384]{2,1,0:T(8,128)(2,1)S(1)} %bitcast.112), channel_id=1, source_target_pairs={{0,1},{1,0},{2,3},{3,2},{4,5},{5,4},{6,7},{7,6},{8,9},{9,8},{10,11... | collective-permute-start | bytes 331784 | tf_op jit(solution)/shard_map/ppermute | solution.py:904
  367.6 8.6 %collective-permute-start.22 = (bf16[3,48,384]{2,1,0:T(8,128)(2,1)S(1)}, bf16[3,48,384]{2,1,0:T(8,128)(2,1)S(1)}, u32[]{:S(2)}, u32[]{:S(2)}) collective-permute-start(bf16[3,48,384]{2,1,0:T(8,128)(2,1)S(1)} %bitcast.111), channel_id=1, source_target_pairs={{0,1},{1,0},{2,3},{3,2},{4,5},{5,4},{6,7},{7,6},{8,9},{9,8},{10,11... | collective-permute-start | bytes 331784 | tf_op jit(solution)/shard_map/ppermute | solution.py:904
  371.2 12.6 %collective-permute-start.18 = (bf16[3,48,384]{2,1,0:T(8,128)(2,1)S(1)}, bf16[3,48,384]{2,1,0:T(8,128)(2,1)S(1)}, u32[]{:S(2)}, u32[]{:S(2)}) collective-permute-start(bf16[3,48,384]{2,1,0:T(8,128)(2,1)S(1)} %fusion.5), channel_id=1, source_target_pairs={{0,2},{1,3},{2,0},{3,1},{4,6},{5,7},{6,4},{7,5},{8,10},{9,11},{10,... | collective-permute-start | bytes 331784 | tf_op jit(solution)/shard_map/ppermute | solution.py:904
  376.3 8.9 %collective-permute-start.23 = (bf16[3,48,384]{2,1,0:T(8,128)(2,1)S(1)}, bf16[3,48,384]{2,1,0:T(8,128)(2,1)S(1)}, u32[]{:S(2)}, u32[]{:S(2)}) collective-permute-start(bf16[3,48,384]{2,1,0:T(8,128)(2,1)S(1)} %fusion.6), channel_id=1, source_target_pairs={{0,2},{1,3},{2,0},{3,1},{4,6},{5,7},{6,4},{7,5},{8,10},{9,11},{10,... | collective-permute-start | bytes 331784 | tf_op jit(solution)/shard_map/ppermute | solution.py:904
  383.9 5.3 %collective-permute-start.19 = (bf16[3,48,384]{2,1,0:T(8,128)(2,1)S(1)}, bf16[3,48,384]{2,1,0:T(8,128)(2,1)S(1)}, u32[]{:S(2)}, u32[]{:S(2)}) collective-permute-start(bf16[3,48,384]{2,1,0:T(8,128)(2,1)S(1)} %add_convert_fusion.1), channel_id=1, source_target_pairs={{0,1},{1,0},{2,3},{3,2},{4,5},{5,4},{6,7},{7,6},{8,9},{9,8},{10,11... | collective-permute-start | bytes 331784 | tf_op jit(solution)/shard_map/ppermute | solution.py:904
  385.2 5.1 %collective-permute-start.24 = (bf16[3,48,384]{2,1,0:T(8,128)(2,1)S(1)}, bf16[3,48,384]{2,1,0:T(8,128)(2,1)S(1)}, u32[]{:S(2)}, u32[]{:S(2)}) collective-permute-start(bf16[3,48,384]{2,1,0:T(8,128)(2,1)S(1)} %add_convert_fusion), channel_id=1, source_target_pairs={{0,1},{1,0},{2,3},{3,2},{4,5},{5,4},{6,7},{7,6},{8,9},{9,8},{10,11... | collective-permute-start | bytes 331784 | tf_op jit(solution)/shard_map/ppermute | solution.py:904
  389.2 2.2 copy-start.7
  390.4 2.8 copy-start.1

commit v3 on v2

--- a/solution.py
+++ b/solution.py
@@ -319,21 +319,18 @@
 
 
 class Reduction:
-    COPIES = 8
-
-    def __init__(self, source, out, scratch, at):
+    def __init__(self, source, out, scratch):
         self.source, self.out = source, out
-        self.own, self.from_core, self.first, self.second, self.near, self.far, self.other = scratch[:7]
-        self.sends, self.receives, self.local = scratch[7:10]
-        self.at = at
-        self.parts, _, _, self.rows, self.width = self.own.shape
+        self.own = source.at[:, :, :, here()[4]]
+        self.from_core, self.first, self.second, self.near, self.far, self.other = scratch[:6]
+        self.sends, self.receives, self.local = scratch[6:9]
+        self.parts, _, _, self.rows, self.width = self.from_core.shape
         self.half, self.top = self.width // 2, self.rows // 2
 
     @staticmethod
     def scratch(parts, block, width):
         half, top = width // 2, block // 2
         return [
-            pltpu.VMEM((parts, 2, 2, block, width), BF16),
             pltpu.VMEM((parts, 2, 2, block, width), BF16),
             pltpu.VMEM((2, parts, 2, block, half), BF16),
             pltpu.VMEM((2, parts, block, half), BF16),
@@ -342,7 +339,7 @@
             pltpu.VMEM((parts, top, width), BF16),
             pltpu.SemaphoreType.DMA((8,)),
             pltpu.SemaphoreType.DMA((8,)),
-            pltpu.SemaphoreType.DMA((3,)),
+            pltpu.SemaphoreType.DMA((2,)),
         ]
 
     def copy(self, number):
@@ -363,16 +360,10 @@
         )[number]()
         return remote(source, target, self.sends, self.receives, number, number, device)
 
-    def load(self):
-        core = here()[4]
-        return pltpu.make_async_copy(self.source.at[:, :, :, core], self.own, self.local.at[0])
-
     def to_cores(self):
         self.copy(0).start()
-        self.load().start()
 
     def to_first(self):
-        self.load().wait()
         self.copy(0).wait()
         for part in range(self.parts):
             for i in range(2):
@@ -424,8 +415,8 @@
         kept = pl.ds(pl.multiple_of((z % 2) * self.top, self.top), self.top)
         given = pl.ds(pl.multiple_of((1 - z % 2) * self.top, self.top), self.top)
         return (
-            pltpu.make_async_copy(self.own.at[:, y, x, kept], self.out.at[:, kept], self.local.at[1]),
-            pltpu.make_async_copy(self.other, self.out.at[:, given], self.local.at[2]),
+            pltpu.make_async_copy(self.own.at[:, y, x, kept], self.out.at[:, kept], self.local.at[0]),
+            pltpu.make_async_copy(self.other, self.out.at[:, given], self.local.at[1]),
         )
 
     def to_out(self):
@@ -517,24 +508,42 @@
     pl.semaphore_wait(barrier, expected)
 
 
+def fixed_any():
+    return pl.BlockSpec(memory_space=pl.ANY)
+
+
 def back_kernel(
-    query_ref, grad_ref, context_ref, logsum_ref, *refs, pieces
+    query_ref, grad_ref, context_ref, logsum_ref, *refs, pieces, parts
 ):
     key_refs, value_refs = refs[:pieces], refs[pieces : 2 * pieces]
-    down_ref, up_ref, layer_ref = refs[2 * pieces : 2 * pieces + 3]
-    refs = refs[2 * pieces + 3 :]
+    refs = refs[2 * pieces :]
+    normed_ref, hidden_grad_ref, whole_context_ref, branch_ref, active_ref, cot0_ref, cot1_ref, layer_ref = refs[:8]
+    refs = refs[8:]
     near = pieces // 2
     query_grad_ref = refs[0]
     key_grad_refs, value_grad_refs = refs[1 : 1 + near], refs[1 + near : 1 + 2 * near]
     far_out, layer_out, down_out, up_out = refs[1 + 2 * near : 5 + 2 * near]
     refs = refs[5 + 2 * near :]
-    down = Reduction(down_ref, down_out, refs[:10], 0)
-    up = Reduction(up_ref, up_out, refs[10:20], 0)
-    far_grads, far_sends, far_receives, layer_sends, layer_receives, layer_local = refs[20:]
+    down_parts, up_parts = refs[:2]
+    chunks = []
+    for number, (which, at, many) in enumerate(back_chunks(down_parts.shape, up_parts.shape)):
+        scratch = refs[2 + 9 * number : 11 + 9 * number]
+        if which == "down":
+            here_rows = pl.ds(at, many)
+            chunks.append(
+                Reduction(down_parts.at[:, :, :, :, here_rows], down_out.at[:, here_rows], scratch)
+            )
+        else:
+            here_parts = pl.ds(at, many)
+            chunks.append(Reduction(up_parts.at[here_parts], up_out.at[here_parts], scratch))
+    one, two, three, four = chunks
+    far_grads, far_sends, far_receives, layer_sends, layer_receives, layer_local = refs[38:]
     back = Return(layer_out, layer_sends, layer_receives, layer_local)
     block = key_refs[0].shape[0]
     layer_blocks = [layer_ref.at[pl.ds(p * block, block)] for p in range(2)]
-    pair, pairs = pl.program_id(0), pl.num_programs(0)
+    step = pl.program_id(0)
+    made = 2 * parts + 1
+    pair, last = step - made, pl.num_programs(0) - 1
 
     def far_copy(which):
         return remote(
@@ -543,96 +552,153 @@
 
     def begin():
         meet(("core", "x", "y", "near", "far"), back)
-        down.to_cores()
-        up.to_cores()
         back.begin(0, layer_blocks[0])
         back.begin(1, layer_blocks[1])
 
-    def far_free():
-        far_copy(pair - 1).wait_send()
-
-    def far_send():
-        far_copy(pair).start()
-
     plan = {
         (0, 0): [begin],
-        (0, 2): [down.to_first],
-        (1, 0): [up.to_first],
-        (1, 3): [down.to_second],
-        (3, 0): [down.to_near],
-        (3, 1): [up.to_second],
-        (3, 3): [down.to_far],
-        (4, 1): [up.to_near],
-        (5, 0): [up.to_far, down.to_other],
-        (5, 3): [down.to_out],
+        (2, 0): [one.to_cores],
+        (4, 0): [one.to_first],
+        (5, 0): [two.to_cores],
+        (8, 0): [one.to_second, two.to_first],
+        (9, 0): [three.to_cores, four.to_cores],
+        (10, 0): [one.to_near],
+        (10, 1): [two.to_second, three.to_first],
+        (10, 3): [one.to_far],
+        (11, 0): [four.to_first],
+        (11, 2): [one.to_other, two.to_near, three.to_second],
+        (12, 0): [one.to_out, two.to_far],
+        (12, 1): [three.to_near],
+        (12, 2): [four.to_second],
+        (12, 3): [three.to_far],
+        (13, 0): [two.to_other],
+        (13, 1): [four.to_near],
+        (13, 2): [three.to_other],
+        (13, 3): [two.to_out, four.to_far],
+        (14, 0): [three.to_out],
+        (14, 1): [four.to_other],
+        (14, 3): [four.to_out],
     }
+
+    def run_plan(place, steps):
+        for (at, where), actions in plan.items():
+            if where == place and at in steps:
+
+                @pl.when(step == at)
+                def _():
+                    for action in actions:
+                        action()
+
+    run_plan(0, range(made))
+
+    @pl.when(step < parts)
+    def _():
+        part = dot(normed_ref[...], hidden_grad_ref[...], TN).astype(BF16)
+        up_parts[step] = part.reshape(up_parts.shape[1:])
+
+    @pl.when(step == parts)
+    def _():
+        part = dot(whole_context_ref[...], branch_ref[...], TN).astype(BF16)
+        up_parts[parts] = part.reshape(up_parts.shape[1:])
+
+    @pl.when((step > parts) & (step < made))
+    def _():
+        part = dot(active_ref[:block], cot0_ref[...], TN) + dot(active_ref[block:], cot1_ref[...], TN)
+        part = part.astype(BF16).reshape(down_parts.shape[3:])
+        at = step - parts - 1
+        down_parts[0, at // 2, at % 2] = part
 
     def before(place):
         def run():
-            for (step, at), actions in plan.items():
-                if at == place:
-
-                    @pl.when(pair == step)
-                    def _():
-                        for action in actions:
-                            action()
-
+            run_plan(place, range(made, 100))
             if place == 0:
-                pl.when(pair > 0)(far_free)
+
+                @pl.when(pair > 0)
+                def _():
+                    far_copy(pair - 1).wait_send()
+
             if place == near:
-                far_send()
+                far_copy(pair).start()
 
         return run
 
-    order = []
-    for i in range(near):
-        order.append((key_refs[near + i], value_refs[near + i], far_grads.at[0, pl.ds(i * block, block)], far_grads.at[1, pl.ds(i * block, block)]))
-    for i in range(near):
-        order.append((key_refs[i], value_refs[i], key_grad_refs[i], value_grad_refs[i]))
-    steps = [one + (before(place),) for place, one in enumerate(order)]
-    attend_back_step(query_ref, grad_ref, context_ref, logsum_ref, steps, query_grad_ref)
-
-    @pl.when(pair == pairs - 1)
+    @pl.when(step >= made)
     def _():
-        up.to_other()
+        order = []
+        for i in range(near):
+            far_rows = pl.ds(i * block, block)
+            order.append(
+                (key_refs[near + i], value_refs[near + i], far_grads.at[0, far_rows], far_grads.at[1, far_rows])
+            )
+        for i in range(near):
+            order.append((key_refs[i], value_refs[i], key_grad_refs[i], value_grad_refs[i]))
+        steps = [one_piece + (before(place),) for place, one_piece in enumerate(order)]
+        attend_back_step(query_ref, grad_ref, context_ref, logsum_ref, steps, query_grad_ref)
+
+    @pl.when(step == last)
+    def _():
         far_copy(pair).wait_send()
 
         def received(which, carry):
             far_copy(which).wait_recv()
             return carry
 
-        lax.fori_loop(0, pairs, received, 0)
+        lax.fori_loop(0, last + 1 - made, received, 0)
         back.finish(layer_blocks)
-        down.finish()
-        up.to_out()
-        up.finish()
-
-
-def back(query, grad, context, logsum, kvs, down_parts, up_parts, layer_out):
+        for chunk in chunks:
+            chunk.finish()
+
+
+def back_chunks(down_shape, up_shape):
+    block, parts = down_shape[-2], up_shape[0]
+    return [
+        ("up", 0, parts // 2),
+        ("up", parts // 2, parts - parts // 2),
+        ("down", 0, block // 2),
+        ("down", block // 2, block // 2),
+    ]
+
+
+def back(query, grad, context, logsum, kvs, normed, hidden_grad, branch, active, cots, layer_out):
     count, width = query.shape
     pairs, pieces, length = width // LANES, len(kvs), kvs[0].shape[0]
     near = pieces // 2
-    row = pl.BlockSpec((count, LANES), lambda p: (0, p))
-    piece = pl.BlockSpec((length, LANES), lambda p: (0, p))
-    anywhere = pl.BlockSpec(memory_space=pl.ANY)
-    sizes = [(parts.shape[0], parts.shape[1] // 8) for parts in (down_parts, up_parts)]
-    split = [
-        parts.reshape(n, 2, 2, 2, block, width) for parts, (n, block) in zip((down_parts, up_parts), sizes)
-    ]
+    parts = hidden_grad.shape[1] // width
+    made = 2 * parts + 1
+    pair = lambda i: jnp.maximum(i - made, 0)
+    row = pl.BlockSpec((count, LANES), lambda i: (0, pair(i)))
+    piece = pl.BlockSpec((length, LANES), lambda i: (0, pair(i)))
+    value = pl.BlockSpec((length, LANES), lambda i: (0, pairs + pair(i)))
+    whole = fixed((count, width))
+    up_rows, down_rows = width // 8, hidden_grad.shape[1] // 8
+    down_shape, up_shape = (1, 2, 2, 2, down_rows, width), (parts + 1, 2, 2, 2, up_rows, width)
     return pl.pallas_call(
-        functools.partial(back_kernel, pieces=pieces),
-        grid=(pairs,),
+        functools.partial(back_kernel, pieces=pieces, parts=parts),
+        grid=(made + pairs,),
         in_specs=[row] * 4
         + [piece] * pieces
-        + [pl.BlockSpec((length, LANES), lambda p: (0, pairs + p))] * pieces
-        + [anywhere] * 3,
-        out_specs=[row] + [piece] * (2 * near) + [anywhere] * 4,
+        + [value] * pieces
+        + [
+            whole,
+            pl.BlockSpec((count, width), lambda i: (0, jnp.minimum(i, parts - 1))),
+            whole,
+            whole,
+            pl.BlockSpec((count, width), lambda i: (0, jnp.clip(i - parts - 1, 0, parts - 1))),
+            fixed((length, width)),
+            fixed((length, width)),
+            fixed_any(),
+        ],
+        out_specs=[row] + [piece] * (2 * near) + [fixed_any()] * 4,
         out_shape=[shape_of((count, width))]
         + [shape_of((length, width))] * (2 * near)
         + [shape_of((pairs, 2, near * length, LANES)), shape_of((2, length, width))]
-        + [shape_of((n, block, width)) for n, block in sizes],
-        scratch_shapes=Reduction.scratch(*sizes[0], width)
-        + Reduction.scratch(*sizes[1], width)
+        + [shape_of((1, down_rows, width)), shape_of((parts + 1, up_rows, width))],
+        scratch_shapes=[pltpu.VMEM(down_shape, BF16), pltpu.VMEM(up_shape, BF16)]
+        + [
+            shape
+            for which, _, many in back_chunks(down_shape, up_shape)
+            for shape in Reduction.scratch(*((1, many) if which == "down" else (many, up_rows)), width)
+        ]
         + [
             pltpu.VMEM((2, near * length, LANES), BF16),
             pltpu.SemaphoreType.DMA((1,)),
@@ -644,9 +710,171 @@
         compiler_params=pltpu.CompilerParams(
             vmem_limit_bytes=VMEM_BYTES, collective_id=0, has_side_effects=True
         ),
-        cost_estimate=cost(80),
+        cost_estimate=cost(100),
         name="back",
-    )(query, grad, context, logsum, *kvs, *kvs, *split, layer_out)
+    )(
+        query, grad, context, logsum, *kvs, *kvs, normed, hidden_grad, context, branch, active, *cots, layer_out
+    )
+
+
+def tail_kernel(
+    query_grad, key0, key1, value0, value1, far, normed, x0, x1, middle_grad, weight,
+    time_ref, gain_ref, feed_ref, marks_ref,
+    tokens_out, qkv_out, sums_ref,
+    query_v, near_v, far_v, normed_v, x_v, middle_v, weight_v, key_v, value_v, token_v,
+    query_parts, key_parts, value_parts, *refs, total_tokens, parts,
+):
+    reductions = []
+    for number, made in enumerate((query_parts, key_parts, value_parts)):
+        reductions.append(Reduction(made, qkv_out.at[pl.ds(number, 1)], refs[9 * number : 9 * number + 9]))
+    of_query, of_key, of_value = reductions
+    sums_in, sums_sends, sums_receives, loads, back_sends, back_receives, back_local = refs[27:]
+    back = Return(tokens_out, back_sends, back_receives, back_local)
+    block, width = x0.shape
+    pairs = width // LANES
+    d, z, _, _, core = here()
+    copies = [
+        pltpu.make_async_copy(source, target, loads.at[number])
+        for number, (source, target) in enumerate(
+            (
+                (normed, normed_v), (query_grad, query_v), (key0, near_v.at[0, 0]), (value0, near_v.at[1, 0]),
+                (far, far_v), (weight, weight_v), (x0, x_v.at[0]), (middle_grad, middle_v),
+                (key1, near_v.at[0, 1]), (value1, near_v.at[1, 1]), (x1, x_v.at[1]),
+            )
+        )
+    ]
+    for copy in copies:
+        copy.start()
+    meet(("core", "x", "y", "near", "far"), back)
+
+    def product(grads, out):
+        out[0] = dot(normed_v[...], grads[...], TN).astype(BF16).reshape(out.shape[1:])
+
+    def start_block(p):
+        held = pl.ds(p * block, block)
+        for pair in range(pairs):
+            lanes = slice(pair * LANES, (pair + 1) * LANES)
+            key_v[held, lanes] = near_v[0, p, :, lanes] + far_v[pair, 0, held]
+            value_v[held, lanes] = near_v[1, p, :, lanes] + far_v[pair, 1, held]
+        normed_grad = 0.0
+        for part, grads in enumerate((query_v, key_v, value_v)):
+            columns = slice(part * width, (part + 1) * width)
+            normed_grad = normed_grad + dot(grads[held], weight_v[:, columns], NT)
+        unit, scale = norm_parts(x_v[p].astype(F32) + wide(time_ref))
+        token_grad = middle_v[held] + norm_backward(normed_grad, wide(gain_ref), unit, scale)
+        token_v[p] = token_grad.astype(BF16)
+        back.begin(p, token_v.at[p])
+        return [
+            column_sum(normed_grad * unit),
+            column_sum(normed_grad),
+            column_sum(query_v[held].astype(F32)),
+            column_sum(value_v[held].astype(F32)),
+            column_sum(token_grad),
+        ]
+
+    def sums_copy(number):
+        to = partners()[("core", "x", "y", "near", "far")[number]]
+        return remote(sums_ref, sums_in.at[number], sums_sends, sums_receives, number, number, to)
+
+    def sums_next(number):
+        sums_copy(number).wait()
+        sums_ref[...] = sums_ref[...] + sums_in[number]
+        if number < 4:
+            sums_copy(number + 1).start()
+
+    copies[0].wait()
+    copies[1].wait()
+    product(query_v, query_parts)
+    of_query.to_cores()
+    for copy in copies[2:8]:
+        copy.wait()
+    first = start_block(0)
+    of_query.to_first()
+    for copy in copies[8:]:
+        copy.wait()
+    second = start_block(1)
+    of_query.to_second()
+    sums = [a + b for a, b in zip(first, second)]
+    sums_ref[...] = jnp.zeros_like(sums_ref)
+    sums_ref[0:4] = feed_ref[0:4]
+    sums_ref[4 : 4 + parts] = feed_ref[8 : 8 + parts]
+    for number in range(4):
+        sums_ref[4 + parts + number : 5 + parts + number] = sums[number]
+    energy = jnp.sum(feed_ref[4:5], keepdims=True) / (width * total_tokens)
+    sums_ref[8 + parts : 9 + parts] = marks_ref[0:1] * energy + marks_ref[1:2]
+    sums_ref[9 + parts : 10 + parts] = marks_ref[2:3]
+    sequence = (d - core + z // 2) * 2 + z % 2
+    sums_ref[pl.ds(16 + sequence, 1)] = sums[4]
+    sums_copy(0).start()
+    product(key_v, key_parts)
+    of_key.to_cores()
+    sums_next(0)
+    product(value_v, value_parts)
+    of_value.to_cores()
+    of_query.to_near()
+    of_key.to_first()
+    sums_next(1)
+    of_query.to_far()
+    of_value.to_first()
+    sums_next(2)
+    of_key.to_second()
+    sums_next(3)
+    of_value.to_second()
+    of_query.to_other()
+    of_key.to_near()
+    sums_next(4)
+    of_value.to_near()
+    of_key.to_far()
+    of_query.to_out()
+    of_value.to_far()
+    of_key.to_other()
+    of_value.to_other()
+    of_key.to_out()
+    of_value.to_out()
+    back.finish([token_v.at[0], token_v.at[1]])
+    for one in reductions:
+        one.finish()
+
+
+def tail(query_grad, key_grads, value_grads, far, normed, xs, middle_grad, weight, time_row, gain, feed_sums, marks, total_tokens, hidden_parts):
+    block, width = xs[0].shape
+    count, total_seqs = 2 * block, 16
+    any_spec = fixed_any()
+    inside = pl.BlockSpec(memory_space=pltpu.VMEM)
+    up_rows = width // 8
+    parts = pltpu.VMEM((1, 2, 2, 2, up_rows, width), BF16)
+    held = lambda *shape, dtype=BF16: pltpu.VMEM(shape, dtype)
+    sums_shape = (16 + total_seqs, width)
+    return pl.pallas_call(
+        functools.partial(tail_kernel, total_tokens=total_tokens, parts=hidden_parts),
+        in_specs=[any_spec] * 11 + [inside] * 4,
+        out_specs=[any_spec, any_spec, inside],
+        out_shape=[
+            shape_of((2, block, width)), shape_of((3, up_rows, width)), shape_of(sums_shape, F32),
+        ],
+        scratch_shapes=[
+            held(count, width), held(2, 2, block, width), held(*far.shape), held(count, width),
+            held(2, block, width), held(count, width, dtype=F32), held(*weight.shape), held(count, width),
+            held(count, width), held(2, block, width), parts, parts, parts,
+        ]
+        + Reduction.scratch(1, up_rows, width) * 3
+        + [
+            held(5, *sums_shape, dtype=F32),
+            pltpu.SemaphoreType.DMA((5,)),
+            pltpu.SemaphoreType.DMA((5,)),
+            pltpu.SemaphoreType.DMA((11,)),
+            pltpu.SemaphoreType.DMA((2,)),
+            pltpu.SemaphoreType.DMA((2,)),
+            pltpu.SemaphoreType.DMA((1,)),
+        ],
+        compiler_params=pltpu.CompilerParams(
+            vmem_limit_bytes=VMEM_BYTES, collective_id=1, has_side_effects=True
+        ),
+        cost_estimate=cost(60),
+        name="tail",
+    )(
+        query_grad, *key_grads, *value_grads, far, normed, *xs, middle_grad, weight, time_row, gain, feed_sums, marks
+    )
 
 
 def gelu_parts(hidden):
@@ -1013,52 +1241,53 @@
         ).astype(dtype)
 
     parts = hidden_width // width
-    down_parts = down_grad(active, cots)[None]
-    up_out_parts = up_out_grad(normed_two, hidden_grad, context, branch)
+    bucket = step_value * BUCKETS // TSTEPS
+    lane = jnp.arange(width)
+    step_row = jnp.where((lane == sequence) & (core == 0), step_value, 0).astype(F32)
+    mark = (lane == bucket).astype(F32)
+    count_row = jnp.where(lane == BUCKETS + bucket, count / total_tokens, 0.0)
     if places.dp == 8:
-        made = back(query, context_grad, context, logsum, kvs, down_parts, up_out_parts, out)
-        query_grad, key_grads, value_grads = made[0], list(made[1:3]), list(made[3:5])
-        far_grads, layer_out = made[5], made[6]
+        made = back(
+            query, context_grad, context, logsum, kvs, normed_two, hidden_grad, branch, active, cots, out
+        )
+        layer_out = made[6]
         down_sum, up_out_sum = made[7][0].astype(F32), made[8].astype(F32)
-        far = jnp.moveaxis(far_grads.reshape(-1, 2, 2, local_len, LANES), 0, 3).reshape(2, 2, local_len, width)
-        far_key, far_value = [far[0, 0], far[0, 1]], [far[1, 0], far[1, 1]]
+        marks = jnp.concatenate([jnp.stack([mark, count_row, step_row]), jnp.zeros((5, width), F32)])
+        tokens_grad, qkv_sum, packed = tail(
+            made[0], made[1:3], made[3:5], made[5], normed, xs, middle_grad, qkv_weight, time_row, row(ln1_gain),
+            feed_sums, marks, total_tokens, parts,
+        )
+        tokens_grad, qkv_sum = tokens_grad.astype(F32), qkv_sum.astype(F32)
+        sums = packed[16:]
     else:
         layer_out = scattered([out[:local_len], out[local_len:]], BF16)
-        down_sum = reduce_parts(down_parts, places)[0]
-        up_out_sum = reduce_parts(up_out_parts, places)
+        down_sum = reduce_parts(down_grad(active, cots)[None], places)[0]
+        up_out_sum = reduce_parts(up_out_grad(normed_two, hidden_grad, context, branch), places)
         made = attend_back(query, context_grad, context, logsum, kvs)
-        query_grad, key_grads, value_grads = made[0], list(made[1:3]), list(made[5:7])
-        far_key = [send(g, places.swap(0)) for g in made[3:5]]
-        far_value = [send(g, places.swap(0)) for g in made[7:9]]
-    token0, token1, projected_grad, start_sums = start_back(
-        query_grad, key_grads + far_key, value_grads + far_value, xs, time_row,
-        middle_grad, row(ln1_gain), qkv_weight,
-    )
-    tokens_grad = scattered([token0, token1], F32)
-    qkv_sum = reduce_parts(qkv_grad(normed, projected_grad), places)
-
-    bucket = step_value * BUCKETS // TSTEPS
-    lane = jnp.arange(width)
-    energy = jnp.sum(feed_sums[4]) / (width * total_tokens)
-    stats_row = jnp.where(lane == bucket, energy, 0.0) + jnp.where(
-        lane == BUCKETS + bucket, count / total_tokens, 0.0
-    )
-    sequence_rows = jnp.where(jnp.arange(total_seqs)[:, None] == sequence, start_sums[4][None], 0.0)
-    step_row = jnp.where(lane[:total_seqs] == sequence, step_value, 0).astype(F32) * jnp.where(core == 0, 1.0, 0.0)
-    packed = jnp.concatenate(
-        [
-            feed_sums[0:4], feed_sums[8 : 8 + parts], start_sums[0:4], stats_row[None],
-            jnp.pad(step_row, (0, width - total_seqs))[None], sequence_rows,
-        ]
-    )
-    packed = sum_everywhere(packed, places)
+        token0, token1, projected_grad, start_sums = start_back(
+            made[0],
+            list(made[1:3]) + [send(g, places.swap(0)) for g in made[3:5]],
+            list(made[5:7]) + [send(g, places.swap(0)) for g in made[7:9]],
+            xs, time_row, middle_grad, row(ln1_gain), qkv_weight,
+        )
+        tokens_grad = scattered([token0, token1], F32)
+        qkv_sum = reduce_parts(qkv_grad(normed, projected_grad), places)
+        energy = jnp.sum(feed_sums[4]) / (width * total_tokens)
+        sequence_rows = jnp.where(jnp.arange(total_seqs)[:, None] == sequence, start_sums[4][None], 0.0)
+        packed = jnp.concatenate(
+            [
+                feed_sums[0:4], feed_sums[8 : 8 + parts], start_sums[0:4],
+                jnp.stack([mark * energy + count_row, step_row]), sequence_rows,
+            ]
+        )
+        packed = sum_everywhere(packed, places)
+        sums = packed[10 + parts :]
     piece = width // places.dp
     mine = lax.dynamic_slice_in_dim(packed[: 8 + parts], d * piece, piece, 1)
     up_piece = hidden_width // places.dp
     up_bias_sum = lax.dynamic_slice_in_dim(packed[4 : 4 + parts].reshape(-1), d * up_piece, up_piece, 0)
     stats = packed[8 + parts]
     steps = packed[9 + parts, :total_seqs].astype(jnp.int32)
-    sums = packed[10 + parts :]
     table_rows = time_table.shape[0] // places.dp
     chosen = (steps[None, :] == (jnp.arange(table_rows) + d * table_rows)[:, None]).astype(F32)
     table_grad = jnp.dot(chosen, sums, precision=lax.Precision.HIGHEST)

time: 398 us -> 321 us (0.81)
  waiting for transfers between devices: 65.6 us -> 15.4 us
  starting transfers between devices: 43.9 us -> 17.1 us
  Pallas kernels: 230 us -> 253 us
  local copies, waits for them, and re-layouts: 35.1 us -> 20.1 us
  other arithmetic: 12.5 us -> 5.77 us
    ppermute x25 -> x7, waiting for transfers between devices: 65.6 us -> 15.4 us  [send(): return lax.ppermute(x, BOTH, order)]
    ppermute x25 -> x7, starting transfers between devices: 43.9 us -> 17.1 us  [send(): return lax.ppermute(x, BOTH, order)]
    pallas_call x5 -> x2, Pallas kernels: 154 us -> 177 us  [the longest x1 111 us: back(): pl.pallas_call(functools.partial(back_kernel, pieces=pieces, parts=parts)...]
    unnamed x54 -> x44, local copies, waits for them, and re-layouts: 8.81 us -> 4.18 us
    slice x5 -> x0, local copies, waits for them, and re-layouts: 4.09 us -> none  [the longest x1 1.71 us: per_device(): far_key, far_value = ([far[0, 0], far[0, 1]], [far[1, 0], far[1, 1]])]
  transfers between devices with their start and end apart: 25 -> 7, of which waited for: 13 -> 1; matrix products, arithmetic and copies ran while one was open for 6% -> 3% of each run, Pallas kernels for 9% -> 11%
where the time goes in v3:
time: 321 us; the launch traced here: 317 us
  Pallas kernels  253 us (79%)
  local copies, waits for them, and re-layouts  20.1 us (6%)
  starting transfers between devices  17.1 us (5%)
  waiting for transfers between devices  15.4 us (5%)
  other arithmetic  5.77 us (2%)
  between operations  3.79 us (1%)
    pallas_call x1, Pallas kernels, back(): pl.pallas_call(functools.partial(back_kernel, pieces=pieces, parts=parts)...  111 us
    pallas_call x1, Pallas kernels, tail(): pl.pallas_call(functools.partial(tail_kernel, total_tokens=total_tokens,...  66.3 us
    pallas_call x1, Pallas kernels, feed(): pl.pallas_call(feed_kernel, grid=(2,), in_specs=[rows(block, width), whol...  34.7 us
    pallas_call x1, Pallas kernels, attend(): pl.pallas_call(functools.partial(attend_kernel, pieces=pieces), grid=(pai...  30.2 us
    ppermute x7, starting transfers between devices, send(): return lax.ppermute(x, BOTH, order)  17.1 us
    ppermute x7, waiting for transfers between devices, send(): return lax.ppermute(x, BOTH, order)  15.4 us
    pallas_call x2, Pallas kernels, project(): pl.pallas_call(project_kernel, grid=(count // block,), in_specs=[rows(blo...  11.4 us
  transfers between devices with their start and end apart: 7, of which 1 were waited for; matrix products, arithmetic and copies ran while one was open for 3% of the time, Pallas kernels for 11%

profile of v3, /device:TPU:0, one launch (start us, length us, event | category | flops | bytes accessed | tf_op | source)
XLA Modules:
  0.0 316.9 jit_solution(4919252527243670720)
XLA Ops:
  0.8 2.8 dynamic-slice_bitcast_fusion.2
  3.5 7.4 %collective-permute-start.2 = (bf16[512,768]{1,0:T(8,128)(2,1)}, bf16[512,768]{1,0:T(8,128)(2,1)}, u32[]{:S(2)}, u32[]{:S(2)}) collective-permute-start(bf16[512,768]{1,0:T(8,128)(2,1)} %get-tuple-element.76), channel_id=1, source_target_pairs={{0,0},{1,1},{2,4},{3,5},{4,2},{5,3},{6,6},{7,7},{8,8},{9,9},{10,12... | collective-permute-start | bytes 2359304 | tf_op jit(solution)/shard_map/ppermute | solution.py:1132
  10.9 3.0 collective-permute-start
  14.0 0.6 reshape.119.gain_ref
  14.6 0.6 reshape.121.bias_ref
  15.2 0.6 reshape.120.shift_ref
  15.8 0.6 dynamic_slice.27
  18.3 0.6 constant_dynamic-slice_fusion.1.time_ref
  18.9 5.7 %project.2 = (bf16[1024,768]{1,0:T(8,128)(2,1)}, bf16[1024,768]{1,0:T(8,128)(2,1)}, bf16[512,1536]{1,0:T(8,128)(2,1)}) custom-call(bf16[512,768]{1,0:T(8,128)(2,1)} %collective-permute-done.2.x_ref.x0_ref.x0, bf16[1,768]{1,0:T(2,128)(2,1)} %constant_dynamic-slice_fusion.1.time_ref, bf16[1,768]{1,0:T(2,128)(2,1)} %reshape.119.gain_ref, ...), custom_call_target="tpu_custom_call" | custom-call | flops 5750000128 | tf_op jit(solution)/shard_map/project/pallas_call | solution.py:91
  24.6 15.4 %collective-permute-done.x_ref.x1_ref.x1 = bf16[512,768]{1,0:T(8,128)(2,1)} collective-permute-done((bf16[512,768]{1,0:T(8,128)(2,1)}, bf16[512,768]{1,0:T(8,128)(2,1)}, u32[]{:S(2)}, u32[]{:S(2)}) %collective-permute-start) | collective-permute-done | bytes 786464 | tf_op jit(solution)/shard_map/ppermute | solution.py:1132
  40.0 5.8 %project.3 = (bf16[1024,768]{1,0:T(8,128)(2,1)}, bf16[1024,768]{1,0:T(8,128)(2,1)}, bf16[512,1536]{1,0:T(8,128)(2,1)}) custom-call(bf16[512,768]{1,0:T(8,128)(2,1)} %collective-permute-done.x_ref.x1_ref.x1, bf16[1,768]{1,0:T(2,128)(2,1)} %constant_dynamic-slice_fusion.1.time_ref, ...), custom_call_target="tpu_custom_call", output_to_operand_aliasing={{0}: (6, {}), {1}: (7, {})} | custom-call | flops 5750000128 | tf_op jit(solution)/shard_map/project/pallas_call | solution.py:91
  45.8 0.5 collective-permute-start.3
  46.4 0.1 dynamic-slice_bitcast_fusion
  46.5 0.9 collective-permute-start.5
  47.4 5.2 %collective-permute-start.6 = (bf16[512,768]{1,0:T(8,128)(2,1)S(1)}, bf16[512,768]{1,0:T(8,128)(2,1)}, u32[]{:S(2)}, u32[]{:S(2)}) collective-permute-start(bf16[512,768]{1,0:T(8,128)(2,1)S(1)} %get-tuple-element.74), channel_id=1, source_target_pairs={{0,1},{1,0},{2,5},{3,4},{4,3},{5,2},{6,7},{7,6},{8,9},{9,8},{10,13... | collective-permute-start | bytes 2359304 | tf_op jit(solution)/shard_map/ppermute | solution.py:1132
  52.6 0.6 reshape.125.up_bias_ref
  53.2 0.6 reshape.122.out_bias_ref
  53.8 0.6 reshape.123.gain_ref
  54.4 0.6 reshape.124.shift_ref
  55.0 0.6 reshape.126.down_bias_ref
  55.6 0.1 pad.3.clone
  55.6 0.6 iota_add_fusion
  56.9 0.7 fusion.5
  57.6 0.7 maximum_maximum_fusion.marks_ref
  58.3 30.2 %attend.1 = (bf16[1024,768]{1,0:T(8,128)(2,1)}, f32[1024,768]{1,0:T(8,128)}) custom-call(bf16[1024,768]{1,0:T(8,128)(2,1)} %get-tuple-element.48.query_ref, bf16[512,1536]{1,0:T(8,128)(2,1)} %get-tuple-element.49.refs_0_.refs_4_, bf16[512,1536]{1,0:T(8,128)(2,1)} %get-tuple-element.50.refs_1_.refs_5_, ...), custom_call_target="tpu_custom_call" | custom-call | flops 36800000000 | tf_op jit(solution)/shard_map/attend/pallas_call | solution.py:199
  88.5 0.9 copy-done.20
  89.3 34.7 %feed.1 = (bf16[1024,768]{1,0:T(8,128)(2,1)}, bf16[1024,3072]{1,0:T(8,128)(2,1)}, bf16[1024,3072]{1,0:T(8,128)(2,1)}, bf16[1024,768]{1,0:T(8,128)(2,1)}, f32[102...) custom-call(bf16[1024,768]{1,0:T(8,128)(2,1)} %get-tuple-element.51.context_ref.refs_10, ...), custom_call_target="tpu_custom_call" | custom-call | flops 39099998208 | tf_op jit(solution)/shard_map/feed/pallas_call | solution.py:938
  124.0 110.8 %back.1 = (bf16[1024,768]{1,0:T(8,128)(2,1)}, bf16[512,768]{1,0:T(8,128)(2,1)}, bf16[512,768]{1,0:T(8,128)(2,1)}, bf16[512,768]{1,0:T(8,128)(2,1)}, bf16[512,768...) custom-call(bf16[1024,768]{1,0:T(8,128)(2,1)} %get-tuple-element.48., ...), custom_call_target="tpu_custom_call" | custom-call | flops 115000000512 | tf_op jit(solution)/shard_map/back/pallas_call | solution.py:675
  234.9 66.3 %tail.1 = (bf16[2,512,768]{2,1,0:T(8,128)(2,1)}, bf16[3,96,768]{2,1,0:T(8,128)(2,1)}, f32[32,768]{1,0:T(8,128)}) custom-call(bf16[1024,768]{1,0:T(8,128)(2,1)} %get-tuple-element.60.query_grad, bf16[512,768]{1,0:T(8,128)(2,1)} %get-tuple-element.61.key0, bf16[512,768]{1,0:T(8,128)(2,1)} %get-tuple-element.62.key1, ...), custom_call_target="tpu_custom_call" | custom-call | flops 69000003584 | tf_op jit(solution)/shard_map/tail/pallas_call | solution.py:848
  301.2 0.7 convert_bitcast_fusion.1
  301.8 0.8 slice.59
  302.6 0.7 slice.69
  303.4 1.3 slice_bitcast_fusion.2
  304.7 0.1 convert_element_type.50
  304.9 0.1 slice_bitcast_fusion
  304.9 0.7 slice_bitcast_fusion.1
  305.7 0.7 copy-done.4
  306.4 1.9 convert_element_type.48
  308.3 0.1 convert_bitcast_fusion
  308.3 1.0 copy.39
  309.3 1.1 copy.40
  310.5 0.0 copy-done.6
  310.5 1.1 bitcast_convert_fusion
  311.6 1.4 fusion
  313.0 0.7 dynamic_slice.33
  313.6 0.6 fusion.6
  314.2 1.1 copy.44
  315.4 1.3 copy-done.1
  (55 shorter events, 0.2 us)
Async XLA Ops:
  0.7 17.7 %copy-start = (bf16[2048,768]{1,0:T(8,128)(2,1)S(1)}, bf16[2048,768]{1,0:T(8,128)(2,1)}, u32[]{:S(2)}) copy-start(bf16[2048,768]{1,0:T(8,128)(2,1)} %param.19) | copy-start | bytes 9437188
  0.7 10.2 %copy-start.19 = (s32[2]{0:T(128)S(1)}, s32[2]{0:T(128)}, u32[]{:S(2)}) copy-start(s32[2]{0:T(128)} %param.18) | copy-start | bytes 28
  0.7 13.3 %copy-start.12 = (bf16[768]{0:T(1024)(128)(2,1)S(1)}, bf16[768]{0:T(1024)(128)(2,1)}, u32[]{:S(2)}) copy-start(bf16[768]{0:T(1024)(128)(2,1)} %param.20) | copy-start | bytes 4612
  0.7 13.8 %copy-start.10 = (bf16[768]{0:T(1024)(128)(2,1)S(1)}, bf16[768]{0:T(1024)(128)(2,1)}, u32[]{:S(2)}) copy-start(bf16[768]{0:T(1024)(128)(2,1)} %param.23) | copy-start | bytes 4612
  0.7 13.8 %copy-start.11 = (bf16[768]{0:T(1024)(128)(2,1)S(1)}, bf16[768]{0:T(1024)(128)(2,1)}, u32[]{:S(2)}) copy-start(bf16[768]{0:T(1024)(128)(2,1)} %param.24) | copy-start | bytes 4612
  0.7 14.5 %copy-start.13 = (bf16[768]{0:T(1024)(128)(2,1)S(1)}, bf16[768]{0:T(1024)(128)(2,1)}, u32[]{:S(2)}) copy-start(bf16[768]{0:T(1024)(128)(2,1)} %param.21) | copy-start | bytes 4612
  3.5 15.4 %collective-permute-start.2 = (bf16[512,768]{1,0:T(8,128)(2,1)}, bf16[512,768]{1,0:T(8,128)(2,1)}, u32[]{:S(2)}, u32[]{:S(2)}) collective-permute-start(bf16[512,768]{1,0:T(8,128)(2,1)} %get-tuple-element.76), channel_id=1, source_target_pairs={{0,0},{1,1},{2,4},{3,5},{4,2},{5,3},{6,6},{7,7},{8,8},{9,9},{10,12... | collective-permute-start | bytes 2359304 | tf_op jit(solution)/shard_map/ppermute | solution.py:1132
  10.9 4.9 %collective-permute-start.1 = (s32[2]{0:T(128)S(1)}, s32[2]{0:T(128)S(1)}, u32[]{:S(2)}, u32[]{:S(2)}) collective-permute-start(s32[2]{0:T(128)S(1)} %copy-done.19), channel_id=1, source_target_pairs={{0,4},{1,5},{2,6},{3,7},{4,0},{5,1},{6,2},{7,3},{8,12},{9,13},{10,... | collective-permute-start | bytes 32 | tf_op jit(solution)/shard_map/ppermute | solution.py:1132
  10.9 29.0 %collective-permute-start = (bf16[512,768]{1,0:T(8,128)(2,1)}, bf16[512,768]{1,0:T(8,128)(2,1)}, u32[]{:S(2)}, u32[]{:S(2)}) collective-permute-start(bf16[512,768]{1,0:T(8,128)(2,1)} %get-tuple-element.77), channel_id=1, source_target_pairs={{0,1},{1,0},{2,5},{3,4},{4,3},{5,2},{6,7},{7,6},{8,9},{9,8},{10,13... | collective-permute-start | bytes 2359304 | tf_op jit(solution)/shard_map/ppermute | solution.py:1132
  40.0 6.4 %copy-start.2 = (bf16[2,512,768]{2,1,0:T(8,128)(2,1)S(1)}, bf16[2,512,768]{2,1,0:T(8,128)(2,1)}, u32[]{:S(2)}) copy-start(bf16[2,512,768]{2,1,0:T(8,128)(2,1)} %param.33) | copy-start | bytes 4718596
  45.8 12.5 %collective-permute-start.4 = (bf16[512,1536]{1,0:T(8,128)(2,1)}, bf16[512,1536]{1,0:T(8,128)(2,1)}, u32[]{:S(2)}, u32[]{:S(2)}) collective-permute-start(bf16[512,1536]{1,0:T(8,128)(2,1)} %get-tuple-element.50.refs_1_.refs_5_), channel_id=1, source_target_pairs={{0,4},{1,5},{2,6},{3,7},{4,0},{5,1},{6,2},{7,3},{8,12},{9,13},{10,... | collective-permute-start | bytes 4718600 | tf_op jit(solution)/shard_map/ppermute | solution.py:1132
  45.8 6.8 %copy-start.9 = (bf16[3072]{0:T(1024)(128)(2,1)S(1)}, bf16[3072]{0:T(1024)(128)(2,1)}, u32[]{:S(2)}) copy-start(bf16[3072]{0:T(1024)(128)(2,1)} %param.30) | copy-start | bytes 18436
  45.8 7.4 %copy-start.14 = (bf16[768]{0:T(1024)(128)(2,1)S(1)}, bf16[768]{0:T(1024)(128)(2,1)}, u32[]{:S(2)}) copy-start(bf16[768]{0:T(1024)(128)(2,1)} %param.26) | copy-start | bytes 4612
  45.8 8.0 %copy-start.15 = (bf16[768]{0:T(1024)(128)(2,1)S(1)}, bf16[768]{0:T(1024)(128)(2,1)}, u32[]{:S(2)}) copy-start(bf16[768]{0:T(1024)(128)(2,1)} %param.27) | copy-start | bytes 4612
  45.8 8.6 %copy-start.16 = (bf16[768]{0:T(1024)(128)(2,1)S(1)}, bf16[768]{0:T(1024)(128)(2,1)}, u32[]{:S(2)}) copy-start(bf16[768]{0:T(1024)(128)(2,1)} %param.28) | copy-start | bytes 4612
  45.8 9.2 %copy-start.17 = (bf16[768]{0:T(1024)(128)(2,1)S(1)}, bf16[768]{0:T(1024)(128)(2,1)}, u32[]{:S(2)}) copy-start(bf16[768]{0:T(1024)(128)(2,1)} %param.32) | copy-start | bytes 4612
  45.8 12.4 %collective-permute-start.3 = (bf16[512,1536]{1,0:T(8,128)(2,1)}, bf16[512,1536]{1,0:T(8,128)(2,1)}, u32[]{:S(2)}, u32[]{:S(2)}) collective-permute-start(bf16[512,1536]{1,0:T(8,128)(2,1)} %get-tuple-element.49.refs_0_.refs_4_), channel_id=1, source_target_pairs={{0,4},{1,5},{2,6},{3,7},{4,0},{5,1},{6,2},{7,3},{8,12},{9,13},{10,... | collective-permute-start | bytes 4718600 | tf_op jit(solution)/shard_map/ppermute | solution.py:1132
  46.5 42.0 %collective-permute-start.5 = (bf16[512,768]{1,0:T(8,128)(2,1)S(1)}, bf16[512,768]{1,0:T(8,128)(2,1)S(1)}, u32[]{:S(2)}, u32[]{:S(2)}) collective-permute-start(bf16[512,768]{1,0:T(8,128)(2,1)S(1)} %get-tuple-element.75), channel_id=1, source_target_pairs={{0,0},{1,1},{2,4},{3,5},{4,2},{5,3},{6,6},{7,7},{8,8},{9,9},{10,12... | collective-permute-start | bytes 2359304 | tf_op jit(solution)/shard_map/ppermute | solution.py:1132
  47.4 41.1 %collective-permute-start.6 = (bf16[512,768]{1,0:T(8,128)(2,1)S(1)}, bf16[512,768]{1,0:T(8,128)(2,1)}, u32[]{:S(2)}, u32[]{:S(2)}) collective-permute-start(bf16[512,768]{1,0:T(8,128)(2,1)S(1)} %get-tuple-element.74), channel_id=1, source_target_pairs={{0,1},{1,0},{2,5},{3,4},{4,3},{5,2},{6,7},{7,6},{8,9},{9,8},{10,13... | collective-permute-start | bytes 2359304 | tf_op jit(solution)/shard_map/ppermute | solution.py:1132
  88.5 0.9 copy-start.20
  234.9 69.8 %copy-start.5 = (bf16[5,96,768]{2,1,0:T(8,128)(2,1)S(1)}, bf16[5,96,768]{2,1,0:T(8,128)(2,1)}, u32[]{:S(2)}) copy-start(bf16[5,96,768]{2,1,0:T(8,128)(2,1)} %get-tuple-element.72) | copy-start | bytes 2211844
  304.8 1.5 copy-start.4
  306.4 1.9 copy-start.7
  309.3 1.2 copy-start.6
  309.3 2.2 copy-start.8
  309.3 2.3 copy-start.18
  310.4 3.8 %copy-start.3 = (bf16[2,512,768]{2,1,0:T(8,128)(2,1)S(1)}, bf16[2,512,768]{2,1,0:T(8,128)(2,1)}, u32[]{:S(2)}) copy-start(bf16[2,512,768]{2,1,0:T(8,128)(2,1)} %get-tuple-element.106) | copy-start | bytes 4718596
  314.2 2.5 copy-start.1

commit v4 on v3

--- a/solution.py
+++ b/solution.py
@@ -14,6 +14,8 @@
 LANES = 128
 VMEM_BYTES = 56 * 1024 * 1024
 BOTH = ("dp", "seq")
+TOKEN_PARTS = 8
+TOKENS_AHEAD = 6
 F32 = jnp.float32
 BF16 = jnp.bfloat16
 NN = (((1,), (0,)), ((), ()))
@@ -68,22 +70,62 @@
     )
 
 
-def project_kernel(x_ref, time_ref, gain_ref, shift_ref, weight_ref, bias_ref, *refs):
+TIME, MARK, SHARE, STEP = range(4)
+
+
+def one_row(ref, at):
+    return ref[at : at + 1].astype(F32)
+
+
+def vector(ref):
+    return ref[...].astype(F32).reshape(1, -1)
+
+
+def whole_vector(v):
+    return pl.BlockSpec(v.shape, lambda *i: (0,), pipeline_mode=pl.Buffered(1))
+
+
+def known_rows(step, sequence, share, time_row):
+    lane = lax.broadcasted_iota(jnp.int32, time_row.shape, 1)
+    bucket = step * BUCKETS // TSTEPS
+    return jnp.concatenate(
+        [
+            time_row,
+            jnp.where(lane == bucket, 1.0, 0.0),
+            jnp.where(lane == BUCKETS + bucket, share, 0.0),
+            jnp.where(lane == sequence, step.astype(F32), 0.0),
+        ],
+        0,
+    )
+
+
+def project_rows(x, info_ref, small, weight_ref):
+    width = x.shape[1]
+    gain, shift, query_bias, value_bias = small
+    unit, _ = norm_parts(x.astype(F32) + one_row(info_ref, TIME))
+    normed = (unit * vector(gain) + vector(shift)).astype(BF16)
+
+    def part(number):
+        made = dot(normed, weight_ref[:, number * width : (number + 1) * width], NN)
+        if number != 1:
+            made = made + vector(query_bias if number == 0 else value_bias)
+        made = made.astype(BF16)
+        return made * jnp.asarray(HEAD_DIM ** (-0.5), BF16) if number == 0 else made
+
+    return normed, part
+
+
+def project_kernel(x_ref, info_ref, weight_ref, *refs):
     normed_ref, query_ref, kv_ref = refs[-3:]
     width = x_ref.shape[1]
-    unit, _ = norm_parts(wide(x_ref) + wide(time_ref))
-    normed = (unit * wide(gain_ref) + wide(shift_ref)).astype(BF16)
+    normed, part = project_rows(x_ref[...], info_ref, refs[:4], weight_ref)
     normed_ref[...] = normed
-    for part in range(3):
-        columns = slice(part * width, (part + 1) * width)
-        made = (dot(normed, weight_ref[:, columns], NN) + bias_ref[:, columns]).astype(BF16)
-        if part == 0:
-            query_ref[...] = made * jnp.asarray(HEAD_DIM ** (-0.5), BF16)
-        else:
-            kv_ref[:, (part - 1) * width : part * width] = made
-
-
-def project(x, time_row, gain, shift, weight, bias, total, begun=None, block=256):
+    query_ref[...] = part(0)
+    kv_ref[:, :width] = part(1)
+    kv_ref[:, width:] = part(2)
+
+
+def project(x, info, small, weight, total, begun=None, block=256):
     count, width = x.shape
     first = 0 if begun is None else total // block - count // block
     later = pl.BlockSpec((block, width), lambda i: (i + first, 0))
@@ -91,14 +133,8 @@
     return pl.pallas_call(
         project_kernel,
         grid=(count // block,),
-        in_specs=[
-            rows(block, width),
-            fixed((1, width)),
-            fixed((1, width)),
-            fixed((1, width)),
-            fixed(weight.shape),
-            fixed(bias.shape),
-        ]
+        in_specs=[rows(block, width), fixed(info.shape), fixed(weight.shape)]
+        + [whole_vector(v) for v in small]
         + [pl.BlockSpec(memory_space=pl.ANY)] * len(extra),
         out_specs=[later, later, rows(block, 2 * width)],
         out_shape=[
@@ -106,11 +142,11 @@
             shape_of((total, width)),
             shape_of((count, 2 * width)),
         ],
-        input_output_aliases={6: 0, 7: 1} if extra else {},
+        input_output_aliases={7: 0, 8: 1} if extra else {},
         compiler_params=params(),
         cost_estimate=cost(5),
         name="project",
-    )(x, time_row, gain, shift, weight, bias, *extra)
+    )(x, info, weight, *small, *extra)
 
 
 def lane_parts():
@@ -429,83 +465,191 @@
             copy.wait()
 
 
-class Return:
-    def __init__(self, out, sends, receives, local):
+class Trade:
+    def __init__(self, out, sends, receives, local, gather=False, parts=1):
         self.out, self.sends, self.receives, self.local = out, sends, receives, local
-
-    def targets(self):
+        self.gather, self.parts = gather, parts
+
+    @staticmethod
+    def semaphores(parts=1):
+        return [pltpu.SemaphoreType.DMA((2, parts)), pltpu.SemaphoreType.DMA((2, parts)), pltpu.SemaphoreType.DMA((parts,))]
+
+    def device(self, p):
         d, z, _, _, core = here()
-        return [(d - core + z // 2, 2 * core + (z + p) % 2) for p in range(2)]
-
-    def sources(self):
-        d, z, _, _, core = here()
-        return [(d - core + z // 2, 2 * core + j) for j in range(2)]
+        return (d - core + z // 2, 2 * core + (z + p) % 2)
 
     def stays(self):
         _, z, _, _, core = here()
         return z // 2 == core
 
+    def slot(self, p):
+        return p if self.gather else lax.axis_index("seq") % 2
+
+    def own_slot(self, p):
+        return p if self.gather else (lax.axis_index("seq") + p) % 2
+
     def greet(self, barrier):
-        _, z, _, _, _ = here()
-        for j, source in enumerate(self.sources()):
-
-            @pl.when(jnp.logical_not(self.stays() & (z % 2 == j)))
-            def _():
-                pl.semaphore_signal(barrier, inc=1, device_id=source, device_id_type=pl.DeviceIdType.MESH)
-
-        return jnp.where(self.stays(), 1, 2)
-
-    def keep(self, block):
-        z = lax.axis_index("seq")
-        return pltpu.make_async_copy(block, self.out.at[z % 2], self.local.at[0])
-
-    def copy(self, p, block):
-        z = lax.axis_index("seq")
-        return remote(block, self.out.at[z % 2], self.sends, self.receives, p, z % 2, self.targets()[p])
-
-    def begin(self, p, block):
-        if p == 1:
-            self.copy(1, block).start()
-            return
-
-        @pl.when(self.stays())
-        def _():
-            self.keep(block).start()
-
         @pl.when(jnp.logical_not(self.stays()))
         def _():
-            self.copy(0, block).start()
-
-    def finish(self, blocks):
-        z = lax.axis_index("seq")
-        self.copy(1, blocks[1]).wait_send()
-
-        @pl.when(self.stays())
-        def _():
-            self.keep(blocks[0]).wait()
-
-        @pl.when(jnp.logical_not(self.stays()))
-        def _():
-            self.copy(0, blocks[0]).wait_send()
-
-        for j in range(2):
-
-            @pl.when(jnp.logical_not(self.stays() & (z % 2 == j)))
-            def _():
-                remote(
-                    blocks[0], self.out.at[j], self.sends, self.receives, 0, j, self.sources()[j]
-                ).wait_recv()
-
-
-def meet(names, *returns):
+            pl.semaphore_signal(barrier, inc=1, device_id=self.device(0), device_id_type=pl.DeviceIdType.MESH)
+
+        pl.semaphore_signal(barrier, inc=1, device_id=self.device(1), device_id_type=pl.DeviceIdType.MESH)
+        return jnp.where(self.stays(), 1, 2)
+
+    def rows(self, ref, part):
+        many = ref.shape[0] // self.parts
+        return ref.at[pl.ds(part * many, many)]
+
+    def keep(self, block, part):
+        return pltpu.make_async_copy(
+            self.rows(block, part), self.rows(self.out.at[self.own_slot(0)], part), self.local.at[part]
+        )
+
+    def copy(self, p, block, part):
+        slot = self.slot(p)
+        return pltpu.make_async_remote_copy(
+            src_ref=self.rows(block, part),
+            dst_ref=self.rows(self.out.at[slot], part),
+            send_sem=self.sends.at[p, part],
+            recv_sem=self.receives.at[slot, part],
+            device_id=self.device(p),
+            device_id_type=pl.DeviceIdType.MESH,
+        )
+
+    def each(self, p, far, near):
+        if p == 1:
+            far()
+            return
+        pl.when(jnp.logical_not(self.stays()))(far)
+        pl.when(self.stays())(near)
+
+    def begin(self, p, block, part=0):
+        self.each(p, lambda: self.copy(p, block, part).start(), lambda: self.keep(block, part).start())
+
+    def sent(self, p, block, part=0):
+        self.each(p, lambda: self.copy(p, block, part).wait_send(), lambda: None)
+
+    def arrived(self, p, block, part=0):
+        slot = self.own_slot(p)
+        target = self.rows(self.out.at[slot], part)
+
+        def far():
+            pltpu.make_async_remote_copy(
+                src_ref=target,
+                dst_ref=target,
+                send_sem=self.sends.at[p, part],
+                recv_sem=self.receives.at[slot, part],
+                device_id=self.device(p),
+                device_id_type=pl.DeviceIdType.MESH,
+            ).wait_recv()
+
+        self.each(p, far, lambda: self.keep(block, part).wait())
+
+
+def meet(names, *trades):
     barrier = pltpu.get_barrier_semaphore()
     to = partners()
     for name in names:
         pl.semaphore_signal(barrier, inc=1, device_id=to[name], device_id_type=pl.DeviceIdType.MESH)
     expected = len(names)
-    for one in returns:
+    for one in trades:
         expected = expected + one.greet(barrier)
     pl.semaphore_wait(barrier, expected)
+
+
+def front_kernel(
+    tokens, weight, table, steps_ref, gain, shift, query_bias, value_bias,
+    x0_out, x1_out, normed_out, query_out, near0_out, near1_out, far0_out, far1_out, info_out,
+    x_v, weight_v, table_v, info_here, info_in, normed_v, query_v, near_v, far_v,
+    load, stores, info_sends, info_receives, sends, receives, *trade, share,
+):
+    d, z, _, _, core = here()
+    block, width = x_v.shape[1:]
+    small = (gain, shift, query_bias, value_bias)
+    trade = Trade(x_v, *trade, gather=True)
+    loaded = pltpu.make_async_copy(weight, weight_v, load.at[0])
+    looked_up = pltpu.make_async_copy(table, table_v, load.at[1])
+    meet(("core",), trade)
+    held = [tokens.at[(z + p) % 2] for p in range(2)]
+    for p in range(2):
+        trade.begin(p, held[p])
+    looked_up.start()
+    loaded.start()
+    steps = [steps_ref[j] for j in range(2)]
+    row = lax.broadcasted_iota(jnp.int32, (16, table.shape[0]), 0)
+    place = lax.broadcasted_iota(jnp.int32, (16, table.shape[0]), 1)
+    wanted = jnp.where(row == 0, steps[0], jnp.where(row == 1, steps[1], -1))
+    chosen = jnp.where(place == wanted, 1.0, 0.0).astype(BF16)
+    looked_up.wait()
+    time_rows = dot(chosen, table_v[...], NN)
+    for j in range(2):
+        info_here[4 * j : 4 * j + 4] = known_rows(steps[j], 2 * d + j, share, time_rows[j : j + 1])
+    known = remote(info_here, info_in, info_sends, info_receives, 0, 0, partners()["core"])
+    known.start()
+    known.wait()
+    mine = jnp.where(z // 2 == core, info_here[...], info_in[...])
+    info_out[0:4] = jnp.where(z % 2 == 0, mine[0:4], mine[4:8])
+    info_out[4:8] = jnp.zeros_like(info_in[4:8])
+    loaded.wait()
+    copies, moved = [], []
+    for p in range(2):
+        trade.arrived(p, held[p])
+        normed, part = project_rows(x_v[p], info_out, small, weight_v)
+        near_v[p, :, :width] = part(1)
+        near_v[p, :, width:] = part(2)
+        moved.append(remote(near_v.at[p], far_v.at[p], sends, receives, p, p, partners()["core"]))
+        moved[p].start()
+        normed_v[p] = normed
+        query_v[p] = part(0)
+        outs = (x0_out, x1_out)[p], (near0_out, near1_out)[p]
+        here_rows = pl.ds(p * block, block)
+        for number, (source, target) in enumerate(
+            (
+                (x_v.at[p], outs[0]), (normed_v.at[p], normed_out.at[here_rows]),
+                (query_v.at[p], query_out.at[here_rows]), (near_v.at[p], outs[1]),
+            )
+        ):
+            copies.append(pltpu.make_async_copy(source, target, stores.at[p, number]))
+            copies[-1].start()
+    for p in range(2):
+        moved[p].wait()
+        copies.append(pltpu.make_async_copy(far_v.at[p], (far0_out, far1_out)[p], stores.at[p, 4]))
+        copies[-1].start()
+    for p in range(2):
+        trade.sent(p, held[p])
+    for copy in copies:
+        copy.wait()
+
+
+def front(tokens, weight, table, steps, small, share):
+    _, block, width = tokens.shape
+    info_shape = (8, width)
+    any_spec = pl.BlockSpec(memory_space=pl.ANY)
+    inside = pl.BlockSpec(memory_space=pltpu.VMEM)
+    pair = pltpu.VMEM((2, block, width), BF16)
+    wide_pair = pltpu.VMEM((2, block, 2 * width), BF16)
+    one = pltpu.SemaphoreType.DMA((1,))
+    two = pltpu.SemaphoreType.DMA((2,))
+    return pl.pallas_call(
+        functools.partial(front_kernel, share=share),
+        in_specs=[any_spec] * 3 + [pl.BlockSpec(memory_space=pltpu.SMEM)] + [inside] * 4,
+        out_specs=[any_spec] * 8 + [inside],
+        out_shape=[shape_of((block, width))] * 2
+        + [shape_of((2 * block, width))] * 2
+        + [shape_of((block, 2 * width))] * 4
+        + [shape_of(info_shape, F32)],
+        scratch_shapes=[
+            pair, pltpu.VMEM(weight.shape, BF16), pltpu.VMEM(table.shape, BF16), pltpu.VMEM(info_shape, F32),
+            pltpu.VMEM(info_shape, F32), pair, pair, wide_pair, wide_pair,
+            two, pltpu.SemaphoreType.DMA((2, 5)), one, one, two, two,
+        ]
+        + Trade.semaphores(),
+        compiler_params=pltpu.CompilerParams(
+            vmem_limit_bytes=VMEM_BYTES, collective_id=2, has_side_effects=True
+        ),
+        cost_estimate=cost(48),
+        name="front",
+    )(tokens, weight, table, steps, *small)
 
 
 def fixed_any():
@@ -537,8 +681,8 @@
             here_parts = pl.ds(at, many)
             chunks.append(Reduction(up_parts.at[here_parts], up_out.at[here_parts], scratch))
     one, two, three, four = chunks
-    far_grads, far_sends, far_receives, layer_sends, layer_receives, layer_local = refs[38:]
-    back = Return(layer_out, layer_sends, layer_receives, layer_local)
+    far_grads, far_sends, far_receives = refs[38:41]
+    back = Trade(layer_out, *refs[41:])
     block = key_refs[0].shape[0]
     layer_blocks = [layer_ref.at[pl.ds(p * block, block)] for p in range(2)]
     step = pl.program_id(0)
@@ -644,7 +788,9 @@
             return carry
 
         lax.fori_loop(0, last + 1 - made, received, 0)
-        back.finish(layer_blocks)
+        for p in range(2):
+            back.sent(p, layer_blocks[p])
+            back.arrived(p, layer_blocks[p])
         for chunk in chunks:
             chunk.finish()
 
@@ -703,10 +849,8 @@
             pltpu.VMEM((2, near * length, LANES), BF16),
             pltpu.SemaphoreType.DMA((1,)),
             pltpu.SemaphoreType.DMA((pairs,)),
-            pltpu.SemaphoreType.DMA((2,)),
-            pltpu.SemaphoreType.DMA((2,)),
-            pltpu.SemaphoreType.DMA((1,)),
-        ],
+        ]
+        + Trade.semaphores(),
         compiler_params=pltpu.CompilerParams(
             vmem_limit_bytes=VMEM_BYTES, collective_id=0, has_side_effects=True
         ),
@@ -719,7 +863,7 @@
 
 def tail_kernel(
     query_grad, key0, key1, value0, value1, far, normed, x0, x1, middle_grad, weight,
-    time_ref, gain_ref, feed_ref, marks_ref,
+    info_ref, gain_ref, feed_ref,
     tokens_out, qkv_out, sums_ref,
     query_v, near_v, far_v, normed_v, x_v, middle_v, weight_v, key_v, value_v, token_v,
     query_parts, key_parts, value_parts, *refs, total_tokens, parts,
@@ -728,8 +872,8 @@
     for number, made in enumerate((query_parts, key_parts, value_parts)):
         reductions.append(Reduction(made, qkv_out.at[pl.ds(number, 1)], refs[9 * number : 9 * number + 9]))
     of_query, of_key, of_value = reductions
-    sums_in, sums_sends, sums_receives, loads, back_sends, back_receives, back_local = refs[27:]
-    back = Return(tokens_out, back_sends, back_receives, back_local)
+    sums_in, sums_sends, sums_receives, loads = refs[27:31]
+    back = Trade(tokens_out, *refs[31:], parts=TOKEN_PARTS)
     block, width = x0.shape
     pairs = width // LANES
     d, z, _, _, core = here()
@@ -760,10 +904,9 @@
         for part, grads in enumerate((query_v, key_v, value_v)):
             columns = slice(part * width, (part + 1) * width)
             normed_grad = normed_grad + dot(grads[held], weight_v[:, columns], NT)
-        unit, scale = norm_parts(x_v[p].astype(F32) + wide(time_ref))
-        token_grad = middle_v[held] + norm_backward(normed_grad, wide(gain_ref), unit, scale)
+        unit, scale = norm_parts(x_v[p].astype(F32) + one_row(info_ref, TIME))
+        token_grad = middle_v[held] + norm_backward(normed_grad, vector(gain_ref), unit, scale)
         token_v[p] = token_grad.astype(BF16)
-        back.begin(p, token_v.at[p])
         return [
             column_sum(normed_grad * unit),
             column_sum(normed_grad),
@@ -782,18 +925,21 @@
         if number < 4:
             sums_copy(number + 1).start()
 
-    copies[0].wait()
-    copies[1].wait()
-    product(query_v, query_parts)
-    of_query.to_cores()
-    for copy in copies[2:8]:
+    def move(number):
+        if number >= TOKENS_AHEAD:
+            p, part = divmod(number - TOKENS_AHEAD, TOKEN_PARTS)
+            back.sent(p, token_v.at[p], part)
+        p, part = divmod(number, TOKEN_PARTS)
+        back.begin(p, token_v.at[p], part)
+
+    for copy in copies[1:8]:
         copy.wait()
     first = start_block(0)
-    of_query.to_first()
+    for number in range(4):
+        move(number)
     for copy in copies[8:]:
         copy.wait()
     second = start_block(1)
-    of_query.to_second()
     sums = [a + b for a, b in zip(first, second)]
     sums_ref[...] = jnp.zeros_like(sums_ref)
     sums_ref[0:4] = feed_ref[0:4]
@@ -801,42 +947,65 @@
     for number in range(4):
         sums_ref[4 + parts + number : 5 + parts + number] = sums[number]
     energy = jnp.sum(feed_ref[4:5], keepdims=True) / (width * total_tokens)
-    sums_ref[8 + parts : 9 + parts] = marks_ref[0:1] * energy + marks_ref[1:2]
-    sums_ref[9 + parts : 10 + parts] = marks_ref[2:3]
+    sums_ref[8 + parts : 9 + parts] = info_ref[MARK : MARK + 1] * energy + info_ref[SHARE : SHARE + 1]
+    sums_ref[9 + parts : 10 + parts] = info_ref[STEP : STEP + 1] * jnp.where(core == 0, 1.0, 0.0)
     sequence = (d - core + z // 2) * 2 + z % 2
     sums_ref[pl.ds(16 + sequence, 1)] = sums[4]
     sums_copy(0).start()
+    move(4)
+    move(5)
+    copies[0].wait()
+    product(query_v, query_parts)
+    of_query.to_cores()
+    move(6)
     product(key_v, key_parts)
     of_key.to_cores()
     sums_next(0)
+    move(7)
+    of_query.to_first()
     product(value_v, value_parts)
     of_value.to_cores()
+    sums_next(1)
+    move(8)
+    of_key.to_first()
+    move(9)
+    of_query.to_second()
+    sums_next(2)
+    move(10)
+    of_value.to_first()
+    move(11)
+    of_key.to_second()
     of_query.to_near()
-    of_key.to_first()
-    sums_next(1)
+    sums_next(3)
+    move(12)
     of_query.to_far()
-    of_value.to_first()
-    sums_next(2)
-    of_key.to_second()
-    sums_next(3)
     of_value.to_second()
+    sums_next(4)
+    of_key.to_near()
+    move(13)
+    of_key.to_far()
+    of_value.to_near()
+    move(14)
     of_query.to_other()
-    of_key.to_near()
-    sums_next(4)
-    of_value.to_near()
-    of_key.to_far()
+    of_value.to_far()
+    move(15)
+    of_key.to_other()
     of_query.to_out()
-    of_value.to_far()
-    of_key.to_other()
     of_value.to_other()
     of_key.to_out()
     of_value.to_out()
-    back.finish([token_v.at[0], token_v.at[1]])
+    total = 2 * TOKEN_PARTS
+    for number in range(total - TOKENS_AHEAD, total):
+        p, part = divmod(number, TOKEN_PARTS)
+        back.sent(p, token_v.at[p], part)
+    for number in range(total):
+        p, part = divmod(number, TOKEN_PARTS)
+        back.arrived(p, token_v.at[p], part)
     for one in reductions:
         one.finish()
 
 
-def tail(query_grad, key_grads, value_grads, far, normed, xs, middle_grad, weight, time_row, gain, feed_sums, marks, total_tokens, hidden_parts):
+def tail(query_grad, key_grads, value_grads, far, normed, xs, middle_grad, weight, info, gain, feed_sums, total_tokens, hidden_parts):
     block, width = xs[0].shape
     count, total_seqs = 2 * block, 16
     any_spec = fixed_any()
@@ -847,7 +1016,7 @@
     sums_shape = (16 + total_seqs, width)
     return pl.pallas_call(
         functools.partial(tail_kernel, total_tokens=total_tokens, parts=hidden_parts),
-        in_specs=[any_spec] * 11 + [inside] * 4,
+        in_specs=[any_spec] * 11 + [inside] * 3,
         out_specs=[any_spec, any_spec, inside],
         out_shape=[
             shape_of((2, block, width)), shape_of((3, up_rows, width)), shape_of(sums_shape, F32),
@@ -863,18 +1032,76 @@
             pltpu.SemaphoreType.DMA((5,)),
             pltpu.SemaphoreType.DMA((5,)),
             pltpu.SemaphoreType.DMA((11,)),
-            pltpu.SemaphoreType.DMA((2,)),
-            pltpu.SemaphoreType.DMA((2,)),
-            pltpu.SemaphoreType.DMA((1,)),
-        ],
+        ]
+        + Trade.semaphores(TOKEN_PARTS),
         compiler_params=pltpu.CompilerParams(
             vmem_limit_bytes=VMEM_BYTES, collective_id=1, has_side_effects=True
         ),
         cost_estimate=cost(60),
         name="tail",
     )(
-        query_grad, *key_grads, *value_grads, far, normed, *xs, middle_grad, weight, time_row, gain, feed_sums, marks
+        query_grad, *key_grads, *value_grads, far, normed, *xs, middle_grad, weight, info, gain, feed_sums
     )
+
+
+def finish_kernel(
+    token_ref, layer_ref, qkv_ref, up_out_ref, out_part_ref, down_ref, sums_ref,
+    token_out, layer_out, qkv_out, up_out, out_out, down_out, table_out, *, total_seqs, steps_row, table_rows,
+):
+    token_out[...] = wide(token_ref)
+    layer_out[...] = layer_ref[...]
+    qkv_out[...] = qkv_ref[0].astype(F32)
+    up_out[...] = up_out_ref[0].astype(F32)
+    out_out[...] = out_part_ref[0].astype(F32)
+    down_out[...] = wide(down_ref)
+    block = table_out.shape[0]
+    first = lax.axis_index("dp") * table_rows + pl.program_id(0) * block
+    place = (lax.broadcasted_iota(jnp.int32, (block, 1), 0) + first).astype(F32)
+    total = jnp.zeros_like(table_out)
+    for s in range(total_seqs):
+        chosen = place == sums_ref[steps_row : steps_row + 1, s : s + 1]
+        total = total + jnp.where(chosen, sums_ref[16 + s : 17 + s], 0.0)
+    table_out[...] = total
+
+
+def finish(token, layer, qkv, up_out, down, sums, table_rows, steps_row):
+    seqs, length, width = token.shape
+    parts, block = up_out.shape[0] - 1, up_out.shape[1]
+    steps = parts
+    rows_at = lambda many: pl.BlockSpec((many // steps, width), lambda i: (i, 0))
+    count = seqs * length
+    wide_rows = rows_at(count)
+    made = pl.pallas_call(
+        functools.partial(
+            finish_kernel, total_seqs=sums.shape[0] - 16, steps_row=steps_row, table_rows=table_rows
+        ),
+        grid=(steps,),
+        in_specs=[
+            wide_rows, wide_rows,
+            pl.BlockSpec((1, block, width), lambda i: (jnp.minimum(i, 2), 0, 0)),
+            pl.BlockSpec((1, block, width), lambda i: (i, 0, 0)),
+            pl.BlockSpec((1, block, width), lambda i: (parts, 0, 0)),
+            rows_at(down.shape[0]),
+            fixed(sums.shape),
+        ],
+        out_specs=[
+            wide_rows, wide_rows,
+            pl.BlockSpec((block, width), lambda i: (0, jnp.minimum(i, 2))),
+            pl.BlockSpec((block, width), lambda i: (0, i)),
+            pl.BlockSpec((block, width), lambda i: (0, 0)),
+            rows_at(down.shape[0]), rows_at(table_rows),
+        ],
+        out_shape=[
+            shape_of((count, width), F32), shape_of((count, width)), shape_of((block, 3 * width), F32),
+            shape_of((block, parts * width), F32), shape_of((block, width), F32), shape_of(down.shape, F32),
+            shape_of((table_rows, width), F32),
+        ],
+        compiler_params=params(),
+        cost_estimate=cost(6),
+        name="finish",
+    )(token.reshape(count, width), layer.reshape(count, width), qkv, up_out, up_out, down, sums)
+    shape = (seqs, length, width)
+    return [made[0].reshape(shape), made[1].reshape(shape)] + list(made[2:])
 
 
 def gelu_parts(hidden):
@@ -884,8 +1111,8 @@
 
 
 def feed_kernel(
-    context_ref, x0_ref, x1_ref, time_ref, cot0_ref, cot1_ref, out_weight_ref, out_bias_ref,
-    gain_ref, shift_ref, up_ref, up_bias_ref, down_ref, down_bias_ref,
+    context_ref, x0_ref, x1_ref, info_ref, cot0_ref, cot1_ref, out_weight_ref, up_ref, down_ref,
+    out_bias_ref, gain_ref, shift_ref, down_bias_ref, up_bias_ref,
     out_ref, active_ref, hidden_grad_ref, normed_ref, middle_grad_ref, branch_ref, context_grad_ref, sums_ref,
 ):
     step = pl.program_id(0)
@@ -897,16 +1124,22 @@
 
     x = jnp.where(step == 0, x0_ref[...], x1_ref[...])
     cot = jnp.where(step == 0, cot0_ref[...], cot1_ref[...])
-    middle = x.astype(F32) + wide(time_ref) + dot(context_ref[...], out_weight_ref[...], NN) + wide(out_bias_ref)
+    middle = (
+        x.astype(F32)
+        + one_row(info_ref, TIME)
+        + dot(context_ref[...], out_weight_ref[...], NN)
+        + vector(out_bias_ref)
+    )
     unit, scale = norm_parts(middle)
-    gain = wide(gain_ref)
-    normed = (unit * gain + wide(shift_ref)).astype(BF16)
+    gain = vector(gain_ref)
+    normed = (unit * gain + vector(shift_ref)).astype(BF16)
     normed_ref[...] = normed
-    out = middle + wide(down_bias_ref)
+    out = middle + vector(down_bias_ref)
     normed_grad = jnp.zeros_like(out)
+    up_bias = vector(up_bias_ref)
     for part in range(hidden_width // width):
         columns = slice(part * width, (part + 1) * width)
-        hidden = dot(normed, up_ref[:, columns], NN) + up_bias_ref[:, columns].astype(F32)
+        hidden = dot(normed, up_ref[:, columns], NN) + up_bias[:, columns]
         active, slope = gelu_parts(hidden)
         active = active.astype(BF16)
         active_ref[:, columns] = active
@@ -929,19 +1162,19 @@
     sums_ref[4:5] += column_sum(out * out)
 
 
-def feed(context, xs, time_row, cots, out_weight, out_bias, gain, shift, up, up_bias, down, down_bias):
+def feed(context, xs, info, small, cots, out_weight, up, down):
     block, width = xs[0].shape
     count, hidden_width = 2 * block, up.shape[1]
     sums_rows = 8 + hidden_width // width + (-(hidden_width // width)) % 8
-    row = fixed((1, width))
     whole = fixed((block, width))
     return pl.pallas_call(
         feed_kernel,
         grid=(2,),
         in_specs=[
-            rows(block, width), whole, whole, row, whole, whole, fixed(out_weight.shape), row, row, row,
-            fixed(up.shape), fixed((1, hidden_width)), fixed(down.shape), row,
-        ],
+            rows(block, width), whole, whole, fixed(info.shape), whole, whole,
+            fixed(out_weight.shape), fixed(up.shape), fixed(down.shape),
+        ]
+        + [whole_vector(v) for v in small],
         out_specs=[
             rows(block, width), rows(block, hidden_width), rows(block, hidden_width), rows(block, width),
             rows(block, width), rows(block, width), rows(block, width),
@@ -955,7 +1188,7 @@
         compiler_params=params(),
         cost_estimate=cost(34),
         name="feed",
-    )(context, *xs, time_row, *cots, out_weight, out_bias, gain, shift, up, up_bias, down, down_bias)
+    )(context, *xs, info, *cots, out_weight, up, down, *small)
 
 
 def down_grad_kernel(active_ref, cot0_ref, cot1_ref, out_ref):
@@ -1034,7 +1267,7 @@
 
 def start_kernel(
     query_grad_ref, key0_ref, key1_ref, far_key0_ref, far_key1_ref, value0_ref, value1_ref, far_value0_ref,
-    far_value1_ref, x0_ref, x1_ref, time_ref, middle_grad_ref, gain_ref, weight_ref,
+    far_value1_ref, x0_ref, x1_ref, info_ref, middle_grad_ref, gain_ref, weight_ref,
     token0_ref, token1_ref, grads_ref, sums_ref,
 ):
     step = pl.program_id(0)
@@ -1057,8 +1290,8 @@
         columns = slice(part * width, (part + 1) * width)
         grads_ref[:, columns] = grad
         normed_grad = normed_grad + dot(grad, weight_ref[:, columns], NT)
-    unit, scale = norm_parts(pick(x0_ref, x1_ref).astype(F32) + wide(time_ref))
-    token_grad = middle_grad_ref[...] + norm_backward(normed_grad, wide(gain_ref), unit, scale)
+    unit, scale = norm_parts(pick(x0_ref, x1_ref).astype(F32) + one_row(info_ref, TIME))
+    token_grad = middle_grad_ref[...] + norm_backward(normed_grad, vector(gain_ref), unit, scale)
 
     @pl.when(step == 0)
     def _():
@@ -1075,18 +1308,17 @@
     sums_ref[4:5] += column_sum(token_grad)
 
 
-def start_back(query_grad, key_grads, value_grads, xs, time_row, middle_grad, gain, weight):
+def start_back(query_grad, key_grads, value_grads, xs, info, middle_grad, gain, weight):
     block, width = xs[0].shape
     count = 2 * block
     whole = fixed((block, width))
-    row = fixed((1, width))
     kept = pl.BlockSpec((block, width), lambda i: (0, 0))
     return pl.pallas_call(
         start_kernel,
         grid=(2,),
         in_specs=[rows(block, width)]
         + [whole] * 10
-        + [row, rows(block, width), row, fixed(weight.shape)],
+        + [fixed(info.shape), rows(block, width), whole_vector(gain), fixed(weight.shape)],
         out_specs=[kept, kept, rows(block, 3 * width), pl.BlockSpec((8, width), lambda i: (0, 0))],
         out_shape=[
             shape_of((block, width)), shape_of((block, width)), shape_of((count, 3 * width)),
@@ -1095,7 +1327,7 @@
         compiler_params=params(),
         cost_estimate=cost(10),
         name="start_back",
-    )(query_grad, *key_grads, *value_grads, *xs, time_row, middle_grad, gain, weight)
+    )(query_grad, *key_grads, *value_grads, *xs, info, middle_grad, gain, weight)
 
 
 class Places:
@@ -1205,32 +1437,38 @@
             blocks.append(send(mine, places.gather_order(turn)))
         return blocks
 
-    far_steps = send(timesteps, places.swap(0))
-    xs = gathered(tokens)
-    cots = gathered(cotangent)
-    here = z // 2 == core
-    step_value = lax.dynamic_index_in_dim(jnp.where(here, timesteps, far_steps), z % 2, 0, keepdims=False)
+    count = 2 * local_len
+    parts = hidden_width // width
+    first_small = (ln1_gain, ln1_bias, q_bias, v_bias)
+    second_small = (out_bias, ln2_gain, ln2_bias, down_bias, up_bias)
     sequence = (d - core + z // 2) * seq_count + z % 2
-    time_row = lax.dynamic_slice_in_dim(time_table, step_value, 1, 0)
-
-    def row(v):
-        return v.reshape(1, -1)
-
-    bias_all = jnp.concatenate(
-        [q_bias.astype(F32), jnp.zeros((width,), F32), v_bias.astype(F32)]
-    ).reshape(1, -1)
-    count = 2 * local_len
-    normed, query, kv0 = project(xs[0], time_row, row(ln1_gain), row(ln1_bias), qkv_weight, bias_all, count)
-    far0 = send(kv0, places.swap(0))
-    normed, query, kv1 = project(
-        xs[1], time_row, row(ln1_gain), row(ln1_bias), qkv_weight, bias_all, count, (normed, query)
-    )
-    far1 = send(kv1, places.swap(0))
-    kvs = [kv0, kv1, far0, far1]
+    if places.dp == 8:
+        made = front(tokens, qkv_weight, time_table, timesteps, first_small, count / total_tokens)
+        xs, (normed, query), kvs, info = made[:2], made[2:4], list(made[4:8]), made[8]
+        cotangent, query = lax.optimization_barrier((cotangent, query))
+        cots = gathered(cotangent)
+    else:
+        info = jnp.concatenate(
+            [
+                known_rows(
+                    timesteps[j], seq_count * d + j, count / total_tokens,
+                    lax.dynamic_slice_in_dim(time_table, timesteps[j], 1, 0).astype(F32),
+                )
+                for j in range(2)
+            ]
+        )
+        far_info = send(info, places.swap(0))
+        xs = gathered(tokens)
+        cots = gathered(cotangent)
+        info = jnp.where(z // 2 == core, info, far_info)
+        info = jnp.pad(jnp.where(z % 2 == 0, info[:4], info[4:]), ((0, 4), (0, 0)))
+        normed, query, kv0 = project(xs[0], info, first_small, qkv_weight, count)
+        far0 = send(kv0, places.swap(0))
+        normed, query, kv1 = project(xs[1], info, first_small, qkv_weight, count, (normed, query))
+        kvs = [kv0, kv1, far0, send(kv1, places.swap(0))]
     context, logsum = attend(query, kvs)
     out, active, hidden_grad, normed_two, middle_grad, branch, context_grad, feed_sums = feed(
-        context, xs, time_row, cots, out_weight, row(out_bias), row(ln2_gain), row(ln2_bias),
-        up_weight, row(up_bias), down_weight, row(down_bias),
+        context, xs, info, second_small, cots, out_weight, up_weight, down_weight
     )
 
     def scattered(blocks, dtype):
@@ -1240,25 +1478,18 @@
             [jnp.where(even, back[0], back[1]), jnp.where(even, back[1], back[0])]
         ).astype(dtype)
 
-    parts = hidden_width // width
-    bucket = step_value * BUCKETS // TSTEPS
-    lane = jnp.arange(width)
-    step_row = jnp.where((lane == sequence) & (core == 0), step_value, 0).astype(F32)
-    mark = (lane == bucket).astype(F32)
-    count_row = jnp.where(lane == BUCKETS + bucket, count / total_tokens, 0.0)
+
     if places.dp == 8:
         made = back(
             query, context_grad, context, logsum, kvs, normed_two, hidden_grad, branch, active, cots, out
         )
-        layer_out = made[6]
-        down_sum, up_out_sum = made[7][0].astype(F32), made[8].astype(F32)
-        marks = jnp.concatenate([jnp.stack([mark, count_row, step_row]), jnp.zeros((5, width), F32)])
         tokens_grad, qkv_sum, packed = tail(
-            made[0], made[1:3], made[3:5], made[5], normed, xs, middle_grad, qkv_weight, time_row, row(ln1_gain),
-            feed_sums, marks, total_tokens, parts,
+            made[0], made[1:3], made[3:5], made[5], normed, xs, middle_grad, qkv_weight, info, ln1_gain,
+            feed_sums, total_tokens, parts,
         )
-        tokens_grad, qkv_sum = tokens_grad.astype(F32), qkv_sum.astype(F32)
-        sums = packed[16:]
+        tokens_grad, layer_out, qkv_sum, up_sum, out_sum, down_sum, table_grad = finish(
+            tokens_grad, made[6], qkv_sum, made[8], made[7][0], packed, time_table.shape[0] // places.dp, 9 + parts
+        )
     else:
         layer_out = scattered([out[:local_len], out[local_len:]], BF16)
         down_sum = reduce_parts(down_grad(active, cots)[None], places)[0]
@@ -1268,7 +1499,7 @@
             made[0],
             list(made[1:3]) + [send(g, places.swap(0)) for g in made[3:5]],
             list(made[5:7]) + [send(g, places.swap(0)) for g in made[7:9]],
-            xs, time_row, middle_grad, row(ln1_gain), qkv_weight,
+            xs, info, middle_grad, ln1_gain, qkv_weight,
         )
         tokens_grad = scattered([token0, token1], F32)
         qkv_sum = reduce_parts(qkv_grad(normed, projected_grad), places)
@@ -1277,23 +1508,28 @@
         packed = jnp.concatenate(
             [
                 feed_sums[0:4], feed_sums[8 : 8 + parts], start_sums[0:4],
-                jnp.stack([mark * energy + count_row, step_row]), sequence_rows,
+                jnp.stack(
+                    [info[MARK] * energy + info[SHARE], info[STEP] * jnp.where(core == 0, 1.0, 0.0)]
+                ),
+                sequence_rows,
             ]
         )
         packed = sum_everywhere(packed, places)
-        sums = packed[10 + parts :]
+        steps = packed[9 + parts, :total_seqs].astype(jnp.int32)
+        table_rows = time_table.shape[0] // places.dp
+        chosen = (steps[None, :] == (jnp.arange(table_rows) + d * table_rows)[:, None]).astype(F32)
+        table_grad = jnp.dot(chosen, packed[10 + parts :], precision=lax.Precision.HIGHEST)
+
+        def side_by_side(stacked):
+            return jnp.moveaxis(stacked, 0, 1).reshape(stacked.shape[1], -1)
+
+        qkv_sum, out_sum = side_by_side(qkv_sum), up_out_sum[parts]
+        up_sum = side_by_side(up_out_sum[:parts])
     piece = width // places.dp
     mine = lax.dynamic_slice_in_dim(packed[: 8 + parts], d * piece, piece, 1)
     up_piece = hidden_width // places.dp
     up_bias_sum = lax.dynamic_slice_in_dim(packed[4 : 4 + parts].reshape(-1), d * up_piece, up_piece, 0)
     stats = packed[8 + parts]
-    steps = packed[9 + parts, :total_seqs].astype(jnp.int32)
-    table_rows = time_table.shape[0] // places.dp
-    chosen = (steps[None, :] == (jnp.arange(table_rows) + d * table_rows)[:, None]).astype(F32)
-    table_grad = jnp.dot(chosen, sums, precision=lax.Precision.HIGHEST)
-
-    def side_by_side(stacked):
-        return jnp.moveaxis(stacked, 0, 1).reshape(stacked.shape[1], -1)
 
     return (
         layer_out,
@@ -1301,14 +1537,14 @@
         table_grad,
         mine[4 + parts],
         mine[5 + parts],
-        side_by_side(qkv_sum),
+        qkv_sum,
         mine[6 + parts],
         mine[7 + parts],
-        up_out_sum[parts],
+        out_sum,
         mine[3],
         mine[1],
         mine[2],
-        side_by_side(up_out_sum[:parts]),
+        up_sum,
         up_bias_sum,
         down_sum,
         mine[0],

time: 321 us -> 312 us (0.972)
  Pallas kernels: 253 us -> 291 us
  waiting for transfers between devices: 15.4 us -> 0.01 us
  local copies, waits for them, and re-layouts: 20.1 us -> 5.41 us
  starting transfers between devices: 17.1 us -> 9.09 us
  other arithmetic: 5.77 us -> 0 us
    pallas_call x2, Pallas kernels: 11.4 us -> 46.1 us  [the longest x1 39.3 us: front(): pl.pallas_call(functools.partial(front_kernel, share=share), in_specs=[an...]
    ppermute x7 -> x2, waiting for transfers between devices: 15.4 us -> 0.01 us  [send(): return lax.ppermute(x, BOTH, order)]
    ppermute x7 -> x2, starting transfers between devices: 17.1 us -> 9.09 us  [send(): return lax.ppermute(x, BOTH, order)]
    reshape x10 -> x0, local copies, waits for them, and re-layouts: 6.87 us -> none  [the longest x7 4.17 us: row(): return v.reshape(1, -1)]
    convert_element_type x7 -> x0, other arithmetic: 3.77 us -> none  [the longest x1 1.9 us: per_device(): tokens_grad, qkv_sum = (tokens_grad.astype(F32), qkv_sum.astype(F32))]
    pallas_call x1, Pallas kernels: 111 us -> 114 us  [back(): pl.pallas_call(functools.partial(back_kernel, pieces=pieces, parts=parts)...]
  transfers between devices with their start and end apart: 7 -> 2, of which waited for: 1 -> 0; matrix products, arithmetic and copies ran while one was open for 3% -> 0% of each run, Pallas kernels for 11% -> 10%
where the time goes in v4:
time: 312 us; the launch traced here: 307 us
  Pallas kernels  291 us (93%)
  starting transfers between devices  9.09 us (3%)
  local copies, waits for them, and re-layouts  5.41 us (2%)
    pallas_call x1, Pallas kernels, back(): pl.pallas_call(functools.partial(back_kernel, pieces=pieces, parts=parts)...  114 us
    pallas_call x1, Pallas kernels, tail(): pl.pallas_call(functools.partial(tail_kernel, total_tokens=total_tokens,...  66.1 us
    pallas_call x1, Pallas kernels, front(): pl.pallas_call(functools.partial(front_kernel, share=share), in_specs=[an...  39.3 us
    pallas_call x1, Pallas kernels, feed(): pl.pallas_call(feed_kernel, grid=(2,), in_specs=[rows(block, width), whol...  34.8 us
    pallas_call x1, Pallas kernels, attend(): pl.pallas_call(functools.partial(attend_kernel, pieces=pieces), grid=(pai...  30.2 us
    ppermute x2, starting transfers between devices, send(): return lax.ppermute(x, BOTH, order)  9.09 us
    pallas_call x1, Pallas kernels, finish(): pl.pallas_call(functools.partial(finish_kernel, total_seqs=sums.shape[0]...  6.8 us
  transfers between devices with their start and end apart: 2, of which 0 were waited for; matrix products, arithmetic and copies ran while one was open for 0% of the time, Pallas kernels for 10%

profile of v4, /device:TPU:0, one launch (start us, length us, event | category | flops | bytes accessed | tf_op | source)
XLA Modules:
  0.0 306.8 jit_solution(16563233549257233414)
XLA Ops:
  0.7 0.0 copy-start
  0.7 39.3 %front.1 = (bf16[512,768]{1,0:T(8,128)(2,1)}, bf16[512,768]{1,0:T(8,128)(2,1)}, bf16[1024,768]{1,0:T(8,128)(2,1)}, bf16[1024,768]{1,0:T(8,128)(2,1)}, bf16[512,1...) custom-call(bf16[2,512,768]{2,1,0:T(8,128)(2,1)} %tokens.1, ...), custom_call_target="tpu_custom_call" | custom-call | flops 55199997952 | tf_op jit(solution)/shard_map/front/pallas_call | solution.py:633
  40.0 0.0 copy-done
  40.0 0.1 dynamic-slice_bitcast_fusion
  40.2 0.9 collective-permute-start
  41.1 8.2 %collective-permute-start.1 = (bf16[512,768]{1,0:T(8,128)(2,1)S(1)}, bf16[512,768]{1,0:T(8,128)(2,1)S(1)}, u32[]{:S(2)}, u32[]{:S(2)}) collective-permute-start(bf16[512,768]{1,0:T(8,128)(2,1)S(1)} %get-tuple-element.98), channel_id=1, source_target_pairs={{0,1},{1,0},{2,5},{3,4},{4,3},{5,2},{6,7},{7,6},{8,9},{9,8},{10,13... | collective-permute-start | bytes 2359304 | tf_op jit(solution)/shard_map/ppermute | solution.py:1364
  49.3 30.2 %attend.1 = (bf16[1024,768]{1,0:T(8,128)(2,1)}, f32[1024,768]{1,0:T(8,128)}) custom-call(bf16[1024,768]{1,0:T(8,128)(2,1)} %get-tuple-element.59.query_ref, bf16[512,1536]{1,0:T(8,128)(2,1)} %get-tuple-element.60.refs_0_.refs_4_, bf16[512,1536]{1,0:T(8,128)(2,1)} %get-tuple-element.61.refs_1_.refs_5_, bf16[512,1536]{1,0:T(8,128)(2,1)} %get-tuple-element.62.refs_2_.refs_6_, ...), custom_call_target="tpu_custom_call" | custom-call | flops 36800000000 | tf_op jit(solution)/shard_map/attend/pallas_call | solution.py:235
  79.4 0.0 collective-permute-done.cot0_ref.refs_13_
  79.4 0.0 copy-start.1
  79.4 0.0 collective-permute-done.1.cot1_ref.refs_14_
  79.5 0.0 copy-start.2
  79.5 0.8 copy-done.1
  80.3 0.3 copy-done.2
  80.6 34.8 %feed.1 = (bf16[1024,768]{1,0:T(8,128)(2,1)}, bf16[1024,3072]{1,0:T(8,128)(2,1)}, bf16[1024,3072]{1,0:T(8,128)(2,1)}, bf16[1024,768]{1,0:T(8,128)(2,1)}, f32[102...) custom-call(bf16[1024,768]{1,0:T(8,128)(2,1)} %get-tuple-element.64.context_ref.refs_10, ...), custom_call_target="tpu_custom_call" | custom-call | flops 39099998208 | tf_op jit(solution)/shard_map/feed/pallas_call | solution.py:1170
  115.4 114.1 %back.1 = (bf16[1024,768]{1,0:T(8,128)(2,1)}, bf16[512,768]{1,0:T(8,128)(2,1)}, bf16[512,768]{1,0:T(8,128)(2,1)}, bf16[512,768]{1,0:T(8,128)(2,1)}, bf16[512,768...) custom-call(bf16[1024,768]{1,0:T(8,128)(2,1)} %get-tuple-element.59., ...), custom_call_target="tpu_custom_call" | custom-call | flops 115000000512 | tf_op jit(solution)/shard_map/back/pallas_call | solution.py:821
  229.5 66.1 %tail.1 = (bf16[2,512,768]{2,1,0:T(8,128)(2,1)}, bf16[3,96,768]{2,1,0:T(8,128)(2,1)}, f32[32,768]{1,0:T(8,128)}) custom-call(bf16[1024,768]{1,0:T(8,128)(2,1)} %get-tuple-element.76.query_grad, bf16[512,768]{1,0:T(8,128)(2,1)} %get-tuple-element.77.key0, bf16[512,768]{1,0:T(8,128)(2,1)} %get-tuple-element.78.key1, ...), custom_call_target="tpu_custom_call" | custom-call | flops 69000003584 | tf_op jit(solution)/shard_map/tail/pallas_call | solution.py:1017
  295.6 0.8 slice.45
  296.4 0.7 slice.53
  297.2 1.3 slice_bitcast_fusion
  298.5 0.7 dynamic_slice.16
  299.2 6.8 %finish.1 = (f32[1024,768]{1,0:T(8,128)}, bf16[1024,768]{1,0:T(8,128)(2,1)}, f32[96,2304]{1,0:T(8,128)}, f32[96,3072]{1,0:T(8,128)}, f32[96,768]{1,0:T(8,128)}, /*index=5*/f32[384,768]{1,0:T(8,128)}, f32[256,768]{1,0:T(8,128)}) custom-call(bf16[1024,768]{1,0:T(8,128)(2,1)} %bitcast.32, bf16[1024,768]{1,0:T(8,128)(2,1)} %bitcast.30, ...), custom_call_target="tpu_custom_call" | custom-call | flops 6899999744 | tf_op jit(solution)/shard_map/finish/pallas_call | solution.py:1074
  306.0 0.6 fusion
  (1 shorter events, 0.0 us)
Async XLA Ops:
  0.7 39.4 %copy-start = (bf16[2,512,768]{2,1,0:T(8,128)(2,1)S(1)}, bf16[2,512,768]{2,1,0:T(8,128)(2,1)}, u32[]{:S(2)}) copy-start(bf16[2,512,768]{2,1,0:T(8,128)(2,1)} %param.33) | copy-start | bytes 4718596
  40.2 39.3 %collective-permute-start = (bf16[512,768]{1,0:T(8,128)(2,1)S(1)}, bf16[512,768]{1,0:T(8,128)(2,1)S(1)}, u32[]{:S(2)}, u32[]{:S(2)}) collective-permute-start(bf16[512,768]{1,0:T(8,128)(2,1)S(1)} %get-tuple-element.99), channel_id=1, source_target_pairs={{0,0},{1,1},{2,4},{3,5},{4,2},{5,3},{6,6},{7,7},{8,8},{9,9},{10,12... | collective-permute-start | bytes 2359304 | tf_op jit(solution)/shard_map/ppermute | solution.py:1364
  41.1 38.4 %collective-permute-start.1 = (bf16[512,768]{1,0:T(8,128)(2,1)S(1)}, bf16[512,768]{1,0:T(8,128)(2,1)S(1)}, u32[]{:S(2)}, u32[]{:S(2)}) collective-permute-start(bf16[512,768]{1,0:T(8,128)(2,1)S(1)} %get-tuple-element.98), channel_id=1, source_target_pairs={{0,1},{1,0},{2,5},{3,4},{4,3},{5,2},{6,7},{7,6},{8,9},{9,8},{10,13... | collective-permute-start | bytes 2359304 | tf_op jit(solution)/shard_map/ppermute | solution.py:1364
  79.4 0.9 copy-start.1
  79.5 1.1 copy-start.2

commit v5 on v4

--- a/solution.py
+++ b/solution.py
@@ -12,7 +12,7 @@
 BUCKETS = 4
 EPS = 1e-05
 LANES = 128
-VMEM_BYTES = 56 * 1024 * 1024
+VMEM_BYTES = 60 * 1024 * 1024
 BOTH = ("dp", "seq")
 TOKEN_PARTS = 8
 TOKENS_AHEAD = 6
@@ -657,17 +657,14 @@
 
 
 def back_kernel(
-    query_ref, grad_ref, context_ref, logsum_ref, *refs, pieces, parts
+    query_ref, grad_ref, context_ref, logsum_ref, *refs, pieces, parts, pairs
 ):
     key_refs, value_refs = refs[:pieces], refs[pieces : 2 * pieces]
     refs = refs[2 * pieces :]
-    normed_ref, hidden_grad_ref, whole_context_ref, branch_ref, active_ref, cot0_ref, cot1_ref, layer_ref = refs[:8]
-    refs = refs[8:]
+    normed_ref, hidden_grad_ref, whole_context, branch, active_ref, cot0, cot1 = refs[:7]
+    first_normed, layer_ref, query_grad_ref, key_out, value_out, layer_out, down_out, up_out, qkv_out = refs[7:16]
+    refs = refs[16:]
     near = pieces // 2
-    query_grad_ref = refs[0]
-    key_grad_refs, value_grad_refs = refs[1 : 1 + near], refs[1 + near : 1 + 2 * near]
-    far_out, layer_out, down_out, up_out = refs[1 + 2 * near : 5 + 2 * near]
-    refs = refs[5 + 2 * near :]
     down_parts, up_parts = refs[:2]
     chunks = []
     for number, (which, at, many) in enumerate(back_chunks(down_parts.shape, up_parts.shape)):
@@ -680,9 +677,15 @@
         else:
             here_parts = pl.ds(at, many)
             chunks.append(Reduction(up_parts.at[here_parts], up_out.at[here_parts], scratch))
-    one, two, three, four = chunks
-    far_grads, far_sends, far_receives = refs[38:41]
-    back = Trade(layer_out, *refs[41:])
+    qkv_parts = refs[38]
+    for group in range(2):
+        lanes = pl.ds(2 * group * LANES, 2 * LANES)
+        scratch = refs[39 + 9 * group : 48 + 9 * group]
+        chunks.append(Reduction(qkv_parts.at[group], qkv_out.at[:, :, lanes], scratch))
+    one, two, three, four, five, six = chunks
+    query_held, near_grads, far_grads, far_in, far_sends, far_receives = refs[57:63]
+    whole_context_ref, branch_ref, cots_ref, first_normed_ref, loads = refs[63:68]
+    back = Trade(layer_out, *refs[68:])
     block = key_refs[0].shape[0]
     layer_blocks = [layer_ref.at[pl.ds(p * block, block)] for p in range(2)]
     step = pl.program_id(0)
@@ -691,37 +694,72 @@
 
     def far_copy(which):
         return remote(
-            far_grads, far_out.at[which], far_sends, far_receives, 0, which, partners()["core"]
+            far_grads, far_in.at[which % 2], far_sends, far_receives, 0, which, partners()["core"]
         )
 
+    loaded = [
+        pltpu.make_async_copy(source, target, loads.at[number])
+        for number, (source, target) in enumerate(
+            (
+                (whole_context, whole_context_ref), (branch, branch_ref), (cot0, cots_ref.at[pl.ds(0, block)]),
+                (cot1, cots_ref.at[pl.ds(block, block)]), (first_normed, first_normed_ref),
+            )
+        )
+    ]
+
     def begin():
+        for copy in loaded:
+            copy.start()
         meet(("core", "x", "y", "near", "far"), back)
         back.begin(0, layer_blocks[0])
         back.begin(1, layer_blocks[1])
+
+    def settle():
+        which = pair - 1
+        slot = which % 2
+        far_copy(which).wait()
+        key_grad = near_grads[slot, 0] + far_in[slot, 0]
+        value_grad = near_grads[slot, 1] + far_in[slot, 1]
+        key_out[...] = key_grad
+        value_out[...] = value_grad
+
+        @pl.when(which < 4)
+        def _():
+            grads = jnp.concatenate([query_held[slot], key_grad, value_grad], 1)
+            product = dot(first_normed_ref[...], grads, TN).astype(BF16)
+            lanes = pl.ds(pl.multiple_of(slot * LANES, LANES), LANES)
+            for part in range(3):
+                block_of = product[:, part * LANES : (part + 1) * LANES]
+                qkv_parts[which // 2, part, :, :, :, :, lanes] = block_of.reshape(qkv_parts.shape[2:6] + (LANES,))
 
     plan = {
         (0, 0): [begin],
         (2, 0): [one.to_cores],
         (4, 0): [one.to_first],
         (5, 0): [two.to_cores],
-        (8, 0): [one.to_second, two.to_first],
-        (9, 0): [three.to_cores, four.to_cores],
-        (10, 0): [one.to_near],
-        (10, 1): [two.to_second, three.to_first],
+        (8, 0): [two.to_first],
+        (9, 0): [three.to_cores, one.to_second],
+        (9, 1): [four.to_cores],
+        (10, 0): [three.to_first, one.to_near],
+        (10, 1): [two.to_second],
+        (10, 2): [four.to_first],
         (10, 3): [one.to_far],
-        (11, 0): [four.to_first],
-        (11, 2): [one.to_other, two.to_near, three.to_second],
-        (12, 0): [one.to_out, two.to_far],
+        (11, 0): [five.to_cores],
+        (11, 1): [two.to_near],
+        (11, 2): [three.to_second, one.to_other],
+        (11, 3): [five.to_first, four.to_second],
+        (12, 0): [two.to_far, one.to_out],
         (12, 1): [three.to_near],
-        (12, 2): [four.to_second],
+        (12, 2): [five.to_second, four.to_near],
         (12, 3): [three.to_far],
-        (13, 0): [two.to_other],
-        (13, 1): [four.to_near],
-        (13, 2): [three.to_other],
-        (13, 3): [two.to_out, four.to_far],
-        (14, 0): [three.to_out],
-        (14, 1): [four.to_other],
-        (14, 3): [four.to_out],
+        (13, 0): [six.to_cores, five.to_near, four.to_far, two.to_other],
+        (13, 1): [six.to_first],
+        (13, 2): [five.to_far],
+        (13, 3): [six.to_second, three.to_other, two.to_out],
+        (14, 1): [six.to_near, four.to_other, five.to_other, three.to_out],
+        (14, 2): [six.to_far],
+        (14, 3): [four.to_out, five.to_out],
+        (15, 0): [six.to_other, six.to_out],
     }
 
     def run_plan(place, steps):
@@ -742,52 +780,48 @@
 
     @pl.when(step == parts)
     def _():
+        for copy in loaded:
+            copy.wait()
         part = dot(whole_context_ref[...], branch_ref[...], TN).astype(BF16)
         up_parts[parts] = part.reshape(up_parts.shape[1:])
 
     @pl.when((step > parts) & (step < made))
     def _():
-        part = dot(active_ref[:block], cot0_ref[...], TN) + dot(active_ref[block:], cot1_ref[...], TN)
-        part = part.astype(BF16).reshape(down_parts.shape[3:])
+        part = dot(active_ref[...], cots_ref[...], TN).astype(BF16).reshape(down_parts.shape[3:])
         at = step - parts - 1
         down_parts[0, at // 2, at % 2] = part
 
     def before(place):
         def run():
-            run_plan(place, range(made, 100))
-            if place == 0:
-
-                @pl.when(pair > 0)
-                def _():
-                    far_copy(pair - 1).wait_send()
-
+            run_plan(place, range(made, made + pairs))
             if place == near:
                 far_copy(pair).start()
 
         return run
 
-    @pl.when(step >= made)
+    pl.when(pair >= 1)(settle)
+
+    @pl.when((step >= made) & (pair < pairs))
     def _():
         order = []
+        slot = pair % 2
         for i in range(near):
             far_rows = pl.ds(i * block, block)
             order.append(
                 (key_refs[near + i], value_refs[near + i], far_grads.at[0, far_rows], far_grads.at[1, far_rows])
             )
         for i in range(near):
-            order.append((key_refs[i], value_refs[i], key_grad_refs[i], value_grad_refs[i]))
+            near_rows = pl.ds(i * block, block)
+            order.append(
+                (key_refs[i], value_refs[i], near_grads.at[slot, 0, near_rows], near_grads.at[slot, 1, near_rows])
+            )
         steps = [one_piece + (before(place),) for place, one_piece in enumerate(order)]
         attend_back_step(query_ref, grad_ref, context_ref, logsum_ref, steps, query_grad_ref)
+        query_held[slot] = query_grad_ref[...]
 
     @pl.when(step == last)
     def _():
-        far_copy(pair).wait_send()
-
-        def received(which, carry):
-            far_copy(which).wait_recv()
-            return carry
-
-        lax.fori_loop(0, last + 1 - made, received, 0)
+        run_plan(0, [made + pairs])
         for p in range(2):
             back.sent(p, layer_blocks[p])
             back.arrived(p, layer_blocks[p])
@@ -805,51 +839,58 @@
     ]
 
 
-def back(query, grad, context, logsum, kvs, normed, hidden_grad, branch, active, cots, layer_out):
+def back(query, grad, context, logsum, kvs, normed, hidden_grad, branch, active, cots, first_normed, layer_out):
     count, width = query.shape
     pairs, pieces, length = width // LANES, len(kvs), kvs[0].shape[0]
     near = pieces // 2
     parts = hidden_grad.shape[1] // width
     made = 2 * parts + 1
-    pair = lambda i: jnp.maximum(i - made, 0)
+    pair = lambda i: jnp.clip(i - made, 0, pairs - 1)
     row = pl.BlockSpec((count, LANES), lambda i: (0, pair(i)))
+    settled = pl.BlockSpec((count, LANES), lambda i: (0, jnp.clip(i - made - 1, 0, pairs - 1)))
     piece = pl.BlockSpec((length, LANES), lambda i: (0, pair(i)))
     value = pl.BlockSpec((length, LANES), lambda i: (0, pairs + pair(i)))
     whole = fixed((count, width))
     up_rows, down_rows = width // 8, hidden_grad.shape[1] // 8
     down_shape, up_shape = (1, 2, 2, 2, down_rows, width), (parts + 1, 2, 2, 2, up_rows, width)
     return pl.pallas_call(
-        functools.partial(back_kernel, pieces=pieces, parts=parts),
-        grid=(made + pairs,),
+        functools.partial(back_kernel, pieces=pieces, parts=parts, pairs=pairs),
+        grid=(made + pairs + 1,),
         in_specs=[row] * 4
         + [piece] * pieces
         + [value] * pieces
         + [
             whole,
             pl.BlockSpec((count, width), lambda i: (0, jnp.minimum(i, parts - 1))),
-            whole,
-            whole,
+            fixed_any(),
+            fixed_any(),
             pl.BlockSpec((count, width), lambda i: (0, jnp.clip(i - parts - 1, 0, parts - 1))),
-            fixed((length, width)),
-            fixed((length, width)),
-            fixed_any(),
+        ]
+        + [fixed_any()] * 4,
+        out_specs=[row, settled, settled] + [fixed_any()] * 4,
+        out_shape=[shape_of((count, width))] * 3
+        + [
+            shape_of((2, length, width)), shape_of((1, down_rows, width)), shape_of((parts + 1, up_rows, width)),
+            shape_of((3, up_rows, 4 * LANES)),
         ],
-        out_specs=[row] + [piece] * (2 * near) + [fixed_any()] * 4,
-        out_shape=[shape_of((count, width))]
-        + [shape_of((length, width))] * (2 * near)
-        + [shape_of((pairs, 2, near * length, LANES)), shape_of((2, length, width))]
-        + [shape_of((1, down_rows, width)), shape_of((parts + 1, up_rows, width))],
         scratch_shapes=[pltpu.VMEM(down_shape, BF16), pltpu.VMEM(up_shape, BF16)]
         + [
             shape
             for which, _, many in back_chunks(down_shape, up_shape)
             for shape in Reduction.scratch(*((1, many) if which == "down" else (many, up_rows)), width)
         ]
+        + [pltpu.VMEM((2, 3, 2, 2, 2, up_rows, 2 * LANES), BF16)]
+        + Reduction.scratch(3, up_rows, 2 * LANES) * 2
         + [
-            pltpu.VMEM((2, near * length, LANES), BF16),
+            pltpu.VMEM((2, count, LANES), BF16),
+            pltpu.VMEM((2, 2, count, LANES), BF16),
+            pltpu.VMEM((2, count, LANES), BF16),
+            pltpu.VMEM((2, 2, count, LANES), BF16),
             pltpu.SemaphoreType.DMA((1,)),
             pltpu.SemaphoreType.DMA((pairs,)),
         ]
+        + [pltpu.VMEM((count, width), BF16)] * 4
+        + [pltpu.SemaphoreType.DMA((5,))]
         + Trade.semaphores(),
         compiler_params=pltpu.CompilerParams(
             vmem_limit_bytes=VMEM_BYTES, collective_id=0, has_side_effects=True
@@ -857,33 +898,33 @@
         cost_estimate=cost(100),
         name="back",
     )(
-        query, grad, context, logsum, *kvs, *kvs, normed, hidden_grad, context, branch, active, *cots, layer_out
+        query, grad, context, logsum, *kvs, *kvs, normed, hidden_grad, context, branch, active, *cots,
+        first_normed, layer_out
     )
 
 
 def tail_kernel(
-    query_grad, key0, key1, value0, value1, far, normed, x0, x1, middle_grad, weight,
+    query_grad, key_grad, value_grad, normed, x0, x1, middle_grad, weight,
     info_ref, gain_ref, feed_ref,
     tokens_out, qkv_out, sums_ref,
-    query_v, near_v, far_v, normed_v, x_v, middle_v, weight_v, key_v, value_v, token_v,
-    query_parts, key_parts, value_parts, *refs, total_tokens, parts,
+    query_v, key_v, value_v, normed_v, x_v, middle_v, weight_v, token_v, last_parts, *refs, total_tokens, parts,
 ):
-    reductions = []
-    for number, made in enumerate((query_parts, key_parts, value_parts)):
-        reductions.append(Reduction(made, qkv_out.at[pl.ds(number, 1)], refs[9 * number : 9 * number + 9]))
-    of_query, of_key, of_value = reductions
-    sums_in, sums_sends, sums_receives, loads = refs[27:31]
-    back = Trade(tokens_out, *refs[31:], parts=TOKEN_PARTS)
+    one = Reduction(last_parts, qkv_out, refs[:9])
+    sums_in, sums_sends, sums_receives, loads = refs[9:13]
+    back = Trade(tokens_out, *refs[13:], parts=TOKEN_PARTS)
     block, width = x0.shape
-    pairs = width // LANES
     d, z, _, _, core = here()
+    total = 2 * TOKEN_PARTS
+    top, bottom = pl.ds(0, block), pl.ds(block, block)
+    later = ((query_grad, query_v), (key_grad, key_v), (value_grad, value_v), (middle_grad, middle_v))
     copies = [
         pltpu.make_async_copy(source, target, loads.at[number])
         for number, (source, target) in enumerate(
             (
-                (normed, normed_v), (query_grad, query_v), (key0, near_v.at[0, 0]), (value0, near_v.at[1, 0]),
-                (far, far_v), (weight, weight_v), (x0, x_v.at[0]), (middle_grad, middle_v),
-                (key1, near_v.at[0, 1]), (value1, near_v.at[1, 1]), (x1, x_v.at[1]),
+                (weight, weight_v), (x0, x_v.at[0]),
+                *((ref.at[top], held.at[top]) for ref, held in later),
+                (normed, normed_v), (x1, x_v.at[1]),
+                *((ref.at[bottom], held.at[bottom]) for ref, held in later),
             )
         )
     ]
@@ -891,15 +932,8 @@
         copy.start()
     meet(("core", "x", "y", "near", "far"), back)
 
-    def product(grads, out):
-        out[0] = dot(normed_v[...], grads[...], TN).astype(BF16).reshape(out.shape[1:])
-
     def start_block(p):
         held = pl.ds(p * block, block)
-        for pair in range(pairs):
-            lanes = slice(pair * LANES, (pair + 1) * LANES)
-            key_v[held, lanes] = near_v[0, p, :, lanes] + far_v[pair, 0, held]
-            value_v[held, lanes] = near_v[1, p, :, lanes] + far_v[pair, 1, held]
         normed_grad = 0.0
         for part, grads in enumerate((query_v, key_v, value_v)):
             columns = slice(part * width, (part + 1) * width)
@@ -932,14 +966,20 @@
         p, part = divmod(number, TOKEN_PARTS)
         back.begin(p, token_v.at[p], part)
 
-    for copy in copies[1:8]:
+    for copy in copies[:6]:
         copy.wait()
     first = start_block(0)
-    for number in range(4):
+    for number in range(TOKENS_AHEAD):
         move(number)
-    for copy in copies[8:]:
+    for copy in copies[6:]:
         copy.wait()
+    lanes = slice(width - 2 * LANES, width)
+    for part, grads in enumerate((query_v, key_v, value_v)):
+        made = dot(normed_v[...], grads[:, lanes], TN).astype(BF16)
+        last_parts[part] = made.reshape(last_parts.shape[1:])
+    one.to_cores()
     second = start_block(1)
+    one.to_first()
     sums = [a + b for a, b in zip(first, second)]
     sums_ref[...] = jnp.zeros_like(sums_ref)
     sums_ref[0:4] = feed_ref[0:4]
@@ -952,86 +992,59 @@
     sequence = (d - core + z // 2) * 2 + z % 2
     sums_ref[pl.ds(16 + sequence, 1)] = sums[4]
     sums_copy(0).start()
-    move(4)
-    move(5)
-    copies[0].wait()
-    product(query_v, query_parts)
-    of_query.to_cores()
-    move(6)
-    product(key_v, key_parts)
-    of_key.to_cores()
+    for number in range(TOKENS_AHEAD, TOKENS_AHEAD + 2):
+        move(number)
     sums_next(0)
-    move(7)
-    of_query.to_first()
-    product(value_v, value_parts)
-    of_value.to_cores()
+    one.to_second()
     sums_next(1)
-    move(8)
-    of_key.to_first()
-    move(9)
-    of_query.to_second()
+    one.to_near()
     sums_next(2)
-    move(10)
-    of_value.to_first()
-    move(11)
-    of_key.to_second()
-    of_query.to_near()
+    for number in range(TOKENS_AHEAD + 2, TOKENS_AHEAD + 4):
+        move(number)
+    one.to_far()
     sums_next(3)
-    move(12)
-    of_query.to_far()
-    of_value.to_second()
+    for number in range(TOKENS_AHEAD + 4, TOKENS_AHEAD + 6):
+        move(number)
+    one.to_other()
     sums_next(4)
-    of_key.to_near()
-    move(13)
-    of_key.to_far()
-    of_value.to_near()
-    move(14)
-    of_query.to_other()
-    of_value.to_far()
-    move(15)
-    of_key.to_other()
-    of_query.to_out()
-    of_value.to_other()
-    of_key.to_out()
-    of_value.to_out()
-    total = 2 * TOKEN_PARTS
+    for number in range(TOKENS_AHEAD + 6, total):
+        move(number)
+    one.to_out()
     for number in range(total - TOKENS_AHEAD, total):
         p, part = divmod(number, TOKEN_PARTS)
         back.sent(p, token_v.at[p], part)
     for number in range(total):
         p, part = divmod(number, TOKEN_PARTS)
         back.arrived(p, token_v.at[p], part)
-    for one in reductions:
-        one.finish()
-
-
-def tail(query_grad, key_grads, value_grads, far, normed, xs, middle_grad, weight, info, gain, feed_sums, total_tokens, hidden_parts):
+    one.finish()
+
+
+def tail(grads, normed, xs, middle_grad, weight, info, gain, feed_sums, total_tokens, hidden_parts):
     block, width = xs[0].shape
     count, total_seqs = 2 * block, 16
     any_spec = fixed_any()
     inside = pl.BlockSpec(memory_space=pltpu.VMEM)
     up_rows = width // 8
-    parts = pltpu.VMEM((1, 2, 2, 2, up_rows, width), BF16)
     held = lambda *shape, dtype=BF16: pltpu.VMEM(shape, dtype)
     sums_shape = (16 + total_seqs, width)
     return pl.pallas_call(
         functools.partial(tail_kernel, total_tokens=total_tokens, parts=hidden_parts),
-        in_specs=[any_spec] * 11 + [inside] * 3,
+        in_specs=[any_spec] * 8 + [inside] * 3,
         out_specs=[any_spec, any_spec, inside],
         out_shape=[
-            shape_of((2, block, width)), shape_of((3, up_rows, width)), shape_of(sums_shape, F32),
+            shape_of((2, block, width)), shape_of((3, up_rows, 2 * LANES)), shape_of(sums_shape, F32),
         ],
         scratch_shapes=[
-            held(count, width), held(2, 2, block, width), held(*far.shape), held(count, width),
-            held(2, block, width), held(count, width, dtype=F32), held(*weight.shape), held(count, width),
-            held(count, width), held(2, block, width), parts, parts, parts,
+            held(count, width), held(count, width), held(count, width), held(count, width),
+            held(2, block, width), held(count, width, dtype=F32), held(*weight.shape), held(2, block, width),
+            held(3, 2, 2, 2, up_rows, 2 * LANES),
         ]
-        + Reduction.scratch(1, up_rows, width) * 3
+        + Reduction.scratch(3, up_rows, 2 * LANES)
         + [
             held(5, *sums_shape, dtype=F32),
             pltpu.SemaphoreType.DMA((5,)),
             pltpu.SemaphoreType.DMA((5,)),
-            pltpu.SemaphoreType.DMA((11,)),
+            pltpu.SemaphoreType.DMA((12,)),
         ]
         + Trade.semaphores(TOKEN_PARTS),
         compiler_params=pltpu.CompilerParams(
@@ -1039,22 +1052,21 @@
         ),
         cost_estimate=cost(60),
         name="tail",
-    )(
-        query_grad, *key_grads, *value_grads, far, normed, *xs, middle_grad, weight, info, gain, feed_sums
-    )
+    )(*grads, normed, *xs, middle_grad, weight, info, gain, feed_sums)
 
 
 def finish_kernel(
-    token_ref, layer_ref, qkv_ref, up_out_ref, out_part_ref, down_ref, sums_ref,
-    token_out, layer_out, qkv_out, up_out, out_out, down_out, table_out, *, total_seqs, steps_row, table_rows,
+    token_ref, layer_ref, qkv_ref, last_qkv_ref, up_out_ref, out_part_ref, down_ref, sums_ref,
+    token_out, layer_out, qkv_out, up_out, out_out, down_out, table_out, *small_outs, total_seqs, parts, table_rows,
 ):
     token_out[...] = wide(token_ref)
     layer_out[...] = layer_ref[...]
-    qkv_out[...] = qkv_ref[0].astype(F32)
+    qkv_out[...] = jnp.concatenate([qkv_ref[0], last_qkv_ref[0]], 1).astype(F32)
     up_out[...] = up_out_ref[0].astype(F32)
     out_out[...] = out_part_ref[0].astype(F32)
     down_out[...] = wide(down_ref)
-    block = table_out.shape[0]
+    block, width = table_out.shape
+    steps_row = 9 + parts
     first = lax.axis_index("dp") * table_rows + pl.program_id(0) * block
     place = (lax.broadcasted_iota(jnp.int32, (block, 1), 0) + first).astype(F32)
     total = jnp.zeros_like(table_out)
@@ -1063,22 +1075,40 @@
         total = total + jnp.where(chosen, sums_ref[16 + s : 17 + s], 0.0)
     table_out[...] = total
 
-
-def finish(token, layer, qkv, up_out, down, sums, table_rows, steps_row):
+    @pl.when(pl.program_id(0) == 0)
+    def _():
+        d = lax.axis_index("dp")
+        piece = small_outs[0].shape[0]
+        turned = pltpu.roll(sums_ref[0:16], lax.rem(width - d * piece, width), 1)
+        order = [row for row in range(8 + parts) if not 4 <= row < 4 + parts]
+        for row, out in zip(order, small_outs):
+            out[...] = turned[row, :piece]
+        up_piece = small_outs[8].shape[0]
+        share = width // up_piece
+        mine = sums_ref[pl.ds(4 + d // share, 1)]
+        mine = pltpu.roll(mine, lax.rem(width - d % share * up_piece, width), 1)
+        small_outs[8][...] = mine[0, :up_piece]
+        small_outs[9][...] = sums_ref[8 + parts, :BUCKETS]
+        small_outs[10][...] = sums_ref[8 + parts, BUCKETS : 2 * BUCKETS]
+
+
+def finish(token, layer, qkv, last_qkv, up_out, down, sums, table_rows, dp):
     seqs, length, width = token.shape
     parts, block = up_out.shape[0] - 1, up_out.shape[1]
     steps = parts
+    small = [width // dp] * 8 + [parts * width // dp] + [BUCKETS] * 2
     rows_at = lambda many: pl.BlockSpec((many // steps, width), lambda i: (i, 0))
     count = seqs * length
     wide_rows = rows_at(count)
     made = pl.pallas_call(
         functools.partial(
-            finish_kernel, total_seqs=sums.shape[0] - 16, steps_row=steps_row, table_rows=table_rows
+            finish_kernel, total_seqs=sums.shape[0] - 16, parts=parts, table_rows=table_rows
         ),
         grid=(steps,),
         in_specs=[
             wide_rows, wide_rows,
-            pl.BlockSpec((1, block, width), lambda i: (jnp.minimum(i, 2), 0, 0)),
+            pl.BlockSpec((1, block, qkv.shape[2]), lambda i: (jnp.minimum(i, 2), 0, 0)),
+            pl.BlockSpec((1, block, last_qkv.shape[2]), lambda i: (jnp.minimum(i, 2), 0, 0)),
             pl.BlockSpec((1, block, width), lambda i: (i, 0, 0)),
             pl.BlockSpec((1, block, width), lambda i: (parts, 0, 0)),
             rows_at(down.shape[0]),
@@ -1090,16 +1120,18 @@
             pl.BlockSpec((block, width), lambda i: (0, i)),
             pl.BlockSpec((block, width), lambda i: (0, 0)),
             rows_at(down.shape[0]), rows_at(table_rows),
-        ],
+        ]
+        + [pl.BlockSpec((many,), lambda i: (0,)) for many in small],
         out_shape=[
             shape_of((count, width), F32), shape_of((count, width)), shape_of((block, 3 * width), F32),
             shape_of((block, parts * width), F32), shape_of((block, width), F32), shape_of(down.shape, F32),
             shape_of((table_rows, width), F32),
-        ],
+        ]
+        + [shape_of((many,), F32) for many in small],
         compiler_params=params(),
         cost_estimate=cost(6),
         name="finish",
-    )(token.reshape(count, width), layer.reshape(count, width), qkv, up_out, up_out, down, sums)
+    )(token.reshape(count, width), layer.reshape(count, width), qkv, last_qkv, up_out, up_out, down, sums)
     shape = (seqs, length, width)
     return [made[0].reshape(shape), made[1].reshape(shape)] + list(made[2:])
 
@@ -1114,20 +1146,38 @@
     context_ref, x0_ref, x1_ref, info_ref, cot0_ref, cot1_ref, out_weight_ref, up_ref, down_ref,
     out_bias_ref, gain_ref, shift_ref, down_bias_ref, up_bias_ref,
     out_ref, active_ref, hidden_grad_ref, normed_ref, middle_grad_ref, branch_ref, context_grad_ref, sums_ref,
+    out_weight_v, up_v, down_v, loads,
 ):
     step = pl.program_id(0)
     width, hidden_width = x0_ref.shape[1], up_ref.shape[1]
 
+    parts = hidden_width // width
+    out_copy = pltpu.make_async_copy(out_weight_ref, out_weight_v, loads.at[0, parts])
+    copies = []
+    for part in range(parts):
+        columns = pl.ds(part * width, width)
+        copies.append(
+            (
+                pltpu.make_async_copy(up_ref.at[:, columns], up_v.at[:, columns], loads.at[0, part]),
+                pltpu.make_async_copy(down_ref.at[columns], down_v.at[columns], loads.at[1, part]),
+            )
+        )
+
     @pl.when(step == 0)
     def _():
+        out_copy.start()
+        for one, two in copies:
+            one.start()
+            two.start()
         sums_ref[...] = jnp.zeros_like(sums_ref)
+        out_copy.wait()
 
     x = jnp.where(step == 0, x0_ref[...], x1_ref[...])
     cot = jnp.where(step == 0, cot0_ref[...], cot1_ref[...])
     middle = (
         x.astype(F32)
         + one_row(info_ref, TIME)
-        + dot(context_ref[...], out_weight_ref[...], NN)
+        + dot(context_ref[...], out_weight_v[...], NN)
         + vector(out_bias_ref)
     )
     unit, scale = norm_parts(middle)
@@ -1137,24 +1187,30 @@
     out = middle + vector(down_bias_ref)
     normed_grad = jnp.zeros_like(out)
     up_bias = vector(up_bias_ref)
-    for part in range(hidden_width // width):
+    for part in range(parts):
         columns = slice(part * width, (part + 1) * width)
-        hidden = dot(normed, up_ref[:, columns], NN) + up_bias[:, columns]
+
+        @pl.when(step == 0)
+        def _():
+            for copy in copies[part]:
+                copy.wait()
+
+        hidden = dot(normed, up_v[:, columns], NN) + up_bias[:, columns]
         active, slope = gelu_parts(hidden)
         active = active.astype(BF16)
         active_ref[:, columns] = active
-        out = out + dot(active, down_ref[columns, :], NN)
-        hidden_grad = (dot(cot, down_ref[columns, :], NT) * slope).astype(BF16)
+        out = out + dot(active, down_v[columns, :], NN)
+        hidden_grad = (dot(cot, down_v[columns, :], NT) * slope).astype(BF16)
         hidden_grad_ref[:, columns] = hidden_grad
         sums_ref[8 + part : 9 + part] += column_sum(hidden_grad.astype(F32))
-        normed_grad = normed_grad + dot(hidden_grad, up_ref[:, columns], NT)
+        normed_grad = normed_grad + dot(hidden_grad, up_v[:, columns], NT)
     out_ref[...] = out.astype(BF16)
     cot = cot.astype(F32)
     middle_grad = cot + norm_backward(normed_grad, gain, unit, scale)
     middle_grad_ref[...] = middle_grad
     branch = middle_grad.astype(BF16)
     branch_ref[...] = branch
-    context_grad_ref[...] = dot(branch, out_weight_ref[...], NT).astype(BF16)
+    context_grad_ref[...] = dot(branch, out_weight_v[...], NT).astype(BF16)
     sums_ref[0:1] += column_sum(cot)
     sums_ref[1:2] += column_sum(normed_grad * unit)
     sums_ref[2:3] += column_sum(normed_grad)
@@ -1172,8 +1228,8 @@
         grid=(2,),
         in_specs=[
             rows(block, width), whole, whole, fixed(info.shape), whole, whole,
-            fixed(out_weight.shape), fixed(up.shape), fixed(down.shape),
         ]
+        + [pl.BlockSpec(memory_space=pl.ANY)] * 3
         + [whole_vector(v) for v in small],
         out_specs=[
             rows(block, width), rows(block, hidden_width), rows(block, hidden_width), rows(block, width),
@@ -1184,6 +1240,10 @@
             shape_of((count, width)), shape_of((count, hidden_width)), shape_of((count, hidden_width)),
             shape_of((count, width)), shape_of((count, width), F32), shape_of((count, width)),
             shape_of((count, width)), shape_of((sums_rows, width), F32),
+        ],
+        scratch_shapes=[
+            pltpu.VMEM(out_weight.shape, BF16), pltpu.VMEM(up.shape, BF16), pltpu.VMEM(down.shape, BF16),
+            pltpu.SemaphoreType.DMA((2, hidden_width // width + 1)),
         ],
         compiler_params=params(),
         cost_estimate=cost(34),
@@ -1481,14 +1541,15 @@
 
     if places.dp == 8:
         made = back(
-            query, context_grad, context, logsum, kvs, normed_two, hidden_grad, branch, active, cots, out
+            query, context_grad, context, logsum, kvs, normed_two, hidden_grad, branch, active, cots,
+            normed, out
         )
-        tokens_grad, qkv_sum, packed = tail(
-            made[0], made[1:3], made[3:5], made[5], normed, xs, middle_grad, qkv_weight, info, ln1_gain,
-            feed_sums, total_tokens, parts,
+        tokens_grad, last_qkv, packed = tail(
+            made[:3], normed, xs, middle_grad, qkv_weight, info, ln1_gain, feed_sums, total_tokens, parts
         )
-        tokens_grad, layer_out, qkv_sum, up_sum, out_sum, down_sum, table_grad = finish(
-            tokens_grad, made[6], qkv_sum, made[8], made[7][0], packed, time_table.shape[0] // places.dp, 9 + parts
+        tokens_grad, layer_out, qkv_sum, up_sum, out_sum, down_sum, table_grad, *small = finish(
+            tokens_grad, made[3], made[6], last_qkv, made[5], made[4][0], packed,
+            time_table.shape[0] // places.dp, places.dp,
         )
     else:
         layer_out = scattered([out[:local_len], out[local_len:]], BF16)
@@ -1525,31 +1586,17 @@
 
         qkv_sum, out_sum = side_by_side(qkv_sum), up_out_sum[parts]
         up_sum = side_by_side(up_out_sum[:parts])
-    piece = width // places.dp
-    mine = lax.dynamic_slice_in_dim(packed[: 8 + parts], d * piece, piece, 1)
-    up_piece = hidden_width // places.dp
-    up_bias_sum = lax.dynamic_slice_in_dim(packed[4 : 4 + parts].reshape(-1), d * up_piece, up_piece, 0)
-    stats = packed[8 + parts]
-
+        piece = width // places.dp
+        mine = lax.dynamic_slice_in_dim(packed[: 8 + parts], d * piece, piece, 1)
+        up_piece = hidden_width // places.dp
+        up_bias_sum = lax.dynamic_slice_in_dim(packed[4 : 4 + parts].reshape(-1), d * up_piece, up_piece, 0)
+        stats = packed[8 + parts]
+        small = [mine[row] for row in (0, 1, 2, 3, 4 + parts, 5 + parts, 6 + parts, 7 + parts)]
+        small += [up_bias_sum, stats[:BUCKETS], stats[BUCKETS : 2 * BUCKETS]]
+    down_bias_sum, gain_two, shift_two, out_bias_sum, gain_one, shift_one, q_sum, v_sum = small[:8]
     return (
-        layer_out,
-        tokens_grad,
-        table_grad,
-        mine[4 + parts],
-        mine[5 + parts],
-        qkv_sum,
-        mine[6 + parts],
-        mine[7 + parts],
-        out_sum,
-        mine[3],
-        mine[1],
-        mine[2],
-        up_sum,
-        up_bias_sum,
-        down_sum,
-        mine[0],
-        stats[:BUCKETS],
-        stats[BUCKETS : 2 * BUCKETS],
+        layer_out, tokens_grad, table_grad, gain_one, shift_one, qkv_sum, q_sum, v_sum, out_sum, out_bias_sum,
+        gain_two, shift_two, up_sum, small[8], down_sum, down_bias_sum, small[9], small[10],
     )
 
 

time: 312 us -> 300 us (0.962)
  Pallas kernels: 291 us -> 284 us
  local copies, waits for them, and re-layouts: 5.41 us -> 1.23 us
    pallas_call x1, Pallas kernels: 66.1 us -> 53.3 us  [tail(): pl.pallas_call(functools.partial(tail_kernel, total_tokens=total_tokens,...]
    pallas_call x1, Pallas kernels: 114 us -> 118 us  [back(): pl.pallas_call(functools.partial(back_kernel, pieces=pieces, parts=parts,...]
where the time goes in v5:
time: 300 us; the launch traced here: 295 us
  Pallas kernels  284 us (95%)
  starting transfers between devices  9.07 us (3%)
    pallas_call x1, Pallas kernels, back(): pl.pallas_call(functools.partial(back_kernel, pieces=pieces, parts=parts,...  118 us
    pallas_call x1, Pallas kernels, tail(): pl.pallas_call(functools.partial(tail_kernel, total_tokens=total_tokens,...  53.3 us
    pallas_call x1, Pallas kernels, front(): pl.pallas_call(functools.partial(front_kernel, share=share), in_specs=[an...  39.3 us
    pallas_call x1, Pallas kernels, feed(): pl.pallas_call(feed_kernel, grid=(2,), in_specs=[rows(block, width), whol...  35.4 us
    pallas_call x1, Pallas kernels, attend(): pl.pallas_call(functools.partial(attend_kernel, pieces=pieces), grid=(pai...  30.2 us
    ppermute x2, starting transfers between devices, send(): return lax.ppermute(x, BOTH, order)  9.07 us
    pallas_call x1, Pallas kernels, finish(): pl.pallas_call(functools.partial(finish_kernel, total_seqs=sums.shape[0]...  7.23 us
  transfers between devices with their start and end apart: 2, of which 0 were waited for; matrix products, arithmetic and copies ran while one was open for 0% of the time, Pallas kernels for 10%

profile of v5, /device:TPU:0, one launch (start us, length us, event | category | flops | bytes accessed | tf_op | source)
XLA Modules:
  0.0 295.0 jit_solution(12994481835025016604)
XLA Ops:
  0.7 0.0 copy-start
  0.7 39.3 %front.1 = (bf16[512,768]{1,0:T(8,128)(2,1)}, bf16[512,768]{1,0:T(8,128)(2,1)}, bf16[1024,768]{1,0:T(8,128)(2,1)}, bf16[1024,768]{1,0:T(8,128)(2,1)}, bf16[512,1...) custom-call(bf16[2,512,768]{2,1,0:T(8,128)(2,1)} %tokens.1, ...), custom_call_target="tpu_custom_call" | custom-call | flops 55199997952 | tf_op jit(solution)/shard_map/front/pallas_call | solution.py:633
  40.0 0.0 copy-done
  40.0 0.1 dynamic-slice_bitcast_fusion
  40.2 8.2 %collective-permute-start.1 = (bf16[512,768]{1,0:T(8,128)(2,1)S(1)}, bf16[512,768]{1,0:T(8,128)(2,1)S(1)}, u32[]{:S(2)}, u32[]{:S(2)}) collective-permute-start(bf16[512,768]{1,0:T(8,128)(2,1)S(1)} %get-tuple-element.116), channel_id=1, source_target_pairs={{0,1},{1,0},{2,5},{3,4},{4,3},{5,2},{6,7},{7,6},{8,9},{9,8},{10,13... | collective-permute-start | bytes 2359304 | tf_op jit(solution)/shard_map/ppermute | solution.py:1424
  48.4 0.9 collective-permute-start
  49.2 30.2 %attend.1 = (bf16[1024,768]{1,0:T(8,128)(2,1)}, f32[1024,768]{1,0:T(8,128)}) custom-call(bf16[1024,768]{1,0:T(8,128)(2,1)} %get-tuple-element.68.query_ref, bf16[512,1536]{1,0:T(8,128)(2,1)} %get-tuple-element.69.refs_0_.refs_4_, bf16[512,1536]{1,0:T(8,128)(2,1)} %get-tuple-element.70.refs_1_.refs_5_, bf16[512,1536]{1,0:T(8,128)(2,1)} %get-tuple-element.71.refs_2_.refs_6_, ...), custom_call_target="tpu_custom_call" | custom-call | flops 36800000000 | tf_op jit(solution)/shard_map/attend/pallas_call | solution.py:235
  79.4 0.0 collective-permute-done.1.cot1_ref.refs_14_
  79.4 0.0 copy-start.1
  79.4 0.0 collective-permute-done.cot0_ref.refs_13_
  79.5 0.0 copy-start.2
  79.5 0.8 copy-done.1
  80.3 0.3 copy-done.2
  80.6 35.4 %feed.1 = (bf16[1024,768]{1,0:T(8,128)(2,1)}, bf16[1024,3072]{1,0:T(8,128)(2,1)}, bf16[1024,3072]{1,0:T(8,128)(2,1)}, bf16[1024,768]{1,0:T(8,128)(2,1)}, f32[102...) custom-call(bf16[1024,768]{1,0:T(8,128)(2,1)} %get-tuple-element.73.context_ref.refs_10, ...), custom_call_target="tpu_custom_call" | custom-call | flops 39099998208 | tf_op jit(solution)/shard_map/feed/pallas_call | solution.py:1226
  116.0 118.1 %back.1 = (bf16[1024,768]{1,0:T(8,128)(2,1)}, bf16[1024,768]{1,0:T(8,128)(2,1)}, bf16[1024,768]{1,0:T(8,128)(2,1)}, bf16[2,512,768]{2,1,0:T(8,128)(2,1)}, bf16[1...) custom-call(bf16[1024,768]{1,0:T(8,128)(2,1)} %get-tuple-element.68.query_ref, ...), custom_call_target="tpu_custom_call" | custom-call | flops 115000000512 | tf_op jit(solution)/shard_map/back/pallas_call | solution.py:856
  234.2 53.3 %tail.1 = (bf16[2,512,768]{2,1,0:T(8,128)(2,1)}, bf16[3,96,256]{2,1,0:T(8,128)(2,1)}, f32[32,768]{1,0:T(8,128)}) custom-call(bf16[1024,768]{1,0:T(8,128)(2,1)} %get-tuple-element.86.query_grad, bf16[1024,768]{1,0:T(8,128)(2,1)} %get-tuple-element.87.key_grad, bf16[1024,768]{1,0:T(8,128)(2,1)} %get-tuple-element.88.value_grad, ...), custom_call_target="tpu_custom_call" | custom-call | flops 69000003584 | tf_op jit(solution)/shard_map/tail/pallas_call | solution.py:1030
  287.5 7.2 %finish.1 = (f32[1024,768]{1,0:T(8,128)}, bf16[1024,768]{1,0:T(8,128)(2,1)}, f32[96,2304]{1,0:T(8,128)}, f32[96,3072]{1,0:T(8,128)}, f32[96,768]{1,0:T(8,128)}, ...) custom-call(bf16[1024,768]{1,0:T(8,128)(2,1)} %bitcast.12, ...), custom_call_target="tpu_custom_call" | custom-call | flops 6899999744 | tf_op jit(solution)/shard_map/finish/pallas_call | solution.py:1103
Async XLA Ops:
  0.7 39.3 %copy-start = (bf16[2,512,768]{2,1,0:T(8,128)(2,1)S(1)}, bf16[2,512,768]{2,1,0:T(8,128)(2,1)}, u32[]{:S(2)}) copy-start(bf16[2,512,768]{2,1,0:T(8,128)(2,1)} %param.33) | copy-start | bytes 4718596
  40.2 39.3 %collective-permute-start.1 = (bf16[512,768]{1,0:T(8,128)(2,1)S(1)}, bf16[512,768]{1,0:T(8,128)(2,1)S(1)}, u32[]{:S(2)}, u32[]{:S(2)}) collective-permute-start(bf16[512,768]{1,0:T(8,128)(2,1)S(1)} %get-tuple-element.116), channel_id=1, source_target_pairs={{0,1},{1,0},{2,5},{3,4},{4,3},{5,2},{6,7},{7,6},{8,9},{9,8},{10,13... | collective-permute-start | bytes 2359304 | tf_op jit(solution)/shard_map/ppermute | solution.py:1424
  48.4 31.1 %collective-permute-start = (bf16[512,768]{1,0:T(8,128)(2,1)S(1)}, bf16[512,768]{1,0:T(8,128)(2,1)S(1)}, u32[]{:S(2)}, u32[]{:S(2)}) collective-permute-start(bf16[512,768]{1,0:T(8,128)(2,1)S(1)} %get-tuple-element.117), channel_id=1, source_target_pairs={{0,0},{1,1},{2,4},{3,5},{4,2},{5,3},{6,6},{7,7},{8,8},{9,9},{10,12... | collective-permute-start | bytes 2359304 | tf_op jit(solution)/shard_map/ppermute | solution.py:1424
  79.4 0.9 copy-start.1
  79.5 1.1 copy-start.2

commit v6 on v5

--- a/solution.py
+++ b/solution.py
@@ -15,7 +15,6 @@
 VMEM_BYTES = 60 * 1024 * 1024
 BOTH = ("dp", "seq")
 TOKEN_PARTS = 8
-TOKENS_AHEAD = 6
 F32 = jnp.float32
 BF16 = jnp.bfloat16
 NN = (((1,), (0,)), ((), ()))
@@ -339,8 +338,14 @@
         "x": (d + 2 - 4 * x, z),
         "y": (d + 4 - 8 * y, z),
         "near": (d, z + 1 - 2 * (z % 2)),
-        "far": (d, (z + 2) % 4),
+        "across": (d, (z + 2) % 4),
+        "inner": (d, 3 - z),
     }
+
+
+def outer():
+    z = lax.axis_index("seq")
+    return (z == 0) | (z == 3)
 
 
 def remote(source, target, sends, receives, send_index, receive_index, device):
@@ -358,41 +363,38 @@
     def __init__(self, source, out, scratch):
         self.source, self.out = source, out
         self.own = source.at[:, :, :, here()[4]]
-        self.from_core, self.first, self.second, self.near, self.far, self.other = scratch[:6]
-        self.sends, self.receives, self.local = scratch[6:9]
+        self.from_core, self.first, self.second, self.near, self.far = scratch[:5]
+        self.sends, self.receives, self.local = scratch[5:8]
         self.parts, _, _, self.rows, self.width = self.from_core.shape
-        self.half, self.top = self.width // 2, self.rows // 2
+        self.half = self.width // 2
 
     @staticmethod
     def scratch(parts, block, width):
-        half, top = width // 2, block // 2
+        half = width // 2
         return [
             pltpu.VMEM((parts, 2, 2, block, width), BF16),
             pltpu.VMEM((2, parts, 2, block, half), BF16),
             pltpu.VMEM((2, parts, block, half), BF16),
-            pltpu.VMEM((parts, top, width), BF16),
-            pltpu.VMEM((parts, top, width), BF16),
-            pltpu.VMEM((parts, top, width), BF16),
+            pltpu.VMEM((parts, block, width), BF16),
+            pltpu.VMEM((parts, block, width), BF16),
             pltpu.SemaphoreType.DMA((8,)),
             pltpu.SemaphoreType.DMA((8,)),
-            pltpu.SemaphoreType.DMA((2,)),
+            pltpu.SemaphoreType.DMA((1,)),
         ]
 
     def copy(self, number):
         d, z, y, x, core = here()
         to = partners()
         left, right = pl.ds(0, self.half), pl.ds(self.half, self.half)
-        kept = pl.ds(pl.multiple_of((z % 2) * self.top, self.top), self.top)
-        given = pl.ds(pl.multiple_of((1 - z % 2) * self.top, self.top), self.top)
         source, target, device = (
             lambda: (self.source.at[:, :, :, 1 - core], self.from_core, to["core"]),
             lambda: (self.own.at[:, :, 1 - x, :, left], self.first.at[0], to["x"]),
             lambda: (self.own.at[:, 1 - y, :, :, right], self.first.at[1], to["y"]),
             lambda: (self.own.at[:, 1 - y, x, :, left], self.second.at[0], to["y"]),
             lambda: (self.own.at[:, y, 1 - x, :, right], self.second.at[1], to["x"]),
-            lambda: (self.own.at[:, y, x, given], self.near, to["near"]),
-            lambda: (self.own.at[:, y, x, kept], self.far, to["far"]),
-            lambda: (self.own.at[:, y, x, kept], self.other, to["near"]),
+            lambda: (self.own.at[:, y, x], self.near, to["near"]),
+            lambda: (self.own.at[:, y, x], self.far, to["inner"]),
+            lambda: (self.own.at[:, y, x], self.near, to["near"]),
         )[number]()
         return remote(source, target, self.sends, self.receives, number, number, device)
 
@@ -428,41 +430,54 @@
         for part in range(self.parts):
             self.own[part, y, x, :, left] = self.own[part, y, x, :, left] + self.second[0, part]
             self.own[part, y, x, :, right] = self.own[part, y, x, :, right] + self.second[1, part]
-        self.copy(5).start()
-
-    def add_rows(self, received):
-        _, z, y, x, _ = here()
-        kept = pl.ds(pl.multiple_of((z % 2) * self.top, self.top), self.top)
+
+        @pl.when(outer())
+        def _():
+            self.copy(5).start()
+
+    def add_whole(self, received):
+        _, _, y, x, _ = here()
         for part in range(self.parts):
-            self.own[part, y, x, kept] = self.own[part, y, x, kept] + received[part]
+            self.own[part, y, x] = self.own[part, y, x] + received[part]
 
     def to_far(self):
-        self.copy(5).wait()
-        self.add_rows(self.near)
-        self.copy(6).start()
+        @pl.when(jnp.logical_not(outer()))
+        def _():
+            self.copy(5).wait_recv()
+            self.add_whole(self.near)
+            self.copy(6).start()
 
     def to_other(self):
-        self.copy(6).wait()
-        self.add_rows(self.far)
-        self.copy(7).start()
-
-    def stores(self):
-        _, z, y, x, _ = here()
-        kept = pl.ds(pl.multiple_of((z % 2) * self.top, self.top), self.top)
-        given = pl.ds(pl.multiple_of((1 - z % 2) * self.top, self.top), self.top)
-        return (
-            pltpu.make_async_copy(self.own.at[:, y, x, kept], self.out.at[:, kept], self.local.at[0]),
-            pltpu.make_async_copy(self.other, self.out.at[:, given], self.local.at[1]),
-        )
+        @pl.when(jnp.logical_not(outer()))
+        def _():
+            self.copy(6).wait()
+            self.add_whole(self.far)
+            self.copy(7).start()
 
     def to_out(self):
-        self.copy(7).wait()
-        for copy in self.stores():
-            copy.start()
+        _, _, y, x, _ = here()
+
+        @pl.when(outer())
+        def _():
+            self.copy(5).wait_send()
+            self.copy(7).wait_recv()
+            pltpu.make_async_copy(self.near, self.out, self.local.at[0]).start()
+
+        @pl.when(jnp.logical_not(outer()))
+        def _():
+            pltpu.make_async_copy(self.own.at[:, y, x], self.out, self.local.at[0]).start()
 
     def finish(self):
-        for copy in self.stores():
-            copy.wait()
+        _, _, y, x, _ = here()
+
+        @pl.when(outer())
+        def _():
+            pltpu.make_async_copy(self.near, self.out, self.local.at[0]).wait()
+
+        @pl.when(jnp.logical_not(outer()))
+        def _():
+            self.copy(7).wait_send()
+            pltpu.make_async_copy(self.own.at[:, y, x], self.out, self.local.at[0]).wait()
 
 
 class Trade:
@@ -668,7 +683,7 @@
     down_parts, up_parts = refs[:2]
     chunks = []
     for number, (which, at, many) in enumerate(back_chunks(down_parts.shape, up_parts.shape)):
-        scratch = refs[2 + 9 * number : 11 + 9 * number]
+        scratch = refs[2 + 8 * number : 10 + 8 * number]
         if which == "down":
             here_rows = pl.ds(at, many)
             chunks.append(
@@ -677,15 +692,15 @@
         else:
             here_parts = pl.ds(at, many)
             chunks.append(Reduction(up_parts.at[here_parts], up_out.at[here_parts], scratch))
-    qkv_parts = refs[38]
+    qkv_parts = refs[34]
     for group in range(2):
         lanes = pl.ds(2 * group * LANES, 2 * LANES)
-        scratch = refs[39 + 9 * group : 48 + 9 * group]
+        scratch = refs[35 + 8 * group : 43 + 8 * group]
         chunks.append(Reduction(qkv_parts.at[group], qkv_out.at[:, :, lanes], scratch))
     one, two, three, four, five, six = chunks
-    query_held, near_grads, far_grads, far_in, far_sends, far_receives = refs[57:63]
-    whole_context_ref, branch_ref, cots_ref, first_normed_ref, loads = refs[63:68]
-    back = Trade(layer_out, *refs[68:])
+    query_held, near_grads, far_grads, far_in, far_sends, far_receives = refs[51:57]
+    whole_context_ref, branch_ref, cots_ref, first_normed_ref, loads = refs[57:62]
+    back = Trade(layer_out, *refs[62:])
     block = key_refs[0].shape[0]
     layer_blocks = [layer_ref.at[pl.ds(p * block, block)] for p in range(2)]
     step = pl.program_id(0)
@@ -710,7 +725,7 @@
     def begin():
         for copy in loaded:
             copy.start()
-        meet(("core", "x", "y", "near", "far"), back)
+        meet(("core", "x", "y", "near", "inner"), back)
         back.begin(0, layer_blocks[0])
         back.begin(1, layer_blocks[1])
 
@@ -748,18 +763,16 @@
         (11, 1): [two.to_near],
         (11, 2): [three.to_second, one.to_other],
         (11, 3): [five.to_first, four.to_second],
-        (12, 0): [two.to_far, one.to_out],
-        (12, 1): [three.to_near],
+        (12, 1): [three.to_near, two.to_far, one.to_out],
         (12, 2): [five.to_second, four.to_near],
-        (12, 3): [three.to_far],
-        (13, 0): [six.to_cores, five.to_near, four.to_far, two.to_other],
-        (13, 1): [six.to_first],
+        (13, 0): [six.to_cores, five.to_near, three.to_far],
+        (13, 1): [six.to_first, four.to_far, two.to_other],
         (13, 2): [five.to_far],
-        (13, 3): [six.to_second, three.to_other, two.to_out],
-        (14, 1): [six.to_near, four.to_other, five.to_other, three.to_out],
-        (14, 2): [six.to_far],
-        (14, 3): [four.to_out, five.to_out],
-        (15, 0): [six.to_other, six.to_out],
+        (13, 3): [six.to_second, three.to_other],
+        (14, 1): [six.to_near, four.to_other, five.to_other, two.to_out],
+        (14, 2): [three.to_out],
+        (14, 3): [six.to_far, five.to_out],
+        (15, 0): [six.to_other, four.to_out, six.to_out],
     }
 
     def run_plan(place, steps):
@@ -909,12 +922,12 @@
     tokens_out, qkv_out, sums_ref,
     query_v, key_v, value_v, normed_v, x_v, middle_v, weight_v, token_v, last_parts, *refs, total_tokens, parts,
 ):
-    one = Reduction(last_parts, qkv_out, refs[:9])
-    sums_in, sums_sends, sums_receives, loads = refs[9:13]
-    back = Trade(tokens_out, *refs[13:], parts=TOKEN_PARTS)
+    one = Reduction(last_parts, qkv_out, refs[:8])
+    sums_in, sums_sends, sums_receives, loads = refs[8:12]
+    back = Trade(tokens_out, *refs[12:], parts=TOKEN_PARTS)
     block, width = x0.shape
     d, z, _, _, core = here()
-    total = 2 * TOKEN_PARTS
+    total, ahead, many = 2 * TOKEN_PARTS, TOKEN_PARTS, block // 2
     top, bottom = pl.ds(0, block), pl.ds(block, block)
     later = ((query_grad, query_v), (key_grad, key_v), (value_grad, value_v), (middle_grad, middle_v))
     copies = [
@@ -930,17 +943,19 @@
     ]
     for copy in copies:
         copy.start()
-    meet(("core", "x", "y", "near", "far"), back)
-
-    def start_block(p):
-        held = pl.ds(p * block, block)
+    meet(("core", "x", "y", "near", "inner", "across"), back)
+
+    def start_block(number):
+        p, at = divmod(number * many, block)
+        held = pl.ds(number * many, many)
+        inner = pl.ds(at, many)
         normed_grad = 0.0
         for part, grads in enumerate((query_v, key_v, value_v)):
             columns = slice(part * width, (part + 1) * width)
             normed_grad = normed_grad + dot(grads[held], weight_v[:, columns], NT)
-        unit, scale = norm_parts(x_v[p].astype(F32) + one_row(info_ref, TIME))
+        unit, scale = norm_parts(x_v[p, inner].astype(F32) + one_row(info_ref, TIME))
         token_grad = middle_v[held] + norm_backward(normed_grad, vector(gain_ref), unit, scale)
-        token_v[p] = token_grad.astype(BF16)
+        token_v[p, inner] = token_grad.astype(BF16)
         return [
             column_sum(normed_grad * unit),
             column_sum(normed_grad),
@@ -950,7 +965,7 @@
         ]
 
     def sums_copy(number):
-        to = partners()[("core", "x", "y", "near", "far")[number]]
+        to = partners()[("core", "x", "y", "near", "across")[number]]
         return remote(sums_ref, sums_in.at[number], sums_sends, sums_receives, number, number, to)
 
     def sums_next(number):
@@ -960,16 +975,19 @@
             sums_copy(number + 1).start()
 
     def move(number):
-        if number >= TOKENS_AHEAD:
-            p, part = divmod(number - TOKENS_AHEAD, TOKEN_PARTS)
+        if number >= ahead:
+            p, part = divmod(number - ahead, TOKEN_PARTS)
             back.sent(p, token_v.at[p], part)
         p, part = divmod(number, TOKEN_PARTS)
         back.begin(p, token_v.at[p], part)
 
     for copy in copies[:6]:
         copy.wait()
-    first = start_block(0)
-    for number in range(TOKENS_AHEAD):
+    sums = start_block(0)
+    for number in range(ahead // 2):
+        move(number)
+    sums = [a + b for a, b in zip(sums, start_block(1))]
+    for number in range(ahead // 2, ahead):
         move(number)
     for copy in copies[6:]:
         copy.wait()
@@ -978,9 +996,9 @@
         made = dot(normed_v[...], grads[:, lanes], TN).astype(BF16)
         last_parts[part] = made.reshape(last_parts.shape[1:])
     one.to_cores()
-    second = start_block(1)
+    sums = [a + b for a, b in zip(sums, start_block(2))]
     one.to_first()
-    sums = [a + b for a, b in zip(first, second)]
+    sums = [a + b for a, b in zip(sums, start_block(3))]
     sums_ref[...] = jnp.zeros_like(sums_ref)
     sums_ref[0:4] = feed_ref[0:4]
     sums_ref[4 : 4 + parts] = feed_ref[8 : 8 + parts]
@@ -992,25 +1010,25 @@
     sequence = (d - core + z // 2) * 2 + z % 2
     sums_ref[pl.ds(16 + sequence, 1)] = sums[4]
     sums_copy(0).start()
-    for number in range(TOKENS_AHEAD, TOKENS_AHEAD + 2):
+    for number in range(ahead, ahead + 2):
         move(number)
     sums_next(0)
     one.to_second()
     sums_next(1)
     one.to_near()
     sums_next(2)
-    for number in range(TOKENS_AHEAD + 2, TOKENS_AHEAD + 4):
+    for number in range(ahead + 2, ahead + 4):
         move(number)
     one.to_far()
     sums_next(3)
-    for number in range(TOKENS_AHEAD + 4, TOKENS_AHEAD + 6):
+    for number in range(ahead + 4, ahead + 6):
         move(number)
     one.to_other()
     sums_next(4)
-    for number in range(TOKENS_AHEAD + 6, total):
+    for number in range(ahead + 6, total):
         move(number)
     one.to_out()
-    for number in range(total - TOKENS_AHEAD, total):
+    for number in range(total - ahead, total):
         p, part = divmod(number, TOKEN_PARTS)
         back.sent(p, token_v.at[p], part)
     for number in range(total):

time: 300 us -> 295 us (0.983)
  the two profiles are of different devices: /device:TPU:0 before, /device:TPU:1 now
where the time goes in v6:
time: 295 us; the launch traced here: 291 us
  Pallas kernels  276 us (94%)
  starting transfers between devices  12.5 us (4%)
    pallas_call x1, Pallas kernels, back(): pl.pallas_call(functools.partial(back_kernel, pieces=pieces, parts=parts,...  110 us
    pallas_call x1, Pallas kernels, tail(): pl.pallas_call(functools.partial(tail_kernel, total_tokens=total_tokens,...  53.8 us
    pallas_call x1, Pallas kernels, front(): pl.pallas_call(functools.partial(front_kernel, share=share), in_specs=[an...  39 us
    pallas_call x1, Pallas kernels, feed(): pl.pallas_call(feed_kernel, grid=(2,), in_specs=[rows(block, width), whol...  35.4 us
    pallas_call x1, Pallas kernels, attend(): pl.pallas_call(functools.partial(attend_kernel, pieces=pieces), grid=(pai...  30.2 us
    ppermute x2, starting transfers between devices, send(): return lax.ppermute(x, BOTH, order)  12.5 us
    pallas_call x1, Pallas kernels, finish(): pl.pallas_call(functools.partial(finish_kernel, total_seqs=sums.shape[0]...  7.23 us
  transfers between devices with their start and end apart: 2, of which 0 were waited for; matrix products, arithmetic and copies ran while one was open for 0% of the time, Pallas kernels for 10%

profile of v6, /device:TPU:1, one launch (start us, length us, event | category | flops | bytes accessed | tf_op | source)
XLA Modules:
  0.0 290.8 jit_solution(15625353953053214088)
XLA Ops:
  0.7 0.0 copy-start
  0.7 39.0 %front.1 = (bf16[512,768]{1,0:T(8,128)(2,1)}, bf16[512,768]{1,0:T(8,128)(2,1)}, bf16[1024,768]{1,0:T(8,128)(2,1)}, bf16[1024,768]{1,0:T(8,128)(2,1)}, bf16[512,1...) custom-call(bf16[2,512,768]{2,1,0:T(8,128)(2,1)} %tokens.1, ...), custom_call_target="tpu_custom_call" | custom-call | flops 55199997952 | tf_op jit(solution)/shard_map/front/pallas_call | solution.py:648
  39.7 0.0 copy-done
  39.7 0.1 dynamic-slice_bitcast_fusion
  39.8 5.8 %collective-permute-start.1 = (bf16[512,768]{1,0:T(8,128)(2,1)S(1)}, bf16[512,768]{1,0:T(8,128)(2,1)S(1)}, u32[]{:S(2)}, u32[]{:S(2)}) collective-permute-start(bf16[512,768]{1,0:T(8,128)(2,1)S(1)} %get-tuple-element.116), channel_id=1, source_target_pairs={{0,1},{1,0},{2,5},{3,4},{4,3},{5,2},{6,7},{7,6},{8,9},{9,8},{10,13... | collective-permute-start | bytes 2359304 | tf_op jit(solution)/shard_map/ppermute | solution.py:1442
  45.6 6.7 %collective-permute-start = (bf16[512,768]{1,0:T(8,128)(2,1)S(1)}, bf16[512,768]{1,0:T(8,128)(2,1)S(1)}, u32[]{:S(2)}, u32[]{:S(2)}) collective-permute-start(bf16[512,768]{1,0:T(8,128)(2,1)S(1)} %get-tuple-element.117), channel_id=1, source_target_pairs={{0,0},{1,1},{2,4},{3,5},{4,2},{5,3},{6,6},{7,7},{8,8},{9,9},{10,12... | collective-permute-start | bytes 2359304 | tf_op jit(solution)/shard_map/ppermute | solution.py:1442
  52.3 30.2 %attend.1 = (bf16[1024,768]{1,0:T(8,128)(2,1)}, f32[1024,768]{1,0:T(8,128)}) custom-call(bf16[1024,768]{1,0:T(8,128)(2,1)} %get-tuple-element.68.query_ref, bf16[512,1536]{1,0:T(8,128)(2,1)} %get-tuple-element.69.refs_0_.refs_4_, bf16[512,1536]{1,0:T(8,128)(2,1)} %get-tuple-element.70.refs_1_.refs_5_, bf16[512,1536]{1,0:T(8,128)(2,1)} %get-tuple-element.71.refs_2_.refs_6_, ...), custom_call_target="tpu_custom_call" | custom-call | flops 36800000000 | tf_op jit(solution)/shard_map/attend/pallas_call | solution.py:234
  82.5 0.0 collective-permute-done.1.cot1_ref.refs_14_
  82.5 0.0 copy-start.1
  82.5 0.0 collective-permute-done.cot0_ref.refs_13_
  82.5 0.0 copy-start.2
  82.5 0.8 copy-done.1
  83.4 0.3 copy-done.2
  83.6 35.4 %feed.1 = (bf16[1024,768]{1,0:T(8,128)(2,1)}, bf16[1024,3072]{1,0:T(8,128)(2,1)}, bf16[1024,3072]{1,0:T(8,128)(2,1)}, bf16[1024,768]{1,0:T(8,128)(2,1)}, f32[102...) custom-call(bf16[1024,768]{1,0:T(8,128)(2,1)} %get-tuple-element.73.context_ref.refs_10, ...), custom_call_target="tpu_custom_call" | custom-call | flops 39099998208 | tf_op jit(solution)/shard_map/feed/pallas_call | solution.py:1244
  119.1 110.5 %back.1 = (bf16[1024,768]{1,0:T(8,128)(2,1)}, bf16[1024,768]{1,0:T(8,128)(2,1)}, bf16[1024,768]{1,0:T(8,128)(2,1)}, bf16[2,512,768]{2,1,0:T(8,128)(2,1)}, bf16[1...) custom-call(bf16[1024,768]{1,0:T(8,128)(2,1)} %get-tuple-element.68.query_ref, ...), custom_call_target="tpu_custom_call" | custom-call | flops 115000000512 | tf_op jit(solution)/shard_map/back/pallas_call | solution.py:869
  229.5 53.8 %tail.1 = (bf16[2,512,768]{2,1,0:T(8,128)(2,1)}, bf16[3,96,256]{2,1,0:T(8,128)(2,1)}, f32[32,768]{1,0:T(8,128)}) custom-call(bf16[1024,768]{1,0:T(8,128)(2,1)} %get-tuple-element.86.query_grad, bf16[1024,768]{1,0:T(8,128)(2,1)} %get-tuple-element.87.key_grad, bf16[1024,768]{1,0:T(8,128)(2,1)} %get-tuple-element.88.value_grad, ...), custom_call_target="tpu_custom_call" | custom-call | flops 69000003584 | tf_op jit(solution)/shard_map/tail/pallas_call | solution.py:1048
  283.4 7.2 %finish.1 = (f32[1024,768]{1,0:T(8,128)}, bf16[1024,768]{1,0:T(8,128)(2,1)}, f32[96,2304]{1,0:T(8,128)}, f32[96,3072]{1,0:T(8,128)}, f32[96,768]{1,0:T(8,128)}, ...) custom-call(bf16[1024,768]{1,0:T(8,128)(2,1)} %bitcast.12, ...), custom_call_target="tpu_custom_call" | custom-call | flops 6899999744 | tf_op jit(solution)/shard_map/finish/pallas_call | solution.py:1121
Async XLA Ops:
  0.7 39.0 %copy-start = (bf16[2,512,768]{2,1,0:T(8,128)(2,1)S(1)}, bf16[2,512,768]{2,1,0:T(8,128)(2,1)}, u32[]{:S(2)}) copy-start(bf16[2,512,768]{2,1,0:T(8,128)(2,1)} %param.33) | copy-start | bytes 4718596
  39.8 42.7 %collective-permute-start.1 = (bf16[512,768]{1,0:T(8,128)(2,1)S(1)}, bf16[512,768]{1,0:T(8,128)(2,1)S(1)}, u32[]{:S(2)}, u32[]{:S(2)}) collective-permute-start(bf16[512,768]{1,0:T(8,128)(2,1)S(1)} %get-tuple-element.116), channel_id=1, source_target_pairs={{0,1},{1,0},{2,5},{3,4},{4,3},{5,2},{6,7},{7,6},{8,9},{9,8},{10,13... | collective-permute-start | bytes 2359304 | tf_op jit(solution)/shard_map/ppermute | solution.py:1442
  45.6 36.9 %collective-permute-start = (bf16[512,768]{1,0:T(8,128)(2,1)S(1)}, bf16[512,768]{1,0:T(8,128)(2,1)S(1)}, u32[]{:S(2)}, u32[]{:S(2)}) collective-permute-start(bf16[512,768]{1,0:T(8,128)(2,1)S(1)} %get-tuple-element.117), channel_id=1, source_target_pairs={{0,0},{1,1},{2,4},{3,5},{4,2},{5,3},{6,6},{7,7},{8,8},{9,9},{10,12... | collective-permute-start | bytes 2359304 | tf_op jit(solution)/shard_map/ppermute | solution.py:1442
  82.5 0.9 copy-start.1
  82.5 1.1 copy-start.2

commit v7 on v6

--- a/solution.py
+++ b/solution.py
@@ -338,7 +338,6 @@
         "x": (d + 2 - 4 * x, z),
         "y": (d + 4 - 8 * y, z),
         "near": (d, z + 1 - 2 * (z % 2)),
-        "across": (d, (z + 2) % 4),
         "inner": (d, 3 - z),
     }
 
@@ -581,13 +580,15 @@
     d, z, _, _, core = here()
     block, width = x_v.shape[1:]
     small = (gain, shift, query_bias, value_bias)
-    trade = Trade(x_v, *trade, gather=True)
+    trade = Trade(x_v, *trade, gather=True, parts=2)
     loaded = pltpu.make_async_copy(weight, weight_v, load.at[0])
     looked_up = pltpu.make_async_copy(table, table_v, load.at[1])
     meet(("core",), trade)
     held = [tokens.at[(z + p) % 2] for p in range(2)]
-    for p in range(2):
-        trade.begin(p, held[p])
+    pieces = [(p, part) for p in range(2) for part in range(2)]
+    many = block // 2
+    for p, part in pieces:
+        trade.begin(p, held[p], part)
     looked_up.start()
     loaded.start()
     steps = [steps_ref[j] for j in range(2)]
@@ -607,31 +608,36 @@
     info_out[4:8] = jnp.zeros_like(info_in[4:8])
     loaded.wait()
     copies, moved = [], []
-    for p in range(2):
-        trade.arrived(p, held[p])
-        normed, part = project_rows(x_v[p], info_out, small, weight_v)
-        near_v[p, :, :width] = part(1)
-        near_v[p, :, width:] = part(2)
-        moved.append(remote(near_v.at[p], far_v.at[p], sends, receives, p, p, partners()["core"]))
-        moved[p].start()
-        normed_v[p] = normed
-        query_v[p] = part(0)
-        outs = (x0_out, x1_out)[p], (near0_out, near1_out)[p]
-        here_rows = pl.ds(p * block, block)
-        for number, (source, target) in enumerate(
+    for number, (p, part) in enumerate(pieces):
+        trade.arrived(p, held[p], part)
+        inner = pl.ds(part * many, many)
+        normed, made = project_rows(x_v[p, inner], info_out, small, weight_v)
+        near_v[p, inner, :width] = made(1)
+        near_v[p, inner, width:] = made(2)
+        moved.append(
+            remote(near_v.at[p, inner], far_v.at[p, inner], sends, receives, number, number, partners()["core"])
+        )
+        moved[number].start()
+        normed_v[p, inner] = normed
+        query_v[p, inner] = made(0)
+        whole = pl.ds(number * many, many)
+        for at, (source, target) in enumerate(
             (
-                (x_v.at[p], outs[0]), (normed_v.at[p], normed_out.at[here_rows]),
-                (query_v.at[p], query_out.at[here_rows]), (near_v.at[p], outs[1]),
+                (x_v.at[p, inner], (x0_out, x1_out)[p].at[inner]), (normed_v.at[p, inner], normed_out.at[whole]),
+                (query_v.at[p, inner], query_out.at[whole]), (near_v.at[p, inner], (near0_out, near1_out)[p].at[inner]),
             )
         ):
-            copies.append(pltpu.make_async_copy(source, target, stores.at[p, number]))
+            copies.append(pltpu.make_async_copy(source, target, stores.at[number, at]))
             copies[-1].start()
-    for p in range(2):
-        moved[p].wait()
-        copies.append(pltpu.make_async_copy(far_v.at[p], (far0_out, far1_out)[p], stores.at[p, 4]))
+    for number, (p, part) in enumerate(pieces):
+        inner = pl.ds(part * many, many)
+        moved[number].wait()
+        copies.append(
+            pltpu.make_async_copy(far_v.at[p, inner], (far0_out, far1_out)[p].at[inner], stores.at[number, 4])
+        )
         copies[-1].start()
-    for p in range(2):
-        trade.sent(p, held[p])
+    for p, part in pieces:
+        trade.sent(p, held[p], part)
     for copy in copies:
         copy.wait()
 
@@ -644,7 +650,7 @@
     pair = pltpu.VMEM((2, block, width), BF16)
     wide_pair = pltpu.VMEM((2, block, 2 * width), BF16)
     one = pltpu.SemaphoreType.DMA((1,))
-    two = pltpu.SemaphoreType.DMA((2,))
+    two, four = pltpu.SemaphoreType.DMA((2,)), pltpu.SemaphoreType.DMA((4,))
     return pl.pallas_call(
         functools.partial(front_kernel, share=share),
         in_specs=[any_spec] * 3 + [pl.BlockSpec(memory_space=pltpu.SMEM)] + [inside] * 4,
@@ -656,9 +662,9 @@
         scratch_shapes=[
             pair, pltpu.VMEM(weight.shape, BF16), pltpu.VMEM(table.shape, BF16), pltpu.VMEM(info_shape, F32),
             pltpu.VMEM(info_shape, F32), pair, pair, wide_pair, wide_pair,
-            two, pltpu.SemaphoreType.DMA((2, 5)), one, one, two, two,
+            two, pltpu.SemaphoreType.DMA((4, 5)), one, one, four, four,
         ]
-        + Trade.semaphores(),
+        + Trade.semaphores(2),
         compiler_params=pltpu.CompilerParams(
             vmem_limit_bytes=VMEM_BYTES, collective_id=2, has_side_effects=True
         ),
@@ -943,7 +949,7 @@
     ]
     for copy in copies:
         copy.start()
-    meet(("core", "x", "y", "near", "inner", "across"), back)
+    meet(("core", "x", "y", "near", "inner"), back)
 
     def start_block(number):
         p, at = divmod(number * many, block)
@@ -965,14 +971,42 @@
         ]
 
     def sums_copy(number):
-        to = partners()[("core", "x", "y", "near", "across")[number]]
+        to = partners()[("core", "x", "y", "near", "inner", "near")[number]]
         return remote(sums_ref, sums_in.at[number], sums_sends, sums_receives, number, number, to)
 
     def sums_next(number):
-        sums_copy(number).wait()
-        sums_ref[...] = sums_ref[...] + sums_in[number]
-        if number < 4:
-            sums_copy(number + 1).start()
+        def add_up():
+            sums_ref[...] = sums_ref[...] + sums_in[number]
+
+        if number < 3:
+            sums_copy(number).wait()
+            add_up()
+            if number < 2:
+                sums_copy(number + 1).start()
+            else:
+                pl.when(outer())(sums_copy(3).start)
+            return
+
+        @pl.when(outer())
+        def _():
+            if number == 3:
+                sums_copy(3).wait_send()
+            if number == 5:
+                sums_copy(5).wait_recv()
+                sums_ref[...] = sums_in[5]
+
+        @pl.when(jnp.logical_not(outer()))
+        def _():
+            if number == 3:
+                sums_copy(3).wait_recv()
+                add_up()
+                sums_copy(4).start()
+            if number == 4:
+                sums_copy(4).wait()
+                add_up()
+                sums_copy(5).start()
+            if number == 5:
+                sums_copy(5).wait_send()
 
     def move(number):
         if number >= ahead:
@@ -1028,6 +1062,7 @@
     for number in range(ahead + 6, total):
         move(number)
     one.to_out()
+    sums_next(5)
     for number in range(total - ahead, total):
         p, part = divmod(number, TOKEN_PARTS)
         back.sent(p, token_v.at[p], part)
@@ -1059,9 +1094,9 @@
         ]
         + Reduction.scratch(3, up_rows, 2 * LANES)
         + [
-            held(5, *sums_shape, dtype=F32),
-            pltpu.SemaphoreType.DMA((5,)),
-            pltpu.SemaphoreType.DMA((5,)),
+            held(6, *sums_shape, dtype=F32),
+            pltpu.SemaphoreType.DMA((6,)),
+            pltpu.SemaphoreType.DMA((6,)),
             pltpu.SemaphoreType.DMA((12,)),
         ]
         + Trade.semaphores(TOKEN_PARTS),

time: 295 us -> 291 us (0.986)
  the two profiles are of different devices: /device:TPU:1 before, /device:TPU:0 now
where the time goes in v7:
time: 291 us; the launch traced here: 286 us
  Pallas kernels  275 us (95%)
  starting transfers between devices  9.08 us (3%)
    pallas_call x1, Pallas kernels, back(): pl.pallas_call(functools.partial(back_kernel, pieces=pieces, parts=parts,...  117 us
    pallas_call x1, Pallas kernels, tail(): pl.pallas_call(functools.partial(tail_kernel, total_tokens=total_tokens,...  47.8 us
    pallas_call x1, Pallas kernels, front(): pl.pallas_call(functools.partial(front_kernel, share=share), in_specs=[an...  37.4 us
    pallas_call x1, Pallas kernels, feed(): pl.pallas_call(feed_kernel, grid=(2,), in_specs=[rows(block, width), whol...  35.4 us
    pallas_call x1, Pallas kernels, attend(): pl.pallas_call(functools.partial(attend_kernel, pieces=pieces), grid=(pai...  30.2 us
    ppermute x2, starting transfers between devices, send(): return lax.ppermute(x, BOTH, order)  9.08 us
    pallas_call x1, Pallas kernels, finish(): pl.pallas_call(functools.partial(finish_kernel, total_seqs=sums.shape[0]...  7.23 us
  transfers between devices with their start and end apart: 2, of which 0 were waited for; matrix products, arithmetic and copies ran while one was open for 0% of the time, Pallas kernels for 11%

profile of v7, /device:TPU:0, one launch (start us, length us, event | category | flops | bytes accessed | tf_op | source)
XLA Modules:
  0.0 286.4 jit_solution(3448709446853621574)
XLA Ops:
  0.7 0.0 copy-start
  0.7 37.4 %front.1 = (bf16[512,768]{1,0:T(8,128)(2,1)}, bf16[512,768]{1,0:T(8,128)(2,1)}, bf16[1024,768]{1,0:T(8,128)(2,1)}, bf16[1024,768]{1,0:T(8,128)(2,1)}, bf16[512,1...) custom-call(bf16[2,512,768]{2,1,0:T(8,128)(2,1)} %tokens.1, ...), custom_call_target="tpu_custom_call" | custom-call | flops 55199997952 | tf_op jit(solution)/shard_map/front/pallas_call | solution.py:654
  38.1 0.0 copy-done
  38.1 0.1 dynamic-slice_bitcast_fusion
  38.2 8.2 %collective-permute-start.1 = (bf16[512,768]{1,0:T(8,128)(2,1)S(1)}, bf16[512,768]{1,0:T(8,128)(2,1)S(1)}, u32[]{:S(2)}, u32[]{:S(2)}) collective-permute-start(bf16[512,768]{1,0:T(8,128)(2,1)S(1)} %get-tuple-element.116), channel_id=1, source_target_pairs={{0,1},{1,0},{2,5},{3,4},{4,3},{5,2},{6,7},{7,6},{8,9},{9,8},{10,13... | collective-permute-start | bytes 2359304 | tf_op jit(solution)/shard_map/ppermute | solution.py:1477
  46.4 0.9 collective-permute-start
  47.3 30.2 %attend.1 = (bf16[1024,768]{1,0:T(8,128)(2,1)}, f32[1024,768]{1,0:T(8,128)}) custom-call(bf16[1024,768]{1,0:T(8,128)(2,1)} %get-tuple-element.68.query_ref, bf16[512,1536]{1,0:T(8,128)(2,1)} %get-tuple-element.69.refs_0_.refs_4_, bf16[512,1536]{1,0:T(8,128)(2,1)} %get-tuple-element.70.refs_1_.refs_5_, bf16[512,1536]{1,0:T(8,128)(2,1)} %get-tuple-element.71.refs_2_.refs_6_, ...), custom_call_target="tpu_custom_call" | custom-call | flops 36800000000 | tf_op jit(solution)/shard_map/attend/pallas_call | solution.py:234
  77.5 0.0 collective-permute-done.1.cot1_ref.refs_14_
  77.5 0.0 copy-start.1
  77.5 0.0 collective-permute-done.cot0_ref.refs_13_
  77.5 0.0 copy-start.2
  77.5 0.8 copy-done.1
  78.4 0.3 copy-done.2
  78.6 35.4 %feed.1 = (bf16[1024,768]{1,0:T(8,128)(2,1)}, bf16[1024,3072]{1,0:T(8,128)(2,1)}, bf16[1024,3072]{1,0:T(8,128)(2,1)}, bf16[1024,768]{1,0:T(8,128)(2,1)}, f32[102...) custom-call(bf16[1024,768]{1,0:T(8,128)(2,1)} %get-tuple-element.73.context_ref.refs_10, ...), custom_call_target="tpu_custom_call" | custom-call | flops 39099998208 | tf_op jit(solution)/shard_map/feed/pallas_call | solution.py:1279
  114.1 117.0 %back.1 = (bf16[1024,768]{1,0:T(8,128)(2,1)}, bf16[1024,768]{1,0:T(8,128)(2,1)}, bf16[1024,768]{1,0:T(8,128)(2,1)}, bf16[2,512,768]{2,1,0:T(8,128)(2,1)}, bf16[1...) custom-call(bf16[1024,768]{1,0:T(8,128)(2,1)} %get-tuple-element.68.query_ref, ...), custom_call_target="tpu_custom_call" | custom-call | flops 115000000512 | tf_op jit(solution)/shard_map/back/pallas_call | solution.py:875
  231.1 47.8 %tail.1 = (bf16[2,512,768]{2,1,0:T(8,128)(2,1)}, bf16[3,96,256]{2,1,0:T(8,128)(2,1)}, f32[32,768]{1,0:T(8,128)}) custom-call(bf16[1024,768]{1,0:T(8,128)(2,1)} %get-tuple-element.86.query_grad, bf16[1024,768]{1,0:T(8,128)(2,1)} %get-tuple-element.87.key_grad, bf16[1024,768]{1,0:T(8,128)(2,1)} %get-tuple-element.88.value_grad, ...), custom_call_target="tpu_custom_call" | custom-call | flops 69000003584 | tf_op jit(solution)/shard_map/tail/pallas_call | solution.py:1083
  278.9 7.2 %finish.1 = (f32[1024,768]{1,0:T(8,128)}, bf16[1024,768]{1,0:T(8,128)(2,1)}, f32[96,2304]{1,0:T(8,128)}, f32[96,3072]{1,0:T(8,128)}, f32[96,768]{1,0:T(8,128)}, ...) custom-call(bf16[1024,768]{1,0:T(8,128)(2,1)} %bitcast.12, ...), custom_call_target="tpu_custom_call" | custom-call | flops 6899999744 | tf_op jit(solution)/shard_map/finish/pallas_call | solution.py:1156
Async XLA Ops:
  0.7 37.4 %copy-start = (bf16[2,512,768]{2,1,0:T(8,128)(2,1)S(1)}, bf16[2,512,768]{2,1,0:T(8,128)(2,1)}, u32[]{:S(2)}) copy-start(bf16[2,512,768]{2,1,0:T(8,128)(2,1)} %param.33) | copy-start | bytes 4718596
  38.2 39.3 %collective-permute-start.1 = (bf16[512,768]{1,0:T(8,128)(2,1)S(1)}, bf16[512,768]{1,0:T(8,128)(2,1)S(1)}, u32[]{:S(2)}, u32[]{:S(2)}) collective-permute-start(bf16[512,768]{1,0:T(8,128)(2,1)S(1)} %get-tuple-element.116), channel_id=1, source_target_pairs={{0,1},{1,0},{2,5},{3,4},{4,3},{5,2},{6,7},{7,6},{8,9},{9,8},{10,13... | collective-permute-start | bytes 2359304 | tf_op jit(solution)/shard_map/ppermute | solution.py:1477
  46.4 31.1 %collective-permute-start = (bf16[512,768]{1,0:T(8,128)(2,1)S(1)}, bf16[512,768]{1,0:T(8,128)(2,1)S(1)}, u32[]{:S(2)}, u32[]{:S(2)}) collective-permute-start(bf16[512,768]{1,0:T(8,128)(2,1)S(1)} %get-tuple-element.117), channel_id=1, source_target_pairs={{0,0},{1,1},{2,4},{3,5},{4,2},{5,3},{6,6},{7,7},{8,8},{9,9},{10,12... | collective-permute-start | bytes 2359304 | tf_op jit(solution)/shard_map/ppermute | solution.py:1477
  77.5 0.9 copy-start.1
  77.5 1.1 copy-start.2

commit v8 on v7

--- a/solution.py
+++ b/solution.py
@@ -769,16 +769,18 @@
         (11, 1): [two.to_near],
         (11, 2): [three.to_second, one.to_other],
         (11, 3): [five.to_first, four.to_second],
-        (12, 1): [three.to_near, two.to_far, one.to_out],
+        (12, 0): [two.to_far],
+        (12, 1): [three.to_near],
         (12, 2): [five.to_second, four.to_near],
-        (13, 0): [six.to_cores, five.to_near, three.to_far],
-        (13, 1): [six.to_first, four.to_far, two.to_other],
-        (13, 2): [five.to_far],
-        (13, 3): [six.to_second, three.to_other],
-        (14, 1): [six.to_near, four.to_other, five.to_other, two.to_out],
-        (14, 2): [three.to_out],
-        (14, 3): [six.to_far, five.to_out],
-        (15, 0): [six.to_other, four.to_out, six.to_out],
+        (13, 0): [six.to_cores, five.to_near, three.to_far, two.to_other],
+        (13, 1): [six.to_first, four.to_far, five.to_far],
+        (13, 2): [three.to_other],
+        (13, 3): [six.to_second],
+        (14, 0): [four.to_other, five.to_other],
+        (14, 1): [six.to_near, one.to_out],
+        (14, 2): [six.to_far],
+        (14, 3): [six.to_other],
+        (15, 0): [two.to_out, three.to_out, four.to_out, five.to_out, six.to_out],
     }
 
     def run_plan(place, steps):

time: 291 us -> 289 us (level)
    pallas_call x1, Pallas kernels: 117 us -> 113 us  [back(): pl.pallas_call(functools.partial(back_kernel, pieces=pieces, parts=parts,...]
where the time goes in v8:
time: 289 us; the launch traced here: 284 us
  Pallas kernels  273 us (94%)
  starting transfers between devices  9.08 us (3%)
    pallas_call x1, Pallas kernels, back(): pl.pallas_call(functools.partial(back_kernel, pieces=pieces, parts=parts,...  113 us
    pallas_call x1, Pallas kernels, tail(): pl.pallas_call(functools.partial(tail_kernel, total_tokens=total_tokens,...  49.2 us
    pallas_call x1, Pallas kernels, front(): pl.pallas_call(functools.partial(front_kernel, share=share), in_specs=[an...  37.4 us
    pallas_call x1, Pallas kernels, feed(): pl.pallas_call(feed_kernel, grid=(2,), in_specs=[rows(block, width), whol...  35.4 us
    pallas_call x1, Pallas kernels, attend(): pl.pallas_call(functools.partial(attend_kernel, pieces=pieces), grid=(pai...  30.2 us
    ppermute x2, starting transfers between devices, send(): return lax.ppermute(x, BOTH, order)  9.08 us
    pallas_call x1, Pallas kernels, finish(): pl.pallas_call(functools.partial(finish_kernel, total_seqs=sums.shape[0]...  7.23 us
  transfers between devices with their start and end apart: 2, of which 0 were waited for; matrix products, arithmetic and copies ran while one was open for 0% of the time, Pallas kernels for 11%

profile of v8, /device:TPU:0, one launch (start us, length us, event | category | flops | bytes accessed | tf_op | source)
XLA Modules:
  0.0 283.9 jit_solution(14509049303960785538)
XLA Ops:
  0.7 0.0 copy-start
  0.7 37.4 %front.1 = (bf16[512,768]{1,0:T(8,128)(2,1)}, bf16[512,768]{1,0:T(8,128)(2,1)}, bf16[1024,768]{1,0:T(8,128)(2,1)}, bf16[1024,768]{1,0:T(8,128)(2,1)}, bf16[512,1...) custom-call(bf16[2,512,768]{2,1,0:T(8,128)(2,1)} %tokens.1, ...), custom_call_target="tpu_custom_call" | custom-call | flops 55199997952 | tf_op jit(solution)/shard_map/front/pallas_call | solution.py:654
  38.1 0.0 copy-done
  38.1 0.1 dynamic-slice_bitcast_fusion
  38.2 8.2 %collective-permute-start.1 = (bf16[512,768]{1,0:T(8,128)(2,1)S(1)}, bf16[512,768]{1,0:T(8,128)(2,1)S(1)}, u32[]{:S(2)}, u32[]{:S(2)}) collective-permute-start(bf16[512,768]{1,0:T(8,128)(2,1)S(1)} %get-tuple-element.116), channel_id=1, source_target_pairs={{0,1},{1,0},{2,5},{3,4},{4,3},{5,2},{6,7},{7,6},{8,9},{9,8},{10,13... | collective-permute-start | bytes 2359304 | tf_op jit(solution)/shard_map/ppermute | solution.py:1479
  46.4 0.9 collective-permute-start
  47.3 30.2 %attend.1 = (bf16[1024,768]{1,0:T(8,128)(2,1)}, f32[1024,768]{1,0:T(8,128)}) custom-call(bf16[1024,768]{1,0:T(8,128)(2,1)} %get-tuple-element.68.query_ref, bf16[512,1536]{1,0:T(8,128)(2,1)} %get-tuple-element.69.refs_0_.refs_4_, bf16[512,1536]{1,0:T(8,128)(2,1)} %get-tuple-element.70.refs_1_.refs_5_, bf16[512,1536]{1,0:T(8,128)(2,1)} %get-tuple-element.71.refs_2_.refs_6_, ...), custom_call_target="tpu_custom_call" | custom-call | flops 36800000000 | tf_op jit(solution)/shard_map/attend/pallas_call | solution.py:234
  77.5 0.0 collective-permute-done.1.cot1_ref.refs_14_
  77.5 0.0 copy-start.1
  77.5 0.0 collective-permute-done.cot0_ref.refs_13_
  77.5 0.0 copy-start.2
  77.5 0.8 copy-done.1
  78.4 0.3 copy-done.2
  78.6 35.4 %feed.1 = (bf16[1024,768]{1,0:T(8,128)(2,1)}, bf16[1024,3072]{1,0:T(8,128)(2,1)}, bf16[1024,3072]{1,0:T(8,128)(2,1)}, bf16[1024,768]{1,0:T(8,128)(2,1)}, f32[102...) custom-call(bf16[1024,768]{1,0:T(8,128)(2,1)} %get-tuple-element.73.context_ref.refs_10, ...), custom_call_target="tpu_custom_call" | custom-call | flops 39099998208 | tf_op jit(solution)/shard_map/feed/pallas_call | solution.py:1281
  114.1 113.2 %back.1 = (bf16[1024,768]{1,0:T(8,128)(2,1)}, bf16[1024,768]{1,0:T(8,128)(2,1)}, bf16[1024,768]{1,0:T(8,128)(2,1)}, bf16[2,512,768]{2,1,0:T(8,128)(2,1)}, bf16[1...) custom-call(bf16[1024,768]{1,0:T(8,128)(2,1)} %get-tuple-element.68.query_ref, ...), custom_call_target="tpu_custom_call" | custom-call | flops 115000000512 | tf_op jit(solution)/shard_map/back/pallas_call | solution.py:877
  227.2 49.2 %tail.1 = (bf16[2,512,768]{2,1,0:T(8,128)(2,1)}, bf16[3,96,256]{2,1,0:T(8,128)(2,1)}, f32[32,768]{1,0:T(8,128)}) custom-call(bf16[1024,768]{1,0:T(8,128)(2,1)} %get-tuple-element.86.query_grad, bf16[1024,768]{1,0:T(8,128)(2,1)} %get-tuple-element.87.key_grad, bf16[1024,768]{1,0:T(8,128)(2,1)} %get-tuple-element.88.value_grad, ...), custom_call_target="tpu_custom_call" | custom-call | flops 69000003584 | tf_op jit(solution)/shard_map/tail/pallas_call | solution.py:1085
  276.5 7.2 %finish.1 = (f32[1024,768]{1,0:T(8,128)}, bf16[1024,768]{1,0:T(8,128)(2,1)}, f32[96,2304]{1,0:T(8,128)}, f32[96,3072]{1,0:T(8,128)}, f32[96,768]{1,0:T(8,128)}, ...) custom-call(bf16[1024,768]{1,0:T(8,128)(2,1)} %bitcast.12, ...), custom_call_target="tpu_custom_call" | custom-call | flops 6899999744 | tf_op jit(solution)/shard_map/finish/pallas_call | solution.py:1158
Async XLA Ops:
  0.7 37.4 %copy-start = (bf16[2,512,768]{2,1,0:T(8,128)(2,1)S(1)}, bf16[2,512,768]{2,1,0:T(8,128)(2,1)}, u32[]{:S(2)}) copy-start(bf16[2,512,768]{2,1,0:T(8,128)(2,1)} %param.33) | copy-start | bytes 4718596
  38.2 39.3 %collective-permute-start.1 = (bf16[512,768]{1,0:T(8,128)(2,1)S(1)}, bf16[512,768]{1,0:T(8,128)(2,1)S(1)}, u32[]{:S(2)}, u32[]{:S(2)}) collective-permute-start(bf16[512,768]{1,0:T(8,128)(2,1)S(1)} %get-tuple-element.116), channel_id=1, source_target_pairs={{0,1},{1,0},{2,5},{3,4},{4,3},{5,2},{6,7},{7,6},{8,9},{9,8},{10,13... | collective-permute-start | bytes 2359304 | tf_op jit(solution)/shard_map/ppermute | solution.py:1479
  46.4 31.1 %collective-permute-start = (bf16[512,768]{1,0:T(8,128)(2,1)S(1)}, bf16[512,768]{1,0:T(8,128)(2,1)S(1)}, u32[]{:S(2)}, u32[]{:S(2)}) collective-permute-start(bf16[512,768]{1,0:T(8,128)(2,1)S(1)} %get-tuple-element.117), channel_id=1, source_target_pairs={{0,0},{1,1},{2,4},{3,5},{4,2},{5,3},{6,6},{7,7},{8,8},{9,9},{10,12... | collective-permute-start | bytes 2359304 | tf_op jit(solution)/shard_map/ppermute | solution.py:1479
  77.5 0.9 copy-start.1
  77.5 1.1 copy-start.2
